TPU v7x, 32 devices: a whole 2x2x4 slice. The times are simulated.
32 devices in a mesh: dp: 4 (over y, x), tensor: 8 (over z, core).
Axes of the slice: x: 2, y: 2, z: 4, core: 2. Of those that a mesh axis runs over, the one named last changes fastest.
Arguments:
- images: bfloat16 [8192, 768], P('dp'), may hold values from -6 to 6
- head: bfloat16 [768, 768], P(None, 'tensor'), may hold values from -0.21875 to 0.21875
- tea_img: bfloat16 [8192, 1536], P('dp'), may hold values from -6 to 6
- stu_txt: bfloat16 [8192, 768], P(('dp', 'tensor')), may hold values from -6 to 6
- tea_txt: bfloat16 [8192, 1536], P(('dp', 'tensor')), may hold values from -6 to 6
Outputs:
- grad_images: float32 [8192, 768], P(('dp', 'tensor'))
- grad_head: float32 [768, 768], P(None, 'tensor')
- grad_text: float32 [8192, 768], P(('dp', 'tensor'))
All inputs are finite; a program needn't handle non-finite values.
Results may differ from a plain program's by a relative error of at most 0.012.
Values may be sent and summed in bfloat16 or wider, within the bound.
No kernel may reach another device: no remote copies, remote signals or barrier semaphores. Data moves between devices by JAX's collectives and lax.ppermute only.
A program may use at most 192 MiB of HBM per device.

v0:
```python
import jax
import jax.numpy as jnp
from jax import lax
from jax.sharding import PartitionSpec as P

logit_scale = 64.0
logit_bias = -2.0
loss_scale = 65536.0


def passed_along(value, axis, steps):
    count = lax.axis_size(axis)
    pairs = [(source, (source + steps) % count) for source in range(count)]
    return lax.ppermute(value, axis, pairs)


def normalize(values):
    floats = values.astype(jnp.float32)
    length = jnp.sqrt(jnp.sum(floats * floats, axis=1, keepdims=True) + 1e-06)
    return (floats / length, length)


def affinity_tile(img_emb, tea_img_emb, txt_piece, tea_piece, factor):
    contract = (((1,), (1,)), ((), ()))
    target = jax.nn.sigmoid(
        logit_scale
        * lax.dot_general(tea_img_emb, tea_piece, contract, preferred_element_type=jnp.float32)
        + logit_bias
    )
    student = (
        logit_scale
        * lax.dot_general(img_emb, txt_piece, contract, preferred_element_type=jnp.float32)
        + logit_bias
    )
    return ((jax.nn.sigmoid(student) - target) * factor).astype(jnp.bfloat16)


def transpose_product(coef, img_emb):
    return lax.dot_general(
        coef, img_emb, (((0,), (0,)), ((), ())), preferred_element_type=jnp.float32
    )


def per_device(images, head, tea_img, stu_txt, tea_txt):
    dp_count = lax.axis_size("dp")
    tensor_count = lax.axis_size("tensor")
    tensor_rank = lax.axis_index("tensor")
    rows = images.shape[0]
    columns = head.shape[1]
    emb_width = columns * tensor_count
    factor = logit_scale * loss_scale / (rows * dp_count)
    proj_local = jnp.dot(images, head, preferred_element_type=jnp.float32).astype(jnp.bfloat16)
    proj = lax.all_gather(proj_local, "tensor", axis=1, tiled=True)
    img_unit, proj_norm = normalize(proj)
    img_emb = img_unit.astype(jnp.bfloat16)
    tea_img_emb = normalize(tea_img)[0].astype(jnp.bfloat16)
    txt_unit, txt_norm = normalize(stu_txt)
    txt_emb = txt_unit.astype(jnp.bfloat16)
    tea_txt_emb = normalize(tea_txt)[0].astype(jnp.bfloat16)
    img_grads = jnp.zeros((rows, emb_width), jnp.float32)
    text_grads = jnp.zeros((stu_txt.shape[0], emb_width), jnp.float32)
    travel_emb = txt_emb
    travel_tea = tea_txt_emb
    for rotation in range(dp_count):
        coef = affinity_tile(img_emb, tea_img_emb, travel_emb, travel_tea, factor)
        img_grads = img_grads + jnp.dot(coef, travel_emb, preferred_element_type=jnp.float32)
        text_grads = text_grads + transpose_product(coef, img_emb)
        if rotation + 1 < dp_count:
            travel_emb, travel_tea = passed_along((travel_emb, travel_tea), "dp", 1)
            text_grads = passed_along(text_grads, "dp", 1)
        else:
            text_grads = passed_along(text_grads, "dp", 1)
    share = rows // tensor_count
    summed = lax.psum(img_grads, "tensor")
    row_dot = jnp.sum(img_unit * summed, axis=1, keepdims=True)
    grad_proj = ((summed - img_unit * row_dot) / proj_norm).astype(jnp.bfloat16)
    own_columns = lax.dynamic_slice_in_dim(grad_proj, tensor_rank * columns, columns, 1)
    head_part = lax.dot_general(
        images, own_columns, (((0,), (0,)), ((), ())), preferred_element_type=jnp.float32
    )
    own_rows = lax.dynamic_slice_in_dim(grad_proj, tensor_rank * share, share, 0)
    head_full = lax.all_gather(head, "tensor", axis=1, tiled=True)
    grad_images = lax.dot_general(
        own_rows, head_full, (((1,), (1,)), ((), ())), preferred_element_type=jnp.float32
    )
    grad_head = lax.psum(head_part, "dp")
    grad_text = (
        text_grads - txt_unit * jnp.sum(txt_unit * text_grads, axis=1, keepdims=True)
    ) / txt_norm
    return (grad_images, grad_head, grad_text)


def solution(mesh):
    placed = (
        P("dp", None),
        P(None, "tensor"),
        P("dp", None),
        P(("dp", "tensor"), None),
        P(("dp", "tensor"), None),
    )
    return jax.shard_map(
        per_device,
        mesh=mesh,
        in_specs=placed,
        out_specs=(P(("dp", "tensor"), None), P(None, "tensor"), P(("dp", "tensor"), None)),
        check_vma=False,
    )
```

profile of v0, /device:TPU:0, one launch (start us, length us, event | category | flops | bytes accessed | tf_op | source)
XLA Modules:
  0.0 340.4 jit_solution(10477401049534778860)
XLA Ops:
  7.2 1.8 copy-done
  9.1 2.7 convolution_convert_fusion
  11.9 0.2 fusion.58
  12.1 0.1 fusion.64
  12.2 3.0 collective-permute-start
  15.2 1.4 fusion.56
  16.6 0.3 fusion.57
  16.9 1.5 collective-permute-start.1
  18.5 4.7 %fusion = f32[2048]{0:T(1024)S(1)} fusion(bf16[2048,1536]{1,0:T(8,128)(2,1)} %param.7), kind=kLoop, calls=%fused_computation.2 | loop fusion | flops 9435136 | bytes 6299648 | tf_op jit(solution)/shard_map/reduce_sum | solution.py:19
  23.2 2.9 collective-permute-done
  26.1 1.1 collective-permute-start.2
  27.2 2.9 fusion.1
  30.1 12.9 %collective-permute-done.1 = bf16[256,1536]{1,0:T(8,128)(2,1)} collective-permute-done((bf16[256,1536]{1,0:T(8,128)(2,1)S(1)}, bf16[256,1536]{1,0:T(8,128)(2,1)}, u32[]{:S(2)}, u32[]{:S(2)}) %collective-permute-start.1) | collective-permute-done | bytes 786464 | tf_op jit(solution)/shard_map/ppermute | solution.py:14
  43.1 1.1 collective-permute-start.3
  44.2 7.3 %collective-permute-done.2 = bf16[256,768]{1,0:T(8,128)(2,1)} collective-permute-done((bf16[256,768]{1,0:T(8,128)(2,1)S(1)}, bf16[256,768]{1,0:T(8,128)(2,1)}, u32[]{:S(2)}, u32[]{:S(2)}) %collective-permute-start.2) | collective-permute-done | bytes 393248 | tf_op jit(solution)/shard_map/ppermute | solution.py:14
  51.5 1.1 collective-permute-start.4
  52.6 4.5 %fusion.36 = f32[2048,256]{1,0:T(8,128)} fusion(bf16[2048,1536]{1,0:T(8,128)(2,1)S(1)} %fusion.1, bf16[256,1536]{1,0:T(8,128)(2,1)} %collective-permute-done.1), kind=kOutput, calls=%fused_computation.51 | convolution fusion | flops 1613234176 | bytes 9175040 | tf_op jit(solution)/shard_map/dot_general | solution.py:27
  57.1 11.2 %collective-permute-done.3 = bf16[256,1536]{1,0:T(8,128)(2,1)S(1)} collective-permute-done((bf16[256,1536]{1,0:T(8,128)(2,1)}, bf16[256,1536]{1,0:T(8,128)(2,1)S(1)}, u32[]{:S(2)}, u32[]{:S(2)}) %collective-permute-start.3) | collective-permute-done | bytes 786464 | tf_op jit(solution)/shard_map/ppermute | solution.py:14
  68.2 1.1 collective-permute-start.5
  69.3 3.4 %fusion.34 = f32[2048,256]{1,0:T(8,128)} fusion(bf16[2048,1536]{1,0:T(8,128)(2,1)S(1)} %fusion.1, bf16[256,1536]{1,0:T(8,128)(2,1)S(1)} %collective-permute-done.3), kind=kOutput, calls=%fused_computation.49 | convolution fusion | flops 1613234176 | bytes 9175040 | tf_op jit(solution)/shard_map/dot_general | solution.py:27
  72.8 19.9 %collective-permute-done.5 = bf16[256,1536]{1,0:T(8,128)(2,1)S(1)} collective-permute-done((bf16[256,1536]{1,0:T(8,128)(2,1)S(1)}, bf16[256,1536]{1,0:T(8,128)(2,1)S(1)}, u32[]{:S(2)}, u32[]{:S(2)}) %collective-permute-start.5) | collective-permute-done | bytes 786464 | tf_op jit(solution)/shard_map/ppermute | solution.py:14
  92.7 3.4 %fusion.32 = f32[2048,256]{1,0:T(8,128)} fusion(bf16[2048,1536]{1,0:T(8,128)(2,1)S(1)} %fusion.1, bf16[256,1536]{1,0:T(8,128)(2,1)S(1)} %collective-permute-done.5), kind=kOutput, calls=%fused_computation.47 | convolution fusion | flops 1613234176 | bytes 9175040 | tf_op jit(solution)/shard_map/dot_general | solution.py:27
  96.1 2.7 fusion.2
  98.9 0.1 copy-done.1
  99.0 1.0 fusion.55
  100.0 1.3 fusion.54
  101.3 2.2 slice-done.1
  103.5 0.2 copy-done.20
  103.6 2.2 fusion.41
  105.9 1.0 fusion.65
  106.9 0.2 copy-done.22
  107.1 0.8 copy-done.23
  108.0 1.5 fusion.53
  109.5 0.1 copy-done.25
  109.5 2.8 fusion.49
  112.3 2.3 fusion.67
  114.7 1.3 fusion.66
  116.0 0.3 copy-done.24
  116.3 2.5 fusion.45
  118.8 1.0 copy-done.18
  119.7 4.7 %add_add_fusion = f32[2048,768]{0,1:T(8,128)} fusion(f32[2048,768]{0,1:T(8,128)S(1)} %fusion.67, f32[2048,768]{0,1:T(8,128)S(1)} %fusion.65, f32[2048,768]{0,1:T(8,128)S(1)} %fusion.66, bf16[2048,256]{1,0:T(8,128)(2,1)S(1)} %fusion.45, bf16[256,768]{1,0:T(8,128)(2,1)} %collective-permute-done.4), kind=kOutput, calls=%fused_computation.9 | convolution fusion | flops 810024960 | bytes 26607616 | tf_op jit(solution)/shard_map/dot_general | solution.py:66
  124.6 3.4 fusion.68
  128.0 0.8 collective-permute-start.6
  128.8 18.9 %collective-permute-done.6 = f32[256,768]{1,0:T(8,128)S(1)} collective-permute-done((f32[256,768]{1,0:T(8,128)S(1)}, f32[256,768]{1,0:T(8,128)S(1)}, u32[]{:S(2)}, u32[]{:S(2)}) %collective-permute-start.6) | collective-permute-done | bytes 786464 | tf_op jit(solution)/shard_map/ppermute | solution.py:14
  147.6 1.0 convolution_add_fusion
  148.7 0.1 collective-permute-start.7
  148.7 1.0 fusion.69
  149.8 17.7 %collective-permute-done.7 = f32[256,768]{1,0:T(8,128)S(1)} collective-permute-done((f32[256,768]{1,0:T(8,128)S(1)}, f32[256,768]{1,0:T(8,128)S(1)}, u32[]{:S(2)}, u32[]{:S(2)}) %collective-permute-start.7) | collective-permute-done | bytes 786464 | tf_op jit(solution)/shard_map/ppermute | solution.py:14
  167.4 1.0 add.134
  168.5 3.3 fusion.70
  171.8 14.7 %collective-permute-done.8 = f32[256,768]{1,0:T(8,128)} collective-permute-done((f32[256,768]{1,0:T(8,128)}, f32[256,768]{1,0:T(8,128)}, u32[]{:S(2)}, u32[]{:S(2)}) %collective-permute-start.8) | collective-permute-done | bytes 786464 | tf_op jit(solution)/shard_map/ppermute | solution.py:14
  186.5 2.2 add.135
  188.7 72.6 %all-reduce.3.cloned.1.call-done = f32[2048,768]{0,1:T(8,128)} async-done(((f32[2048,768]{0,1:T(8,128)}), f32[2048,768]{0,1:T(8,128)}) %all-reduce.3.cloned.1.call-update) | async-done | bytes 6291472 | tf_op jit(solution)/shard_map/psum | solution.py:74
  261.2 4.8 %multiply_reduce_fusion = f32[2048]{0:T(1024)S(1)} fusion(f32[2048,768]{0,1:T(8,128)} %all-reduce.3.cloned.1.call-done, f32[2048]{0:T(1024)S(1)} %add_sqrt_fusion.1, bf16[2048,768]{0,1:T(8,128)(2,1)} %all-gather.3.cloned.1.call-done), kind=kLoop, calls=%fused_computation.8 | loop fusion | flops 6289408 | bytes 9453568 | tf_op jit(solution)/shard_map/reduce_sum | solution.py:75
  266.0 1.7 copy-done.3
  267.7 1.4 divide_convert_fusion
  269.1 1.7 copy-done.7
  270.8 1.4 convolution_bitcast_fusion
  272.2 13.5 %all-gather.5.cloned.1.call-done = bf16[768,768]{0,1:T(8,128)(2,1)} async-done(((bf16[768,96]{0,1:T(8,128)(2,1)}), bf16[768,768]{0,1:T(8,128)(2,1)}) %all-gather.5.cloned.1.call-update) | async-done | bytes 1179664 | tf_op jit(solution)/shard_map/all_gather | solution.py:82
  285.7 2.8 fusion.60
  288.5 1.4 multiply_reduce_fusion.1
  289.8 2.2 subtract_divide_fusion
  292.1 40.1 %all-reduce.5.cloned.1.call-done = f32[768,96]{0,1:T(8,128)} async-done(((f32[768,96]{0,1:T(8,128)}), f32[768,96]{0,1:T(8,128)}) %all-reduce.5.cloned.1.call-update) | async-done | bytes 294928 | tf_op jit(solution)/shard_map/psum | solution.py:86
  332.2 1.7 copy.18
  (63 shorter events, 0.4 us)
Async XLA Ops:
  7.2 1.9 copy-start
  7.2 4.7 %copy-start.5 = (bf16[256,768]{1,0:T(8,128)(2,1)S(1)}, bf16[256,768]{1,0:T(8,128)(2,1)}, u32[]{:S(2)}) copy-start(bf16[256,768]{1,0:T(8,128)(2,1)} %param.8) | copy-start | bytes 1179652
  7.2 89.0 %all-gather.3.cloned.1.call-start = ((), (), s32[]{:S(2)}) async-start(), calls=%async_computation | async-start | bytes 3538944 | tf_op jit(solution)/shard_map/all_gather | solution.py:53
  11.8 249.4 %all-reduce.3.cloned.1.call-start = ((), (), s32[]{:S(2)}) async-start(), calls=%async_computation.1 | async-start | bytes 12582912 | tf_op jit(solution)/shard_map/psum | solution.py:74
  11.9 4.7 %copy-start.10 = (bf16[256,1536]{1,0:T(8,128)(2,1)S(1)}, bf16[256,1536]{1,0:T(8,128)(2,1)}, u32[]{:S(2)}) copy-start(bf16[256,1536]{1,0:T(8,128)(2,1)} %param.9) | copy-start | bytes 2359300
  12.2 11.0 %copy-start.16 = (bf16[256,768]{1,0:T(8,128)(2,1)}, bf16[256,768]{1,0:T(8,128)(2,1)S(1)}, u32[]{:S(2)}) copy-start(bf16[256,768]{1,0:T(8,128)(2,1)S(1)} %fusion.64) | copy-start | bytes 1179652
  12.2 13.9 %collective-permute-start = (bf16[256,768]{1,0:T(8,128)(2,1)S(1)}, bf16[256,768]{1,0:T(8,128)(2,1)S(1)}, u32[]{:S(2)}, u32[]{:S(2)}) collective-permute-start(bf16[256,768]{1,0:T(8,128)(2,1)S(1)} %fusion.64), channel_id=1, source_target_pairs={{0,8},{8,16},{16,24},{24,0},{1,9},{9,17},{17,25},{25,1},{2,10},{10... | collective-permute-start | bytes 1179656 | tf_op jit(solution)/shard_map/ppermute | solution.py:14
  16.9 6.3 %copy-start.19 = (bf16[256,1536]{1,0:T(8,128)(2,1)}, bf16[256,1536]{1,0:T(8,128)(2,1)S(1)}, u32[]{:S(2)}) copy-start(bf16[256,1536]{1,0:T(8,128)(2,1)S(1)} %fusion.57) | copy-start | bytes 2359300
  16.9 10.3 %copy-start.4 = (bf16[2048,1536]{1,0:T(8,128)(2,1)S(1)}, bf16[2048,1536]{1,0:T(8,128)(2,1)}, u32[]{:S(2)}) copy-start(bf16[2048,1536]{1,0:T(8,128)(2,1)} %param.7) | copy-start | bytes 18874372
  16.9 26.1 %collective-permute-start.1 = (bf16[256,1536]{1,0:T(8,128)(2,1)S(1)}, bf16[256,1536]{1,0:T(8,128)(2,1)}, u32[]{:S(2)}, u32[]{:S(2)}) collective-permute-start(bf16[256,1536]{1,0:T(8,128)(2,1)S(1)} %fusion.57), channel_id=1, source_target_pairs={{0,8},{8,16},{16,24},{24,0},{1,9},{9,17},{17,25},{25,1},{2,10},{10... | collective-permute-start | bytes 2359304 | tf_op jit(solution)/shard_map/ppermute | solution.py:14
  26.1 4.0 %copy-start.21 = (bf16[256,768]{1,0:T(8,128)(2,1)}, bf16[256,768]{1,0:T(8,128)(2,1)S(1)}, u32[]{:S(2)}) copy-start(bf16[256,768]{1,0:T(8,128)(2,1)S(1)} %collective-permute-done) | copy-start | bytes 1179652
  26.1 25.4 %collective-permute-start.2 = (bf16[256,768]{1,0:T(8,128)(2,1)S(1)}, bf16[256,768]{1,0:T(8,128)(2,1)}, u32[]{:S(2)}, u32[]{:S(2)}) collective-permute-start(bf16[256,768]{1,0:T(8,128)(2,1)S(1)} %collective-permute-done), channel_id=1, source_target_pairs={{0,8},{8,16},{16,24},{24,0},{1,9},{9,17},{17,25},{25,1},{2,10},{10... | collective-permute-start | bytes 1179656 | tf_op jit(solution)/shard_map/ppermute | solution.py:14
  30.1 62.6 %copy-start.6 = (bf16[2048,1536]{1,0:T(8,128)(2,1)}, bf16[2048,1536]{1,0:T(8,128)(2,1)S(1)}, u32[]{:S(2)}) copy-start(bf16[2048,1536]{1,0:T(8,128)(2,1)S(1)} %fusion.1) | copy-start | bytes 18874372
  43.1 25.2 %collective-permute-start.3 = (bf16[256,1536]{1,0:T(8,128)(2,1)}, bf16[256,1536]{1,0:T(8,128)(2,1)S(1)}, u32[]{:S(2)}, u32[]{:S(2)}) collective-permute-start(bf16[256,1536]{1,0:T(8,128)(2,1)} %collective-permute-done.1), channel_id=1, source_target_pairs={{0,8},{8,16},{16,24},{24,0},{1,9},{9,17},{17,25},{25,1},{2,10},{10... | collective-permute-start | bytes 2359304 | tf_op jit(solution)/shard_map/ppermute | solution.py:14
  51.5 64.5 %collective-permute-start.4 = (bf16[256,768]{1,0:T(8,128)(2,1)}, bf16[256,768]{1,0:T(8,128)(2,1)}, u32[]{:S(2)}, u32[]{:S(2)}) collective-permute-start(bf16[256,768]{1,0:T(8,128)(2,1)} %collective-permute-done.2), channel_id=1, source_target_pairs={{0,8},{8,16},{16,24},{24,0},{1,9},{9,17},{17,25},{25,1},{2,10},{10... | collective-permute-start | bytes 1179656 | tf_op jit(solution)/shard_map/ppermute | solution.py:14
  68.2 24.5 %collective-permute-start.5 = (bf16[256,1536]{1,0:T(8,128)(2,1)S(1)}, bf16[256,1536]{1,0:T(8,128)(2,1)S(1)}, u32[]{:S(2)}, u32[]{:S(2)}) collective-permute-start(bf16[256,1536]{1,0:T(8,128)(2,1)S(1)} %collective-permute-done.3), channel_id=1, source_target_pairs={{0,8},{8,16},{16,24},{24,0},{1,9},{9,17},{17,25},{25,1},{2,10},{10... | collective-permute-start | bytes 2359304 | tf_op jit(solution)/shard_map/ppermute | solution.py:14
  96.1 2.8 copy-start.1
  99.0 1.0 copy-start.17
  99.0 2.3 slice-start
  100.0 16.0 %copy-start.8 = (bf16[2048,768]{0,1:T(8,128)(2,1)}, bf16[2048,768]{0,1:T(8,128)(2,1)S(1)}, u32[]{:S(2)}) copy-start(bf16[2048,768]{0,1:T(8,128)(2,1)S(1)} %fusion.55) | copy-start | bytes 9437188
  100.0 3.5 %slice-start.1 = ((s8[6291456]{0:T(1024)(128)(4,1)}), s8[4194304]{0:T(1024)(128)(4,1)S(1)}, s32[]{:S(2)}) async-start(s8[6291456]{0:T(1024)(128)(4,1)} %bitcast.38), calls=%async_computation.5 | async-start | bytes 8388608
  100.0 3.6 %copy-start.20 = (bf16[256,1536]{1,0:T(8,128)(2,1)S(1)}, bf16[256,1536]{1,0:T(8,128)(2,1)}, u32[]{:S(2)}) copy-start(bf16[256,1536]{1,0:T(8,128)(2,1)} %copy-done.19) | copy-start | bytes 2359300
  105.8 1.1 copy-start.15
  105.9 1.3 copy-start.22
  105.9 2.1 copy-start.23
  107.9 1.6 copy-start.25
  109.5 5.1 %copy-start.13 = (bf16[2048,256]{1,0:T(8,128)(2,1)}, bf16[2048,256]{1,0:T(8,128)(2,1)S(1)}, u32[]{:S(2)}) copy-start(bf16[2048,256]{1,0:T(8,128)(2,1)S(1)} %fusion.53) | copy-start | bytes 3145732
  112.3 2.3 copy-start.11
  114.7 1.6 copy-start.24
  118.8 1.0 copy-start.18
  124.5 161.2 %all-gather.5.cloned.1.call-start = ((), (), s32[]{:S(2)}) async-start(), calls=%async_computation.2 | async-start | bytes 1327104 | tf_op jit(solution)/shard_map/all_gather | solution.py:82
  124.5 23.1 %copy-start.9 = (bf16[2048,768]{0,1:T(8,128)(2,1)S(1)}, bf16[2048,768]{0,1:T(8,128)(2,1)}, u32[]{:S(2)}) copy-start(bf16[2048,768]{0,1:T(8,128)(2,1)} %copy-done.8) | copy-start | bytes 9437188
  124.5 23.1 %copy-start.14 = (bf16[2048,256]{1,0:T(8,128)(2,1)S(1)}, bf16[2048,256]{1,0:T(8,128)(2,1)}, u32[]{:S(2)}) copy-start(bf16[2048,256]{1,0:T(8,128)(2,1)} %copy-done.13) | copy-start | bytes 3145732
  127.9 20.8 %copy-start.12 = (bf16[2048,256]{1,0:T(8,128)(2,1)S(1)}, bf16[2048,256]{1,0:T(8,128)(2,1)}, u32[]{:S(2)}) copy-start(bf16[2048,256]{1,0:T(8,128)(2,1)} %copy-done.11) | copy-start | bytes 3145732
  128.0 19.7 %collective-permute-start.6 = (f32[256,768]{1,0:T(8,128)S(1)}, f32[256,768]{1,0:T(8,128)S(1)}, u32[]{:S(2)}, u32[]{:S(2)}) collective-permute-start(f32[256,768]{1,0:T(8,128)S(1)} %fusion.68), channel_id=1, source_target_pairs={{0,8},{8,16},{16,24},{24,0},{1,9},{9,17},{17,25},{25,1},{2,10},{10... | collective-permute-start | bytes 2359304 | tf_op jit(solution)/shard_map/ppermute | solution.py:14
  148.7 18.8 %collective-permute-start.7 = (f32[256,768]{1,0:T(8,128)S(1)}, f32[256,768]{1,0:T(8,128)S(1)}, u32[]{:S(2)}, u32[]{:S(2)}) collective-permute-start(f32[256,768]{1,0:T(8,128)S(1)} %convolution_add_fusion), channel_id=1, source_target_pairs={{0,8},{8,16},{16,24},{24,0},{1,9},{9,17},{17,25},{25,1},{2,10},{10... | collective-permute-start | bytes 2359304 | tf_op jit(solution)/shard_map/ppermute | solution.py:14
  168.4 18.1 %collective-permute-start.8 = (f32[256,768]{1,0:T(8,128)}, f32[256,768]{1,0:T(8,128)}, u32[]{:S(2)}, u32[]{:S(2)}) collective-permute-start(f32[256,768]{1,0:T(8,128)} %add.134), channel_id=1, source_target_pairs={{0,8},{8,16},{16,24},{24,0},{1,9},{9,17},{17,25},{25,1},{2,10},{10... | collective-permute-start | bytes 2359304 | tf_op jit(solution)/shard_map/ppermute | solution.py:14
  168.4 163.7 %all-reduce.5.cloned.1.call-start = ((), (), s32[]{:S(2)}) async-start(), calls=%async_computation.3 | async-start | bytes 589824 | tf_op jit(solution)/shard_map/psum | solution.py:86
  188.6 99.8 %collective-permute-start.9 = (f32[256,768]{1,0:T(8,128)}, f32[256,768]{1,0:T(8,128)}, u32[]{:S(2)}, u32[]{:S(2)}) collective-permute-start(f32[256,768]{1,0:T(8,128)} %add.135), channel_id=1, source_target_pairs={{0,8},{8,16},{16,24},{24,0},{1,9},{9,17},{17,25},{25,1},{2,10},{10... | collective-permute-start | bytes 2359304 | tf_op jit(solution)/shard_map/ppermute | solution.py:14
  261.2 4.8 %copy-start.2 = (bf16[2048,768]{0,1:T(8,128)(2,1)S(1)}, bf16[2048,768]{0,1:T(8,128)(2,1)}, u32[]{:S(2)}) copy-start(bf16[2048,768]{0,1:T(8,128)(2,1)} %all-gather.3.cloned.1.call-done) | copy-start | bytes 9437188
  261.2 6.5 %copy-start.3 = (f32[2048,768]{0,1:T(8,128)S(1)}, f32[2048,768]{0,1:T(8,128)}, u32[]{:S(2)}) copy-start(f32[2048,768]{0,1:T(8,128)} %all-reduce.3.cloned.1.call-done) | copy-start | bytes 18874372
  269.1 1.7 copy-start.7
Sparse Core Ops, SparseCore 0:
  11.9 40.9 all-gather.2
  124.6 136.5 all-reduce.2
  262.9 22.7 all-gather.4
  289.0 43.0 all-reduce.4
where the time goes:
time: 341 us; the launch traced here: 340 us
  waiting for transfers between devices  232 us (68%)
  matrix products  46.6 us (14%)
  other arithmetic  26.2 us (8%)
  between operations  14.2 us (4%)
  local copies, waits for them, and re-layouts  11.8 us (3%)
  starting transfers between devices  10 us (3%)
    ppermute x10, waiting for transfers between devices, passed_along(): return lax.ppermute(value, axis, pairs)  105 us
    psum x1, waiting for transfers between devices, per_device(): summed = lax.psum(img_grads, 'tensor')  72.6 us
    psum x1, waiting for transfers between devices, per_device(): grad_head = lax.psum(head_part, 'dp')  40.1 us
    dot_general x4, matrix products, affinity_tile(): lax.dot_general(tea_img_emb, tea_piece, contract, preferred_element_type=...  13.6 us
    all_gather x1, waiting for transfers between devices, per_device(): head_full = lax.all_gather(head, 'tensor', axis=1, tiled=True)  13.5 us
    unnamed x57, local copies, waits for them, and re-layouts  11.8 us
    ppermute x10, starting transfers between devices, passed_along(): return lax.ppermute(value, axis, pairs)  9.83 us
    dot_general x4, matrix products, per_device(): jnp.dot(coef, travel_emb, preferred_element_type=jnp.float32)  9.36 us
  transfers between devices with their start and end apart: 14, of which 11 were waited for; matrix products, arithmetic and copies ran while one was open for 18% of the time, Pallas kernels for 0%

commit v1 on v0

v1 whole, which is shorter than its diff:
```python
import functools
import jax
import jax.numpy as jnp
from jax import lax
from jax.experimental import pallas as pl
from jax.experimental.pallas import tpu as pltpu
from jax.sharding import PartitionSpec as P

logit_scale = 64.0
logit_bias = -2.0
loss_scale = 65536.0
half_scale = 0.5 * logit_scale
half_bias = 0.5 * logit_bias
bf16 = jnp.bfloat16
f32 = jnp.float32
NT = (((1,), (1,)), ((), ()))
TN = (((0,), (0,)), ((), ()))


def params():
    return pltpu.CompilerParams(vmem_limit_bytes=48 * 1024 * 1024)


def cost(flops, moved, trans=0):
    return pl.CostEstimate(flops=int(flops), bytes_accessed=int(moved), transcendentals=int(trans))


def swap(value, axis, mask):
    count = lax.axis_size(axis)
    return lax.ppermute(value, axis, [(source, source ^ mask) for source in range(count)])


def inverse_length(floats):
    return lax.rsqrt(jnp.sum(floats * floats, axis=1, keepdims=True) + 1e-06)


def text_kernel(tea_ref, stu_ref, low_ref, high_ref):
    half, tea_width = low_ref.shape[0], tea_ref.shape[1]
    for place, out_ref in enumerate((low_ref, high_ref)):
        rows = pl.ds(place * half, half)
        tea = tea_ref[rows, :].astype(f32)
        out_ref[:, :tea_width] = (tea * inverse_length(tea)).astype(bf16)
        stu = stu_ref[rows, :].astype(f32)
        out_ref[:, tea_width:] = (stu * inverse_length(stu)).astype(bf16)


def text_parts(tea_txt, stu_txt):
    share, tea_width = tea_txt.shape
    width = tea_width + stu_txt.shape[1]
    part = jax.ShapeDtypeStruct((share // 2, width), bf16)
    return pl.pallas_call(
        text_kernel,
        out_shape=(part, part),
        compiler_params=params(),
        cost_estimate=cost(4 * share * width, 4 * share * width),
    )(tea_txt, stu_txt)


def teacher_kernel(tea_ref, out_ref):
    tea = tea_ref[...].astype(f32)
    out_ref[...] = (tea * inverse_length(tea)).astype(bf16) * half_scale


def teacher_emb(tea_img, chunk):
    rows, width = tea_img.shape
    spec = pl.BlockSpec((chunk, width), lambda i: (i, 0))
    return pl.pallas_call(
        teacher_kernel,
        grid=(rows // chunk,),
        in_specs=[spec],
        out_specs=spec,
        out_shape=jax.ShapeDtypeStruct((rows, width), bf16),
        compiler_params=params(),
        cost_estimate=cost(4 * rows * width, 4 * rows * width),
    )(tea_img)


def proj_kernel(order_ref, images_ref, near_ref, far_ref, proj_ref, emb_ref, head_ref):
    columns = near_ref.shape[1]
    count = near_ref.shape[0]

    @pl.when(pl.program_id(0) == 0)
    def _():
        for k in range(count):
            for place, ref in enumerate((near_ref, far_ref)):
                start = pl.multiple_of(order_ref[2 * k + place] * columns, columns)
                head_ref[pl.ds(start, columns), :] = ref[k]

    proj = lax.dot_general(images_ref[...], head_ref[...], NT, preferred_element_type=f32).astype(bf16)
    floats = proj.astype(f32)
    proj_ref[...] = proj
    emb_ref[...] = (floats * inverse_length(floats)).astype(bf16) * half_scale


def projections(order, images, near, far, chunk):
    rows, depth = images.shape
    count, columns, _ = near.shape
    width = 2 * count * columns
    piece = pl.BlockSpec((count, columns, depth), lambda i, order: (0, 0, 0))
    row = pl.BlockSpec((chunk, width), lambda i, order: (i, 0))
    return pl.pallas_call(
        proj_kernel,
        grid_spec=pltpu.PrefetchScalarGridSpec(
            num_scalar_prefetch=1,
            grid=(rows // chunk,),
            in_specs=[pl.BlockSpec((chunk, depth), lambda i, order: (i, 0)), piece, piece],
            out_specs=[row, row, pl.BlockSpec((width, depth), lambda i, order: (0, 0))],
        ),
        out_shape=(
            jax.ShapeDtypeStruct((rows, width), bf16),
            jax.ShapeDtypeStruct((rows, width), bf16),
            jax.ShapeDtypeStruct((width, depth), bf16),
        ),
        compiler_params=params(),
        cost_estimate=cost(2 * rows * depth * width, 6 * rows * depth),
    )(order, images, near, far)


def pair_tile(tea_ref, emb_ref, texts, grads_ref):
    tea_width = tea_ref.shape[1]
    emb = emb_ref[...]
    target = lax.dot_general(tea_ref[...], texts[:, :tea_width], NT, preferred_element_type=f32)
    student = lax.dot_general(emb, texts[:, tea_width:], NT, preferred_element_type=f32)
    coef = (jnp.tanh(student + half_bias) - jnp.tanh(target + half_bias)).astype(bf16)
    grads_ref[...] += lax.dot_general(coef, emb, TN, preferred_element_type=f32)
    return jnp.dot(coef, texts[:, tea_width:], preferred_element_type=f32)


def early_kernel(count, summed, *refs):
    tea_ref, emb_ref = refs[:2]
    text_refs = refs[2 : 2 + count]
    refs = refs[2 + count :]
    if summed:
        before_ref, refs = refs[0], refs[1:]
    out_ref, grads_ref, texts_ref = refs
    half = text_refs[0].shape[0]

    @pl.when(pl.program_id(0) == 0)
    def _():
        for k in range(count):
            texts_ref[pl.ds(k * half, half), :] = text_refs[k][...]
        grads_ref[...] = jnp.zeros_like(grads_ref)

    grads = pair_tile(tea_ref, emb_ref, texts_ref, grads_ref)
    out_ref[...] = grads + before_ref[...] if summed else grads


def early(tea_emb, emb, texts, before, chunk):
    rows, tea_width = tea_emb.shape
    emb_width = emb.shape[1]
    half, width = texts[0].shape
    count = len(texts)
    size = count * half
    row = lambda wide: pl.BlockSpec((chunk, wide), lambda i: (i, 0))
    whole = lambda shape: pl.BlockSpec(shape, lambda i: (0, 0))
    given = [tea_emb, emb, *texts] + ([] if before is None else [before])
    return pl.pallas_call(
        functools.partial(early_kernel, count, before is not None),
        grid=(rows // chunk,),
        in_specs=[row(tea_width), row(emb_width)]
        + [whole((half, width))] * count
        + ([] if before is None else [row(emb_width)]),
        out_specs=[row(emb_width), whole((size, emb_width))],
        out_shape=(
            jax.ShapeDtypeStruct((rows, emb_width), f32),
            jax.ShapeDtypeStruct((size, emb_width), f32),
        ),
        scratch_shapes=[pltpu.VMEM((size, width), bf16)],
        compiler_params=params(),
        cost_estimate=cost(2 * rows * size * (width + 2 * emb_width), 2 * rows * (width + 4 * emb_width)),
    )(*given)


def late_kernel(count, masks, summed, order_ref, *refs):
    tea_ref, emb_ref, proj_ref, before_ref = refs[:4]
    text_refs = refs[4 : 4 + count]
    refs = refs[4 + count :]
    if summed:
        texts_before_ref, refs = refs[0], refs[1:]
    give_ref, keep_refs, grads_ref, texts_ref = refs[0], refs[1 : 1 + masks], refs[-2], refs[-1]
    half = text_refs[0].shape[0]
    share = tea_ref.shape[0]
    step = pl.program_id(0)

    @pl.when(step == 0)
    def _():
        for k in range(count):
            texts_ref[pl.ds(k * half, half), :] = text_refs[k][...]
        grads_ref[...] = texts_before_ref[...] if summed else jnp.zeros_like(grads_ref)

    grads = pair_tile(tea_ref, emb_ref, texts_ref, grads_ref) + before_ref[...]
    floats = proj_ref[...].astype(f32)
    inverse = inverse_length(floats)
    unit = floats * inverse
    along = jnp.sum(unit * grads, axis=1, keepdims=True)
    part = ((grads - unit * along) * inverse).astype(bf16)
    for k in range(masks):

        @pl.when(step == 2 * k)
        def _(k=k):
            give_ref[pl.ds(k * share, share), :] = part

        @pl.when(step == 2 * k + 1)
        def _(k=k):
            keep_refs[k][...] = part


def late(order, tea_emb, emb, proj, before, texts, texts_before, share):
    rows, tea_width = tea_emb.shape
    emb_width = emb.shape[1]
    half, width = texts[0].shape
    count = len(texts)
    size = count * half
    steps = order.shape[0]
    masks = steps // 2
    row = lambda wide: pl.BlockSpec((share, wide), lambda i, order: (order[i], 0))
    whole = lambda shape: pl.BlockSpec(shape, lambda i, order: (0, 0))
    summed = texts_before is not None
    given = [tea_emb, emb, proj, before, *texts] + ([texts_before] if summed else [])
    out = pl.pallas_call(
        functools.partial(late_kernel, count, masks, summed),
        grid_spec=pltpu.PrefetchScalarGridSpec(
            num_scalar_prefetch=1,
            grid=(steps,),
            in_specs=[row(tea_width), row(emb_width), row(emb_width), row(emb_width)]
            + [whole((half, width))] * count
            + ([whole((size, emb_width))] if summed else []),
            out_specs=[whole((masks * share, emb_width))]
            + [whole((share, emb_width))] * masks
            + [whole((size, emb_width))],
            scratch_shapes=[pltpu.VMEM((size, width), bf16)],
        ),
        out_shape=[jax.ShapeDtypeStruct((masks * share, emb_width), bf16)]
        + [jax.ShapeDtypeStruct((share, emb_width), bf16)] * masks
        + [jax.ShapeDtypeStruct((size, emb_width), f32)],
        compiler_params=params(),
        cost_estimate=cost(
            2 * steps * share * size * (width + 2 * emb_width), 2 * steps * share * (width + 4 * emb_width)
        ),
    )(order, *given)
    return out[0], out[1:-1], out[-1]


def head_kernel(count, order_ref, images_ref, *refs):
    part_refs = refs[:count]
    near_ref, far_ref, total_ref = refs[count:]
    columns = near_ref.shape[0] // count
    step = pl.program_id(0)

    @pl.when(step == 0)
    def _():
        total_ref[...] = jnp.zeros_like(total_ref)

    for k in range(count):

        @pl.when(step == k)
        def _(k=k):
            total_ref[...] += lax.dot_general(
                part_refs[k][...], images_ref[...], TN, preferred_element_type=f32
            )

    @pl.when(step == count - 1)
    def _():
        for k in range(count):
            for place, ref in enumerate((near_ref, far_ref)):
                start = pl.multiple_of(order_ref[2 * k + place] * columns, columns)
                ref[pl.ds(k * columns, columns), :] = total_ref[pl.ds(start, columns), :].astype(bf16)


def head_parts(order, images, parts, columns):
    depth = images.shape[1]
    share, width = parts[0].shape
    count = len(parts)
    whole = lambda shape: pl.BlockSpec(shape, lambda i, order: (0, 0))
    piece = jax.ShapeDtypeStruct((count * columns, depth), bf16)
    return pl.pallas_call(
        functools.partial(head_kernel, count),
        grid_spec=pltpu.PrefetchScalarGridSpec(
            num_scalar_prefetch=1,
            grid=(count,),
            in_specs=[pl.BlockSpec((share, depth), lambda i, order: (order[2 * i], 0))]
            + [whole((share, width))] * count,
            out_specs=[whole(piece.shape)] * 2,
            scratch_shapes=[pltpu.VMEM((width, depth), f32)],
        ),
        out_shape=(piece, piece),
        compiler_params=params(),
        cost_estimate=cost(2 * count * share * width * depth, 4 * count * share * width),
    )(order, images, *parts)


def images_kernel(scale, *refs):
    part_refs, head_ref, out_ref = refs[:-2], refs[-2], refs[-1]
    total = part_refs[0][...].astype(f32)
    for ref in part_refs[1:]:
        total += ref[...].astype(f32)
    out_ref[...] = scale * jnp.dot(total.astype(bf16), head_ref[...], preferred_element_type=f32)


def image_grads(parts, head, scale):
    share, width = parts[0].shape
    depth = head.shape[1]
    return pl.pallas_call(
        functools.partial(images_kernel, scale),
        out_shape=jax.ShapeDtypeStruct((share, depth), f32),
        compiler_params=params(),
        cost_estimate=cost(2 * share * width * depth, 4 * share * width),
    )(*parts, head)


def per_device(images, head, tea_img, stu_txt, tea_txt):
    dp_count = lax.axis_size("dp")
    tensor_count = lax.axis_size("tensor")
    rank = lax.axis_index("tensor")
    rows = images.shape[0]
    columns = head.shape[1]
    share = rows // tensor_count
    half = share // 2
    pairs = tensor_count // 2
    bits = dp_count.bit_length() - 1
    chunk = 2 * share
    factor = 0.5 * logit_scale * loss_scale / (rows * dp_count)

    low, high = text_parts(tea_txt, stu_txt)
    lows, highs = {0: low}, {0: high}
    for stage in range(bits):
        for mask in list(lows):
            lows[mask ^ (1 << stage)] = swap(lows[mask], "dp", 1 << stage)
        for mask in list(highs):
            other = 1 << (bits - 1 - stage)
            highs[mask ^ other] = swap(highs[mask], "dp", other)

    head_t = head.T
    near = jnp.stack([head_t] + [swap(head_t, "tensor", 2 * k) for k in range(1, pairs)])
    far = swap(near, "tensor", 1)
    order = jnp.stack([rank ^ (2 * k + place) for k in range(pairs) for place in range(2)]).astype(jnp.int32)

    tea_emb = teacher_emb(tea_img, chunk)
    proj, emb, head_full = projections(order, images, near, far, chunk)

    text_grads = {}
    image_part, text_grads[0] = early(tea_emb, emb, [lows[0], highs[0]], None, chunk)
    middle = list(range(1, dp_count - 1))
    texts = [part for mask in middle for part in (lows[mask], highs[mask])]
    image_part, grads = early(tea_emb, emb, texts, image_part, chunk)
    for k, mask in enumerate(middle):
        text_grads[mask] = grads[k * share : (k + 1) * share]
    last = dp_count - 1
    first_masks = list(range(pairs // 2, pairs))[::-1]
    second_masks = list(range(pairs // 2))[::-1]
    orders = [
        jnp.stack([rank ^ (2 * k + place) for k in masks for place in (1, 0)]).astype(jnp.int32)
        for masks in (first_masks, second_masks)
    ]
    texts = [lows[last], highs[last]]
    give_a, keep_a, grads = late(orders[0], tea_emb, emb, proj, image_part, texts, None, share)
    take_a = swap(give_a, "tensor", 1)
    give_b, keep_b, grads = late(orders[1], tea_emb, emb, proj, image_part, texts, grads, share)
    take_b = swap(give_b, "tensor", 1)
    text_grads[last] = grads

    reduced = {}
    for masks, keep, take in ((first_masks, keep_a, take_a), (second_masks, keep_b, take_b)):
        for k, mask in enumerate(masks):
            reduced[mask] = keep[k] + take[k * share : (k + 1) * share]
    arrived = [swap(reduced[mask], "tensor", 2 * mask) for mask in range(1, pairs)[::-1]]
    grad_images = image_grads([reduced[0]] + arrived, head_full, factor)

    sums = []
    for part in range(2):
        held = {m: text_grads[m][part * half : (part + 1) * half] for m in range(dp_count)}
        for stage in range(bits):
            bit = 1 << ((bits - 1 - stage) if part == 0 else stage)
            sent = [m for m in sorted(held) if m & bit]
            got = swap(jnp.stack([held[m] for m in sent]).astype(bf16), "dp", bit)
            for k, m in enumerate(sent):
                held[m ^ bit] = held[m ^ bit] + got[k].astype(f32)
                del held[m]
        sums.append(held[0])
    total = jnp.concatenate(sums) * (factor / half_scale)
    stu = stu_txt.astype(f32)
    inverse = inverse_length(stu)
    unit = stu * inverse
    grad_text = (total - unit * jnp.sum(unit * total, axis=1, keepdims=True)) * inverse

    near_part, far_part = head_parts(order, images, [reduced[mask] for mask in range(pairs)], columns)
    summed = near_part + swap(far_part, "tensor", 1)
    pieces = summed.reshape(pairs, columns, images.shape[1])
    own = pieces[0].astype(f32)
    for k in range(1, pairs):
        own = own + swap(pieces[k], "tensor", 2 * k).astype(f32)
    for bit in range(bits):
        rounded = lax.reduce_precision(own, 8, 7)
        own = rounded + swap(rounded.astype(bf16), "dp", 1 << bit).astype(f32)
    grad_head = own.T * factor
    return (grad_images, grad_head, grad_text)


def solution(mesh):
    placed = (
        P("dp", None),
        P(None, "tensor"),
        P("dp", None),
        P(("dp", "tensor"), None),
        P(("dp", "tensor"), None),
    )
    return jax.shard_map(
        per_device,
        mesh=mesh,
        in_specs=placed,
        out_specs=(P(("dp", "tensor"), None), P(None, "tensor"), P(("dp", "tensor"), None)),
        check_vma=False,
    )
```

time: 341 us -> 150 us (0.44)
  waiting for transfers between devices: 232 us -> 48.1 us
  Pallas kernels: 0 us -> 59.6 us
  matrix products: 46.6 us -> 0 us
  other arithmetic: 26.2 us -> 4.43 us
  starting transfers between devices: 10 us -> 30.1 us
  between operations: 14.2 us -> 0.83 us
  local copies, waits for them, and re-layouts: 11.8 us -> 5.9 us
    psum x2 -> x0, waiting for transfers between devices: 113 us -> none  [the longest x1 72.6 us: per_device(): summed = lax.psum(img_grads, 'tensor')]
    pallas_call x0 -> x9, Pallas kernels: none -> 59.6 us  [the longest x2 24.2 us: early(): pl.pallas_call(functools.partial(early_kernel, count, before is not None)...]
    ppermute x10 -> x25, waiting for transfers between devices: 105 us -> 48.1 us  [swap(): lax.ppermute(value, axis, [(source, source ^ mask) for source in range(co...]
    dot_general x19 -> x0, matrix products: 46.6 us -> none  [the longest x4 13.6 us: affinity_tile(): lax.dot_general(tea_img_emb, tea_piece, contract, preferred_element_type=...]
    ppermute x10 -> x25, starting transfers between devices: 9.83 us -> 30.1 us  [swap(): lax.ppermute(value, axis, [(source, source ^ mask) for source in range(co...]
    reduce_sum x6 -> x2, other arithmetic: 15.1 us -> 0.46 us  [the longest x1 0.31 us: per_device(): jnp.sum(unit * total, axis=1, keepdims=True)]
    all_gather x2 -> x0, waiting for transfers between devices: 13.5 us -> none  [the longest x1 13.5 us: per_device(): head_full = lax.all_gather(head, 'tensor', axis=1, tiled=True)]
    unnamed x57 -> x12, local copies, waits for them, and re-layouts: 11.8 us -> 5.73 us
  transfers between devices with their start and end apart: 14 -> 25, of which waited for: 11 -> 8; matrix products, arithmetic and copies ran while one was open for 18% -> 2% of each run, Pallas kernels for 0% -> 29%
where the time goes in v1:
time: 150 us; the launch traced here: 149 us
  Pallas kernels  59.6 us (40%)
  waiting for transfers between devices  48.1 us (32%)
  starting transfers between devices  30.1 us (20%)
  local copies, waits for them, and re-layouts  5.9 us (4%)
  other arithmetic  4.43 us (3%)
    ppermute x25, waiting for transfers between devices, swap(): lax.ppermute(value, axis, [(source, source ^ mask) for source in range(co...  48.1 us
    ppermute x25, starting transfers between devices, swap(): lax.ppermute(value, axis, [(source, source ^ mask) for source in range(co...  30.1 us
    pallas_call x2, Pallas kernels, early(): pl.pallas_call(functools.partial(early_kernel, count, before is not None)...  24.2 us
    pallas_call x2, Pallas kernels, late(): pl.pallas_call(functools.partial(late_kernel, count, masks, summed), grid...  15.9 us
    pallas_call x1, Pallas kernels, projections(): pl.pallas_call(proj_kernel, grid_spec=pltpu.PrefetchScalarGridSpec(num_sc...  7.6 us
    pallas_call x1, Pallas kernels, teacher_emb(): pl.pallas_call(teacher_kernel, grid=(rows // chunk,), in_specs=[spec], ou...  6.96 us
    unnamed x12, local copies, waits for them, and re-layouts  5.73 us
    pallas_call x1, Pallas kernels, head_parts(): pl.pallas_call(functools.partial(head_kernel, count), grid_spec=pltpu.Pre...  3.02 us
  transfers between devices with their start and end apart: 25, of which 8 were waited for; matrix products, arithmetic and copies ran while one was open for 2% of the time, Pallas kernels for 29%

profile of v1, /device:TPU:0, one launch (start us, length us, event | category | flops | bytes accessed | tf_op | source)
XLA Modules:
  0.0 149.0 jit_solution(9989150568477024058)
XLA Ops:
  0.6 5.1 %collective-permute-start.2 = (bf16[96,768]{1,0:T(8,128)(2,1)}, bf16[96,768]{1,0:T(8,128)(2,1)S(1)}, u32[]{:S(2)}, u32[]{:S(2)}) collective-permute-start(bf16[96,768]{1,0:T(8,128)(2,1)} %bitcast.54), channel_id=1, source_target_pairs={{0,6},{1,7},{2,4},{3,5},{4,2},{5,3},{6,0},{7,1},{8,14},{9,15},{10,... | collective-permute-start | bytes 442376 | tf_op jit(solution)/shard_map/ppermute | solution.py:30
  5.7 0.0 collective-permute-start.1
  5.7 0.6 collective-permute-start
  6.4 1.0 copy-done.2
  7.4 1.1 copy-done.5
  8.5 0.4 shard_map.78
  8.9 1.7 %collective-permute-start.4 = (bf16[128,2304]{1,0:T(8,128)(2,1)S(1)}, bf16[128,2304]{1,0:T(8,128)(2,1)S(1)}, u32[]{:S(2)}, u32[]{:S(2)}) collective-permute-start(bf16[128,2304]{1,0:T(8,128)(2,1)S(1)} %get-tuple-element.24.refs_2_), channel_id=1, source_target_pairs={{0,8},{8,0},{16,24},{24,16},{1,9},{9,1},{17,25},{25,17},{2,10},{10... | collective-permute-start | bytes 1769480 | tf_op jit(solution)/shard_map/ppermute | solution.py:30
  10.6 1.5 %collective-permute-start.7 = (bf16[128,2304]{1,0:T(8,128)(2,1)S(1)}, bf16[128,2304]{1,0:T(8,128)(2,1)S(1)}, u32[]{:S(2)}, u32[]{:S(2)}) collective-permute-start(bf16[128,2304]{1,0:T(8,128)(2,1)S(1)} %get-tuple-element.25.refs_3_), channel_id=1, source_target_pairs={{0,16},{8,24},{16,0},{24,8},{1,17},{9,25},{17,1},{25,9},{2,18},{10... | collective-permute-start | bytes 1769480 | tf_op jit(solution)/shard_map/ppermute | solution.py:30
  12.1 0.0 collective-permute-done.2
  12.1 6.3 %collective-permute-done.1 = bf16[96,768]{1,0:T(8,128)(2,1)S(1)} collective-permute-done((bf16[96,768]{1,0:T(8,128)(2,1)}, bf16[96,768]{1,0:T(8,128)(2,1)S(1)}, u32[]{:S(2)}, u32[]{:S(2)}) %collective-permute-start.1) | collective-permute-done | bytes 147488 | tf_op jit(solution)/shard_map/ppermute | solution.py:30
  18.4 1.0 pad_maximum_fusion.near_ref
  19.4 0.1 collective-permute-start.3
  19.5 1.6 %collective-permute-start.5 = (bf16[128,2304]{1,0:T(8,128)(2,1)S(1)}, bf16[128,2304]{1,0:T(8,128)(2,1)S(1)}, u32[]{:S(2)}, u32[]{:S(2)}) collective-permute-start(bf16[128,2304]{1,0:T(8,128)(2,1)S(1)} %get-tuple-element.25.refs_3_), channel_id=1, source_target_pairs={{0,8},{8,0},{16,24},{24,16},{1,9},{9,1},{17,25},{25,17},{2,10},{10... | collective-permute-start | bytes 1769480 | tf_op jit(solution)/shard_map/ppermute | solution.py:30
  21.1 1.5 %collective-permute-start.6 = (bf16[128,2304]{1,0:T(8,128)(2,1)S(1)}, bf16[128,2304]{1,0:T(8,128)(2,1)}, u32[]{:S(2)}, u32[]{:S(2)}) collective-permute-start(bf16[128,2304]{1,0:T(8,128)(2,1)S(1)} %get-tuple-element.24.refs_2_), channel_id=1, source_target_pairs={{0,16},{8,24},{16,0},{24,8},{1,17},{9,25},{17,1},{25,9},{2,18},{10... | collective-permute-start | bytes 1769480 | tf_op jit(solution)/shard_map/ppermute | solution.py:30
  22.6 0.1 stack.91.order_ref
  22.7 7.0 %shard_map.76.refs_0_ = bf16[2048,1536]{1,0:T(8,128)(2,1)} custom-call(bf16[2048,1536]{1,0:T(8,128)(2,1)} %tea_ref.2), custom_call_target="tpu_custom_call" | custom-call | flops 12582912 | bytes 12582912 | tf_op jit(solution)/shard_map/pallas_call | solution.py:67
  29.6 0.1 pad_add_fusion.order_ref
  29.7 0.1 pad_add_fusion.1.order_ref
  29.8 0.5 collective-permute-start.8
  30.3 0.5 collective-permute-start.9
  30.8 7.6 %shard_map.77 = (bf16[2048,768]{1,0:T(8,128)(2,1)S(1)}, bf16[2048,768]{1,0:T(8,128)(2,1)}, bf16[768,768]{1,0:T(8,128)(2,1)S(1)}) custom-call(s32[8]{0:T(128)S(1)} %stack.91.order_ref, bf16[2048,768]{1,0:T(8,128)(2,1)} %images_ref.3, bf16[4,96,768]{2,1,0:T(8,128)(2,1)S(1)} %pad_maximum_fusion.near_ref, bf16[4,96,768]{2,1,0:T(8,128)(2,1)} %collective-permute-done.3.far_ref), custom_call_target="tpu_custom_call" | custom-call | flops 2415919104 | bytes 9437184 | tf_op jit(solution)/shard_map/pallas_call | solution.py:101
  38.5 1.7 %copy-done = bf16[2048,768]{1,0:T(8,128)(2,1)} copy-done((bf16[2048,768]{1,0:T(8,128)(2,1)}, bf16[2048,768]{1,0:T(8,128)(2,1)S(1)}, u32[]{:S(2)}) %copy-start) | copy-done | bytes 3145752
  40.2 1.9 %copy-done.1 = bf16[2048,768]{1,0:T(8,128)(2,1)S(1)} copy-done((bf16[2048,768]{1,0:T(8,128)(2,1)S(1)}, bf16[2048,768]{1,0:T(8,128)(2,1)}, u32[]{:S(2)}) %copy-start.1) | copy-done | bytes 3145752
  42.0 10.3 %shard_map.79 = (f32[2048,768]{1,0:T(8,128)}, f32[256,768]{1,0:T(8,128)S(1)}) custom-call(bf16[2048,1536]{1,0:T(8,128)(2,1)} %shard_map.76.refs_0_, bf16[2048,768]{1,0:T(8,128)(2,1)S(1)} %copy-done.1, bf16[128,2304]{1,0:T(8,128)(2,1)S(1)} %get-tuple-element.24.refs_2_, bf16[128,2304]{1,0:T(8,128)(2,1)S(1)} %get-tuple-element.25.refs_3_), custom_call_target="tpu_custom_call" | custom-call | flops 4026531840 | bytes 22020096 | tf_op jit(solution)/shard_map/pallas_call | solution.py:157
  52.4 13.9 %shard_map.80 = (f32[2048,768]{1,0:T(8,128)}, f32[512,768]{1,0:T(8,128)S(1)}) custom-call(bf16[2048,1536]{1,0:T(8,128)(2,1)} %shard_map.76.refs_0_, bf16[2048,768]{1,0:T(8,128)(2,1)} %get-tuple-element.22.refs_1_, bf16[128,2304]{1,0:T(8,128)(2,1)S(1)} %collective-permute-done.4.refs_2_, bf16[128,2304]{1,0:T(8,128)(2,1)S(1)} %collective-permute-done.5.refs_3_, ...), custom_call_target="tpu_custom_call" | custom-call | flops 8053063680 | bytes 22020096 | tf_op jit(solution)/shard_map/pallas_call | solution.py:157
  66.3 8.0 %shard_map.81 = (bf16[512,768]{1,0:T(8,128)(2,1)S(1)}, bf16[256,768]{1,0:T(8,128)(2,1)S(1)}, bf16[256,768]{1,0:T(8,128)(2,1)S(1)}, f32[256,768]{1,0:T(8,128)S(1)}) custom-call(s32[4]{0:T(128)S(1)} %pad_add_fusion.1.order_ref, bf16[2048,1536]{1,0:T(8,128)(2,1)} %shard_map.76.refs_0_, bf16[2048,768]{1,0:T(8,128)(2,1)} %get-tuple-element.22.refs_1_, ...), custom_call_target="tpu_custom_call" | custom-call | flops 2013265920 | bytes 11010048 | tf_op jit(solution)/shard_map/pallas_call | solution.py:220
  74.3 8.0 %shard_map.82 = (bf16[512,768]{1,0:T(8,128)(2,1)S(1)}, bf16[256,768]{1,0:T(8,128)(2,1)S(1)}, bf16[256,768]{1,0:T(8,128)(2,1)S(1)}, f32[256,768]{1,0:T(8,128)S(1)}) custom-call(s32[4]{0:T(128)S(1)} %pad_add_fusion.order_ref, bf16[2048,1536]{1,0:T(8,128)(2,1)} %shard_map.76.refs_0_, bf16[2048,768]{1,0:T(8,128)(2,1)} %get-tuple-element.22.refs_1_, ...), custom_call_target="tpu_custom_call" | custom-call | flops 2013265920 | bytes 11010048 | tf_op jit(solution)/shard_map/pallas_call | solution.py:220
  82.2 0.1 collective-permute-start.10
  82.3 0.5 collective-permute-start.11
  82.8 0.1 convert.22
  82.9 0.1 slice_bitcast_fusion.6
  83.0 0.0 copy-start.4
  83.1 1.6 %collective-permute-start.21 = (bf16[2,128,768]{2,1,0:T(8,128)(2,1)S(1)}, bf16[2,128,768]{2,1,0:T(8,128)(2,1)S(1)}, u32[]{:S(2)}, u32[]{:S(2)}) collective-permute-start(bf16[2,128,768]{2,1,0:T(8,128)(2,1)S(1)} %pad_maximum_fusion.1), channel_id=1, source_target_pairs={{0,16},{8,24},{16,0},{24,8},{1,17},{9,25},{17,1},{25,9},{2,18},{10... | collective-permute-start | bytes 1179656 | tf_op jit(solution)/shard_map/ppermute | solution.py:30
  84.7 1.6 %collective-permute-start.23 = (bf16[2,128,768]{2,1,0:T(8,128)(2,1)S(1)}, bf16[2,128,768]{2,1,0:T(8,128)(2,1)S(1)}, u32[]{:S(2)}, u32[]{:S(2)}) collective-permute-start(bf16[2,128,768]{2,1,0:T(8,128)(2,1)S(1)} %pad_maximum_fusion.2), channel_id=1, source_target_pairs={{0,8},{8,0},{16,24},{24,16},{1,9},{9,1},{17,25},{25,17},{2,10},{10... | collective-permute-start | bytes 1179656 | tf_op jit(solution)/shard_map/ppermute | solution.py:30
  86.2 0.1 slice_add_fusion
  86.3 0.0 copy-start.3
  86.3 0.1 slice_add_fusion.1
  86.4 3.0 %shard_map.84 = (bf16[384,768]{1,0:T(8,128)(2,1)S(1)}, bf16[384,768]{1,0:T(8,128)(2,1)S(1)}) custom-call(s32[8]{0:T(128)S(1)} %stack.91.order_ref, bf16[2048,768]{1,0:T(8,128)(2,1)S(1)} %copy-done.4, bf16[256,768]{1,0:T(8,128)(2,1)S(1)} %get-tuple-element.48.refs_0_, bf16[256,768]{1,0:T(8,128)(2,1)S(1)} %get-tuple-element.47.refs_1_, ...), custom_call_target="tpu_custom_call" | custom-call | flops 1207959552 | bytes 3145728 | tf_op jit(solution)/shard_map/pallas_call | solution.py:276
  89.5 0.1 collective-permute-start.15
  89.6 0.2 fusion.5
  89.7 4.5 %collective-permute-done.21 = bf16[2,128,768]{2,1,0:T(8,128)(2,1)S(1)} collective-permute-done((bf16[2,128,768]{2,1,0:T(8,128)(2,1)S(1)}, bf16[2,128,768]{2,1,0:T(8,128)(2,1)S(1)}, u32[]{:S(2)}, u32[]{:S(2)}) %collective-permute-start.21) | collective-permute-done | bytes 393248 | tf_op jit(solution)/shard_map/ppermute | solution.py:30
  94.2 1.3 collective-permute-done.23
  95.6 0.1 fusion.8
  95.6 1.6 %collective-permute-start.22 = (bf16[1,128,768]{2,1,0:T(8,128)(2,1)S(1)}, bf16[1,128,768]{2,1,0:T(8,128)(2,1)S(1)}, u32[]{:S(2)}, u32[]{:S(2)}) collective-permute-start(bf16[1,128,768]{2,1,0:T(8,128)(2,1)S(1)} %get-tuple-element.41), channel_id=1, source_target_pairs={{0,8},{8,0},{16,24},{24,16},{1,9},{9,1},{17,25},{25,17},{2,10},{10... | collective-permute-start | bytes 589832 | tf_op jit(solution)/shard_map/ppermute | solution.py:30
  97.2 0.5 collective-permute-start.24
  97.7 0.1 add.63
  97.9 2.6 %collective-permute-start.18 = (bf16[96,768]{1,0:T(8,128)(2,1)S(1)}, bf16[96,768]{1,0:T(8,128)(2,1)S(1)}, u32[]{:S(2)}, u32[]{:S(2)}) collective-permute-start(bf16[96,768]{1,0:T(8,128)(2,1)S(1)} %get-tuple-element.52), channel_id=1, source_target_pairs={{0,6},{1,7},{2,4},{3,5},{4,2},{5,3},{6,0},{7,1},{8,14},{9,15},{10,... | collective-permute-start | bytes 442376 | tf_op jit(solution)/shard_map/ppermute | solution.py:30
  100.5 1.9 %collective-permute-start.16 = (bf16[96,768]{1,0:T(8,128)(2,1)S(1)}, bf16[96,768]{1,0:T(8,128)(2,1)S(1)}, u32[]{:S(2)}, u32[]{:S(2)}) collective-permute-start(bf16[96,768]{1,0:T(8,128)(2,1)S(1)} %get-tuple-element.51), channel_id=1, source_target_pairs={{0,2},{1,3},{2,0},{3,1},{4,6},{5,7},{6,4},{7,5},{8,10},{9,11},{10,... | collective-permute-start | bytes 442376 | tf_op jit(solution)/shard_map/ppermute | solution.py:30
  102.3 0.5 collective-permute-done.24
  102.9 0.1 convert_add_fusion.3
  103.0 3.6 %collective-permute-done.18 = bf16[96,768]{1,0:T(8,128)(2,1)S(1)} collective-permute-done((bf16[96,768]{1,0:T(8,128)(2,1)S(1)}, bf16[96,768]{1,0:T(8,128)(2,1)S(1)}, u32[]{:S(2)}, u32[]{:S(2)}) %collective-permute-start.18) | collective-permute-done | bytes 147488 | tf_op jit(solution)/shard_map/ppermute | solution.py:30
  106.5 5.2 %collective-permute-done.17 = bf16[96,768]{1,0:T(8,128)(2,1)S(1)} collective-permute-done((bf16[96,768]{1,0:T(8,128)(2,1)S(1)}, bf16[96,768]{1,0:T(8,128)(2,1)S(1)}, u32[]{:S(2)}, u32[]{:S(2)}) %collective-permute-start.17) | collective-permute-done | bytes 147488 | tf_op jit(solution)/shard_map/ppermute | solution.py:30
  111.8 0.1 fusion.11
  111.8 0.6 collective-permute-start.19
  112.5 0.3 fusion.2
  112.8 1.4 collective-permute-start.12
  114.2 3.0 %collective-permute-start.14 = (bf16[256,768]{1,0:T(8,128)(2,1)S(1)}, bf16[256,768]{1,0:T(8,128)(2,1)S(1)}, u32[]{:S(2)}, u32[]{:S(2)}) collective-permute-start(bf16[256,768]{1,0:T(8,128)(2,1)S(1)} %get-tuple-element.47.refs_1_), channel_id=1, source_target_pairs={{0,2},{1,3},{2,0},{3,1},{4,6},{5,7},{6,4},{7,5},{8,10},{9,11},{10,... | collective-permute-start | bytes 1179656 | tf_op jit(solution)/shard_map/ppermute | solution.py:30
  117.2 0.1 fusion.10
  117.3 1.6 %collective-permute-start.20 = (bf16[96,768]{1,0:T(8,128)(2,1)S(1)}, bf16[96,768]{1,0:T(8,128)(2,1)S(1)}, u32[]{:S(2)}, u32[]{:S(2)}) collective-permute-start(bf16[96,768]{1,0:T(8,128)(2,1)S(1)} %fusion.10), channel_id=1, source_target_pairs={{0,16},{8,24},{16,0},{24,8},{1,17},{9,25},{17,1},{25,9},{2,18},{10... | collective-permute-start | bytes 442376 | tf_op jit(solution)/shard_map/ppermute | solution.py:30
  118.9 1.1 fusion.4
  120.0 6.8 %collective-permute-done.12.refs_1_ = bf16[256,768]{1,0:T(8,128)(2,1)S(1)} collective-permute-done((bf16[256,768]{1,0:T(8,128)(2,1)S(1)}, bf16[256,768]{1,0:T(8,128)(2,1)S(1)}, u32[]{:S(2)}, u32[]{:S(2)}) %collective-permute-start.12) | collective-permute-done | bytes 393248 | tf_op jit(solution)/shard_map/ppermute | solution.py:30
  126.8 19.9 %collective-permute-done.13.refs_2_ = bf16[256,768]{1,0:T(8,128)(2,1)S(1)} collective-permute-done((bf16[256,768]{1,0:T(8,128)(2,1)S(1)}, bf16[256,768]{1,0:T(8,128)(2,1)S(1)}, u32[]{:S(2)}, u32[]{:S(2)}) %collective-permute-start.13) | collective-permute-done | bytes 393248 | tf_op jit(solution)/shard_map/ppermute | solution.py:30
  146.6 1.5 shard_map.83
  148.1 0.9 multiply_bitcast_fusion
  (29 shorter events, 0.2 us)
Async XLA Ops:
  0.6 11.5 %collective-permute-start.2 = (bf16[96,768]{1,0:T(8,128)(2,1)}, bf16[96,768]{1,0:T(8,128)(2,1)S(1)}, u32[]{:S(2)}, u32[]{:S(2)}) collective-permute-start(bf16[96,768]{1,0:T(8,128)(2,1)} %bitcast.54), channel_id=1, source_target_pairs={{0,6},{1,7},{2,4},{3,5},{4,2},{5,3},{6,0},{7,1},{8,14},{9,15},{10,... | collective-permute-start | bytes 442376 | tf_op jit(solution)/shard_map/ppermute | solution.py:30
  5.7 12.7 %collective-permute-start.1 = (bf16[96,768]{1,0:T(8,128)(2,1)}, bf16[96,768]{1,0:T(8,128)(2,1)S(1)}, u32[]{:S(2)}, u32[]{:S(2)}) collective-permute-start(bf16[96,768]{1,0:T(8,128)(2,1)} %bitcast.55), channel_id=1, source_target_pairs={{0,4},{1,5},{2,6},{3,7},{4,0},{5,1},{6,2},{7,3},{8,12},{9,13},{10,... | collective-permute-start | bytes 442376 | tf_op jit(solution)/shard_map/ppermute | solution.py:30
  5.7 12.7 %collective-permute-start = (bf16[96,768]{1,0:T(8,128)(2,1)}, bf16[96,768]{1,0:T(8,128)(2,1)S(1)}, u32[]{:S(2)}, u32[]{:S(2)}) collective-permute-start(bf16[96,768]{1,0:T(8,128)(2,1)} %bitcast.56), channel_id=1, source_target_pairs={{0,2},{1,3},{2,0},{3,1},{4,6},{5,7},{6,4},{7,5},{8,10},{9,11},{10,... | collective-permute-start | bytes 442376 | tf_op jit(solution)/shard_map/ppermute | solution.py:30
  6.4 1.0 copy-start.2
  7.4 1.1 copy-start.5
  8.9 20.9 %collective-permute-start.4 = (bf16[128,2304]{1,0:T(8,128)(2,1)S(1)}, bf16[128,2304]{1,0:T(8,128)(2,1)S(1)}, u32[]{:S(2)}, u32[]{:S(2)}) collective-permute-start(bf16[128,2304]{1,0:T(8,128)(2,1)S(1)} %get-tuple-element.24.refs_2_), channel_id=1, source_target_pairs={{0,8},{8,0},{16,24},{24,16},{1,9},{9,1},{17,25},{25,17},{2,10},{10... | collective-permute-start | bytes 1769480 | tf_op jit(solution)/shard_map/ppermute | solution.py:30
  10.6 19.7 %collective-permute-start.7 = (bf16[128,2304]{1,0:T(8,128)(2,1)S(1)}, bf16[128,2304]{1,0:T(8,128)(2,1)S(1)}, u32[]{:S(2)}, u32[]{:S(2)}) collective-permute-start(bf16[128,2304]{1,0:T(8,128)(2,1)S(1)} %get-tuple-element.25.refs_3_), channel_id=1, source_target_pairs={{0,16},{8,24},{16,0},{24,8},{1,17},{9,25},{17,1},{25,9},{2,18},{10... | collective-permute-start | bytes 1769480 | tf_op jit(solution)/shard_map/ppermute | solution.py:30
  19.4 11.4 %collective-permute-start.3 = (bf16[4,96,768]{2,1,0:T(8,128)(2,1)S(1)}, bf16[4,96,768]{2,1,0:T(8,128)(2,1)}, u32[]{:S(2)}, u32[]{:S(2)}) collective-permute-start(bf16[4,96,768]{2,1,0:T(8,128)(2,1)S(1)} %pad_maximum_fusion.near_ref), channel_id=1, source_target_pairs={{0,1},{1,0},{2,3},{3,2},{4,5},{5,4},{6,7},{7,6},{8,9},{9,8},{10,11... | collective-permute-start | bytes 1769480 | tf_op jit(solution)/shard_map/ppermute | solution.py:30
  19.5 32.9 %collective-permute-start.5 = (bf16[128,2304]{1,0:T(8,128)(2,1)S(1)}, bf16[128,2304]{1,0:T(8,128)(2,1)S(1)}, u32[]{:S(2)}, u32[]{:S(2)}) collective-permute-start(bf16[128,2304]{1,0:T(8,128)(2,1)S(1)} %get-tuple-element.25.refs_3_), channel_id=1, source_target_pairs={{0,8},{8,0},{16,24},{24,16},{1,9},{9,1},{17,25},{25,17},{2,10},{10... | collective-permute-start | bytes 1769480 | tf_op jit(solution)/shard_map/ppermute | solution.py:30
  21.1 31.3 %collective-permute-start.6 = (bf16[128,2304]{1,0:T(8,128)(2,1)S(1)}, bf16[128,2304]{1,0:T(8,128)(2,1)}, u32[]{:S(2)}, u32[]{:S(2)}) collective-permute-start(bf16[128,2304]{1,0:T(8,128)(2,1)S(1)} %get-tuple-element.24.refs_2_), channel_id=1, source_target_pairs={{0,16},{8,24},{16,0},{24,8},{1,17},{9,25},{17,1},{25,9},{2,18},{10... | collective-permute-start | bytes 1769480 | tf_op jit(solution)/shard_map/ppermute | solution.py:30
  29.8 36.5 %collective-permute-start.8 = (bf16[128,2304]{1,0:T(8,128)(2,1)S(1)}, bf16[128,2304]{1,0:T(8,128)(2,1)S(1)}, u32[]{:S(2)}, u32[]{:S(2)}) collective-permute-start(bf16[128,2304]{1,0:T(8,128)(2,1)S(1)} %collective-permute-done.4.refs_2_), channel_id=1, source_target_pairs={{0,16},{8,24},{16,0},{24,8},{1,17},{9,25},{17,1},{25,9},{2,18},{10... | collective-permute-start | bytes 1769480 | tf_op jit(solution)/shard_map/ppermute | solution.py:30
  30.3 36.0 %collective-permute-start.9 = (bf16[128,2304]{1,0:T(8,128)(2,1)S(1)}, bf16[128,2304]{1,0:T(8,128)(2,1)S(1)}, u32[]{:S(2)}, u32[]{:S(2)}) collective-permute-start(bf16[128,2304]{1,0:T(8,128)(2,1)S(1)} %collective-permute-done.7.refs_5_), channel_id=1, source_target_pairs={{0,8},{8,0},{16,24},{24,16},{1,9},{9,1},{17,25},{25,17},{2,10},{10... | collective-permute-start | bytes 1769480 | tf_op jit(solution)/shard_map/ppermute | solution.py:30
  38.4 1.7 %copy-start = (bf16[2048,768]{1,0:T(8,128)(2,1)}, bf16[2048,768]{1,0:T(8,128)(2,1)S(1)}, u32[]{:S(2)}) copy-start(bf16[2048,768]{1,0:T(8,128)(2,1)S(1)} %get-tuple-element.23.refs_2_) | copy-start | bytes 9437188
  40.2 1.9 %copy-start.1 = (bf16[2048,768]{1,0:T(8,128)(2,1)S(1)}, bf16[2048,768]{1,0:T(8,128)(2,1)}, u32[]{:S(2)}) copy-start(bf16[2048,768]{1,0:T(8,128)(2,1)} %get-tuple-element.22.refs_1_) | copy-start | bytes 9437188
  82.2 4.0 %collective-permute-start.10 = (bf16[512,768]{1,0:T(8,128)(2,1)S(1)}, bf16[512,768]{1,0:T(8,128)(2,1)S(1)}, u32[]{:S(2)}, u32[]{:S(2)}) collective-permute-start(bf16[512,768]{1,0:T(8,128)(2,1)S(1)} %get-tuple-element.30), channel_id=1, source_target_pairs={{0,1},{1,0},{2,3},{3,2},{4,5},{5,4},{6,7},{7,6},{8,9},{9,8},{10,11... | collective-permute-start | bytes 2359304 | tf_op jit(solution)/shard_map/ppermute | solution.py:30
  82.3 4.0 %collective-permute-start.11 = (bf16[512,768]{1,0:T(8,128)(2,1)S(1)}, bf16[512,768]{1,0:T(8,128)(2,1)S(1)}, u32[]{:S(2)}, u32[]{:S(2)}) collective-permute-start(bf16[512,768]{1,0:T(8,128)(2,1)S(1)} %get-tuple-element.32), channel_id=1, source_target_pairs={{0,1},{1,0},{2,3},{3,2},{4,5},{5,4},{6,7},{7,6},{8,9},{9,8},{10,11... | collective-permute-start | bytes 2359304 | tf_op jit(solution)/shard_map/ppermute | solution.py:30
  83.0 3.4 %copy-start.4 = (bf16[2048,768]{1,0:T(8,128)(2,1)S(1)}, bf16[2048,768]{1,0:T(8,128)(2,1)}, u32[]{:S(2)}) copy-start(bf16[2048,768]{1,0:T(8,128)(2,1)} %images_ref.3) | copy-start | bytes 9437188
  83.1 11.2 %collective-permute-start.21 = (bf16[2,128,768]{2,1,0:T(8,128)(2,1)S(1)}, bf16[2,128,768]{2,1,0:T(8,128)(2,1)S(1)}, u32[]{:S(2)}, u32[]{:S(2)}) collective-permute-start(bf16[2,128,768]{2,1,0:T(8,128)(2,1)S(1)} %pad_maximum_fusion.1), channel_id=1, source_target_pairs={{0,16},{8,24},{16,0},{24,8},{1,17},{9,25},{17,1},{25,9},{2,18},{10... | collective-permute-start | bytes 1179656 | tf_op jit(solution)/shard_map/ppermute | solution.py:30
  84.7 10.9 %collective-permute-start.23 = (bf16[2,128,768]{2,1,0:T(8,128)(2,1)S(1)}, bf16[2,128,768]{2,1,0:T(8,128)(2,1)S(1)}, u32[]{:S(2)}, u32[]{:S(2)}) collective-permute-start(bf16[2,128,768]{2,1,0:T(8,128)(2,1)S(1)} %pad_maximum_fusion.2), channel_id=1, source_target_pairs={{0,8},{8,0},{16,24},{24,16},{1,9},{9,1},{17,25},{25,17},{2,10},{10... | collective-permute-start | bytes 1179656 | tf_op jit(solution)/shard_map/ppermute | solution.py:30
  86.3 3.2 %copy-start.3 = (bf16[256,768]{1,0:T(8,128)(2,1)S(1)}, bf16[256,768]{1,0:T(8,128)(2,1)}, u32[]{:S(2)}) copy-start(bf16[256,768]{1,0:T(8,128)(2,1)} %stu_ref.1) | copy-start | bytes 1179652
  89.5 8.2 %collective-permute-start.15 = (bf16[384,768]{1,0:T(8,128)(2,1)S(1)}, bf16[384,768]{1,0:T(8,128)(2,1)S(1)}, u32[]{:S(2)}, u32[]{:S(2)}) collective-permute-start(bf16[384,768]{1,0:T(8,128)(2,1)S(1)} %get-tuple-element.37), channel_id=1, source_target_pairs={{0,1},{1,0},{2,3},{3,2},{4,5},{5,4},{6,7},{7,6},{8,9},{9,8},{10,11... | collective-permute-start | bytes 1769480 | tf_op jit(solution)/shard_map/ppermute | solution.py:30
  95.6 6.7 %collective-permute-start.22 = (bf16[1,128,768]{2,1,0:T(8,128)(2,1)S(1)}, bf16[1,128,768]{2,1,0:T(8,128)(2,1)S(1)}, u32[]{:S(2)}, u32[]{:S(2)}) collective-permute-start(bf16[1,128,768]{2,1,0:T(8,128)(2,1)S(1)} %get-tuple-element.41), channel_id=1, source_target_pairs={{0,8},{8,0},{16,24},{24,16},{1,9},{9,1},{17,25},{25,17},{2,10},{10... | collective-permute-start | bytes 589832 | tf_op jit(solution)/shard_map/ppermute | solution.py:30
  97.2 5.7 %collective-permute-start.24 = (bf16[1,128,768]{2,1,0:T(8,128)(2,1)S(1)}, bf16[1,128,768]{2,1,0:T(8,128)(2,1)S(1)}, u32[]{:S(2)}, u32[]{:S(2)}) collective-permute-start(bf16[1,128,768]{2,1,0:T(8,128)(2,1)S(1)} %get-tuple-element.42), channel_id=1, source_target_pairs={{0,16},{8,24},{16,0},{24,8},{1,17},{9,25},{17,1},{25,9},{2,18},{10... | collective-permute-start | bytes 589832 | tf_op jit(solution)/shard_map/ppermute | solution.py:30
  97.9 8.6 %collective-permute-start.18 = (bf16[96,768]{1,0:T(8,128)(2,1)S(1)}, bf16[96,768]{1,0:T(8,128)(2,1)S(1)}, u32[]{:S(2)}, u32[]{:S(2)}) collective-permute-start(bf16[96,768]{1,0:T(8,128)(2,1)S(1)} %get-tuple-element.52), channel_id=1, source_target_pairs={{0,6},{1,7},{2,4},{3,5},{4,2},{5,3},{6,0},{7,1},{8,14},{9,15},{10,... | collective-permute-start | bytes 442376 | tf_op jit(solution)/shard_map/ppermute | solution.py:30
  100.5 11.3 %collective-permute-start.17 = (bf16[96,768]{1,0:T(8,128)(2,1)S(1)}, bf16[96,768]{1,0:T(8,128)(2,1)S(1)}, u32[]{:S(2)}, u32[]{:S(2)}) collective-permute-start(bf16[96,768]{1,0:T(8,128)(2,1)S(1)} %get-tuple-element.53), channel_id=1, source_target_pairs={{0,4},{1,5},{2,6},{3,7},{4,0},{5,1},{6,2},{7,3},{8,12},{9,13},{10,... | collective-permute-start | bytes 442376 | tf_op jit(solution)/shard_map/ppermute | solution.py:30
  100.5 11.3 %collective-permute-start.16 = (bf16[96,768]{1,0:T(8,128)(2,1)S(1)}, bf16[96,768]{1,0:T(8,128)(2,1)S(1)}, u32[]{:S(2)}, u32[]{:S(2)}) collective-permute-start(bf16[96,768]{1,0:T(8,128)(2,1)S(1)} %get-tuple-element.51), channel_id=1, source_target_pairs={{0,2},{1,3},{2,0},{3,1},{4,6},{5,7},{6,4},{7,5},{8,10},{9,11},{10,... | collective-permute-start | bytes 442376 | tf_op jit(solution)/shard_map/ppermute | solution.py:30
  111.8 5.4 %collective-permute-start.19 = (bf16[96,768]{1,0:T(8,128)(2,1)S(1)}, bf16[96,768]{1,0:T(8,128)(2,1)S(1)}, u32[]{:S(2)}, u32[]{:S(2)}) collective-permute-start(bf16[96,768]{1,0:T(8,128)(2,1)S(1)} %fusion.11), channel_id=1, source_target_pairs={{0,8},{8,0},{16,24},{24,16},{1,9},{9,1},{17,25},{25,17},{2,10},{10... | collective-permute-start | bytes 442376 | tf_op jit(solution)/shard_map/ppermute | solution.py:30
  112.8 14.0 %collective-permute-start.12 = (bf16[256,768]{1,0:T(8,128)(2,1)S(1)}, bf16[256,768]{1,0:T(8,128)(2,1)S(1)}, u32[]{:S(2)}, u32[]{:S(2)}) collective-permute-start(bf16[256,768]{1,0:T(8,128)(2,1)S(1)} %get-tuple-element.50.refs_3_), channel_id=1, source_target_pairs={{0,6},{1,7},{2,4},{3,5},{4,2},{5,3},{6,0},{7,1},{8,14},{9,15},{10,... | collective-permute-start | bytes 1179656 | tf_op jit(solution)/shard_map/ppermute | solution.py:30
  114.2 32.4 %collective-permute-start.13 = (bf16[256,768]{1,0:T(8,128)(2,1)S(1)}, bf16[256,768]{1,0:T(8,128)(2,1)S(1)}, u32[]{:S(2)}, u32[]{:S(2)}) collective-permute-start(bf16[256,768]{1,0:T(8,128)(2,1)S(1)} %get-tuple-element.49.refs_2_), channel_id=1, source_target_pairs={{0,4},{1,5},{2,6},{3,7},{4,0},{5,1},{6,2},{7,3},{8,12},{9,13},{10,... | collective-permute-start | bytes 1179656 | tf_op jit(solution)/shard_map/ppermute | solution.py:30
  114.2 32.4 %collective-permute-start.14 = (bf16[256,768]{1,0:T(8,128)(2,1)S(1)}, bf16[256,768]{1,0:T(8,128)(2,1)S(1)}, u32[]{:S(2)}, u32[]{:S(2)}) collective-permute-start(bf16[256,768]{1,0:T(8,128)(2,1)S(1)} %get-tuple-element.47.refs_1_), channel_id=1, source_target_pairs={{0,2},{1,3},{2,0},{3,1},{4,6},{5,7},{6,4},{7,5},{8,10},{9,11},{10,... | collective-permute-start | bytes 1179656 | tf_op jit(solution)/shard_map/ppermute | solution.py:30
  117.3 30.8 %collective-permute-start.20 = (bf16[96,768]{1,0:T(8,128)(2,1)S(1)}, bf16[96,768]{1,0:T(8,128)(2,1)S(1)}, u32[]{:S(2)}, u32[]{:S(2)}) collective-permute-start(bf16[96,768]{1,0:T(8,128)(2,1)S(1)} %fusion.10), channel_id=1, source_target_pairs={{0,16},{8,24},{16,0},{24,8},{1,17},{9,25},{17,1},{25,9},{2,18},{10... | collective-permute-start | bytes 442376 | tf_op jit(solution)/shard_map/ppermute | solution.py:30

commit v2 on v1

--- a/solution.py
+++ b/solution.py
@@ -1,4 +1,5 @@
 import functools
+import math
 import jax
 import jax.numpy as jnp
 from jax import lax
@@ -18,7 +19,14 @@
 
 
 def params():
-    return pltpu.CompilerParams(vmem_limit_bytes=48 * 1024 * 1024)
+    return pltpu.CompilerParams(vmem_limit_bytes=22 * 1024 * 1024)
+
+
+resident = pl.BlockSpec(memory_space=pltpu.VMEM)
+
+
+def pinned(value):
+    return pltpu.with_memory_space_constraint(value, pltpu.VMEM)
 
 
 def cost(flops, moved, trans=0):
@@ -57,27 +65,29 @@
 
 
 def teacher_kernel(tea_ref, out_ref):
+    chunk = tea_ref.shape[0]
+    rows = pl.ds(pl.multiple_of(pl.program_id(0) * chunk, chunk), chunk)
     tea = tea_ref[...].astype(f32)
-    out_ref[...] = (tea * inverse_length(tea)).astype(bf16) * half_scale
-
-
-def teacher_emb(tea_img, chunk):
+    out_ref[rows, :] = (tea * inverse_length(tea)).astype(bf16) * half_scale
+
+
+def teacher_emb(tea_img):
     rows, width = tea_img.shape
-    spec = pl.BlockSpec((chunk, width), lambda i: (i, 0))
+    chunk = math.gcd(rows, 512)
     return pl.pallas_call(
         teacher_kernel,
         grid=(rows // chunk,),
-        in_specs=[spec],
-        out_specs=spec,
-        out_shape=jax.ShapeDtypeStruct((rows, width), bf16),
-        compiler_params=params(),
-        cost_estimate=cost(4 * rows * width, 4 * rows * width),
+        in_specs=[pl.BlockSpec((chunk, width), lambda i: (i, 0))],
+        out_specs=resident,
+        out_shape=pltpu.VMEM((rows, width), bf16),
+        compiler_params=params(),
+        cost_estimate=cost(4 * rows * width, 2 * rows * width),
     )(tea_img)
 
 
 def proj_kernel(order_ref, images_ref, near_ref, far_ref, proj_ref, emb_ref, head_ref):
-    columns = near_ref.shape[1]
-    count = near_ref.shape[0]
+    count, columns = near_ref.shape[:2]
+    chunk = images_ref.shape[0]
 
     @pl.when(pl.program_id(0) == 0)
     def _():
@@ -86,44 +96,44 @@
                 start = pl.multiple_of(order_ref[2 * k + place] * columns, columns)
                 head_ref[pl.ds(start, columns), :] = ref[k]
 
+    rows = pl.ds(pl.multiple_of(pl.program_id(0) * chunk, chunk), chunk)
     proj = lax.dot_general(images_ref[...], head_ref[...], NT, preferred_element_type=f32).astype(bf16)
     floats = proj.astype(f32)
-    proj_ref[...] = proj
-    emb_ref[...] = (floats * inverse_length(floats)).astype(bf16) * half_scale
-
-
-def projections(order, images, near, far, chunk):
+    proj_ref[rows, :] = proj
+    emb_ref[rows, :] = (floats * inverse_length(floats)).astype(bf16) * half_scale
+
+
+def projections(order, images, near, far):
     rows, depth = images.shape
     count, columns, _ = near.shape
     width = 2 * count * columns
-    piece = pl.BlockSpec((count, columns, depth), lambda i, order: (0, 0, 0))
-    row = pl.BlockSpec((chunk, width), lambda i, order: (i, 0))
+    chunk = math.gcd(rows, 512)
     return pl.pallas_call(
         proj_kernel,
         grid_spec=pltpu.PrefetchScalarGridSpec(
             num_scalar_prefetch=1,
             grid=(rows // chunk,),
-            in_specs=[pl.BlockSpec((chunk, depth), lambda i, order: (i, 0)), piece, piece],
-            out_specs=[row, row, pl.BlockSpec((width, depth), lambda i, order: (0, 0))],
+            in_specs=[pl.BlockSpec((chunk, depth), lambda i, order: (i, 0)), resident, resident],
+            out_specs=[resident, resident, resident],
         ),
         out_shape=(
-            jax.ShapeDtypeStruct((rows, width), bf16),
-            jax.ShapeDtypeStruct((rows, width), bf16),
+            pltpu.VMEM((rows, width), bf16),
+            pltpu.VMEM((rows, width), bf16),
             jax.ShapeDtypeStruct((width, depth), bf16),
         ),
         compiler_params=params(),
-        cost_estimate=cost(2 * rows * depth * width, 6 * rows * depth),
+        cost_estimate=cost(2 * rows * depth * width, 2 * rows * depth),
     )(order, images, near, far)
 
 
-def pair_tile(tea_ref, emb_ref, texts, grads_ref):
-    tea_width = tea_ref.shape[1]
-    emb = emb_ref[...]
-    target = lax.dot_general(tea_ref[...], texts[:, :tea_width], NT, preferred_element_type=f32)
+def pair_tile(tea, emb, texts, grads_ref):
+    tea_width = tea.shape[1]
+    target = lax.dot_general(tea, texts[:, :tea_width], NT, preferred_element_type=f32)
     student = lax.dot_general(emb, texts[:, tea_width:], NT, preferred_element_type=f32)
     coef = (jnp.tanh(student + half_bias) - jnp.tanh(target + half_bias)).astype(bf16)
+    part = jnp.dot(coef, texts[:, tea_width:], preferred_element_type=f32)
     grads_ref[...] += lax.dot_general(coef, emb, TN, preferred_element_type=f32)
-    return jnp.dot(coef, texts[:, tea_width:], preferred_element_type=f32)
+    return part
 
 
 def early_kernel(count, summed, *refs):
@@ -134,40 +144,36 @@
         before_ref, refs = refs[0], refs[1:]
     out_ref, grads_ref, texts_ref = refs
     half = text_refs[0].shape[0]
-
-    @pl.when(pl.program_id(0) == 0)
-    def _():
-        for k in range(count):
-            texts_ref[pl.ds(k * half, half), :] = text_refs[k][...]
-        grads_ref[...] = jnp.zeros_like(grads_ref)
-
-    grads = pair_tile(tea_ref, emb_ref, texts_ref, grads_ref)
-    out_ref[...] = grads + before_ref[...] if summed else grads
-
-
-def early(tea_emb, emb, texts, before, chunk):
-    rows, tea_width = tea_emb.shape
+    size = tea_ref.shape[0]
+    chunk = math.gcd(size, 512)
+    for k in range(count):
+        texts_ref[pl.ds(k * half, half), :] = text_refs[k][...]
+    grads_ref[...] = jnp.zeros_like(grads_ref)
+    for k in range(size // chunk):
+        rows = pl.ds(k * chunk, chunk)
+        part = pair_tile(tea_ref[rows, :], emb_ref[rows, :], texts_ref, grads_ref)
+        out_ref[rows, :] = part + before_ref[rows, :] if summed else part
+
+
+def early(tea_emb, emb, texts, before):
+    rows = tea_emb.shape[0]
     emb_width = emb.shape[1]
     half, width = texts[0].shape
     count = len(texts)
     size = count * half
-    row = lambda wide: pl.BlockSpec((chunk, wide), lambda i: (i, 0))
-    whole = lambda shape: pl.BlockSpec(shape, lambda i: (0, 0))
-    given = [tea_emb, emb, *texts] + ([] if before is None else [before])
+    given = [pinned(tea_emb), pinned(emb), *texts] + ([] if before is None else [pinned(before)])
     return pl.pallas_call(
         functools.partial(early_kernel, count, before is not None),
-        grid=(rows // chunk,),
-        in_specs=[row(tea_width), row(emb_width)]
-        + [whole((half, width))] * count
-        + ([] if before is None else [row(emb_width)]),
-        out_specs=[row(emb_width), whole((size, emb_width))],
+        in_specs=[resident] * len(given),
+        out_specs=[resident, resident],
         out_shape=(
-            jax.ShapeDtypeStruct((rows, emb_width), f32),
+            pltpu.VMEM((rows, emb_width), f32),
             jax.ShapeDtypeStruct((size, emb_width), f32),
         ),
+        input_output_aliases={} if before is None else {len(given) - 1: 0},
         scratch_shapes=[pltpu.VMEM((size, width), bf16)],
         compiler_params=params(),
-        cost_estimate=cost(2 * rows * size * (width + 2 * emb_width), 2 * rows * (width + 4 * emb_width)),
+        cost_estimate=cost(2 * rows * size * (width + 2 * emb_width), 2 * size * (width + 2 * emb_width)),
     )(*given)
 
 
@@ -177,65 +183,45 @@
     refs = refs[4 + count :]
     if summed:
         texts_before_ref, refs = refs[0], refs[1:]
-    give_ref, keep_refs, grads_ref, texts_ref = refs[0], refs[1 : 1 + masks], refs[-2], refs[-1]
+    give_ref, keep_refs, grads_ref, texts_ref, part_ref = refs[0], refs[1 : 1 + masks], *refs[-3:]
     half = text_refs[0].shape[0]
-    share = tea_ref.shape[0]
-    step = pl.program_id(0)
-
-    @pl.when(step == 0)
-    def _():
-        for k in range(count):
-            texts_ref[pl.ds(k * half, half), :] = text_refs[k][...]
-        grads_ref[...] = texts_before_ref[...] if summed else jnp.zeros_like(grads_ref)
-
-    grads = pair_tile(tea_ref, emb_ref, texts_ref, grads_ref) + before_ref[...]
-    floats = proj_ref[...].astype(f32)
-    inverse = inverse_length(floats)
-    unit = floats * inverse
-    along = jnp.sum(unit * grads, axis=1, keepdims=True)
-    part = ((grads - unit * along) * inverse).astype(bf16)
+    share = keep_refs[0].shape[0]
+    for k in range(count):
+        texts_ref[pl.ds(k * half, half), :] = text_refs[k][...]
+    grads_ref[...] = texts_before_ref[...] if summed else jnp.zeros_like(grads_ref)
     for k in range(masks):
-
-        @pl.when(step == 2 * k)
-        def _(k=k):
-            give_ref[pl.ds(k * share, share), :] = part
-
-        @pl.when(step == 2 * k + 1)
-        def _(k=k):
-            keep_refs[k][...] = part
+        rows = pl.ds(pl.multiple_of(order_ref[k] * (2 * share), 2 * share), 2 * share)
+        grads = pair_tile(tea_ref[rows, :], emb_ref[rows, :], texts_ref, grads_ref) + before_ref[rows, :]
+        floats = proj_ref[rows, :].astype(f32)
+        inverse = inverse_length(floats)
+        unit = floats * inverse
+        along = jnp.sum(unit * grads, axis=1, keepdims=True)
+        part_ref[...] = ((grads - unit * along) * inverse).astype(bf16)
+        side = order_ref[masks]
+        keep_refs[k][...] = part_ref[pl.ds(pl.multiple_of(side * share, share), share), :]
+        give_ref[pl.ds(k * share, share), :] = part_ref[pl.ds(pl.multiple_of((1 - side) * share, share), share), :]
 
 
 def late(order, tea_emb, emb, proj, before, texts, texts_before, share):
-    rows, tea_width = tea_emb.shape
-    emb_width = emb.shape[1]
+    tea_width, emb_width = tea_emb.shape[1], emb.shape[1]
     half, width = texts[0].shape
     count = len(texts)
     size = count * half
-    steps = order.shape[0]
-    masks = steps // 2
-    row = lambda wide: pl.BlockSpec((share, wide), lambda i, order: (order[i], 0))
-    whole = lambda shape: pl.BlockSpec(shape, lambda i, order: (0, 0))
+    masks = order.shape[0] - 1
     summed = texts_before is not None
-    given = [tea_emb, emb, proj, before, *texts] + ([texts_before] if summed else [])
+    given = [pinned(tea_emb), pinned(emb), pinned(proj), pinned(before), *texts]
+    given += [texts_before] if summed else []
     out = pl.pallas_call(
         functools.partial(late_kernel, count, masks, summed),
-        grid_spec=pltpu.PrefetchScalarGridSpec(
-            num_scalar_prefetch=1,
-            grid=(steps,),
-            in_specs=[row(tea_width), row(emb_width), row(emb_width), row(emb_width)]
-            + [whole((half, width))] * count
-            + ([whole((size, emb_width))] if summed else []),
-            out_specs=[whole((masks * share, emb_width))]
-            + [whole((share, emb_width))] * masks
-            + [whole((size, emb_width))],
-            scratch_shapes=[pltpu.VMEM((size, width), bf16)],
-        ),
+        in_specs=[pl.BlockSpec(memory_space=pltpu.SMEM)] + [resident] * len(given),
+        out_specs=[resident] * (masks + 2),
         out_shape=[jax.ShapeDtypeStruct((masks * share, emb_width), bf16)]
         + [jax.ShapeDtypeStruct((share, emb_width), bf16)] * masks
         + [jax.ShapeDtypeStruct((size, emb_width), f32)],
+        scratch_shapes=[pltpu.VMEM((size, width), bf16), pltpu.VMEM((2 * share, emb_width), bf16)],
         compiler_params=params(),
         cost_estimate=cost(
-            2 * steps * share * size * (width + 2 * emb_width), 2 * steps * share * (width + 4 * emb_width)
+            4 * masks * share * size * (width + 2 * emb_width), 4 * masks * share * emb_width
         ),
     )(order, *given)
     return out[0], out[1:-1], out[-1]
@@ -318,7 +304,6 @@
     half = share // 2
     pairs = tensor_count // 2
     bits = dp_count.bit_length() - 1
-    chunk = 2 * share
     factor = 0.5 * logit_scale * loss_scale / (rows * dp_count)
 
     low, high = text_parts(tea_txt, stu_txt)
@@ -335,21 +320,21 @@
     far = swap(near, "tensor", 1)
     order = jnp.stack([rank ^ (2 * k + place) for k in range(pairs) for place in range(2)]).astype(jnp.int32)
 
-    tea_emb = teacher_emb(tea_img, chunk)
-    proj, emb, head_full = projections(order, images, near, far, chunk)
+    tea_emb = teacher_emb(tea_img)
+    proj, emb, head_full = projections(order, images, near, far)
 
     text_grads = {}
-    image_part, text_grads[0] = early(tea_emb, emb, [lows[0], highs[0]], None, chunk)
+    image_part, text_grads[0] = early(tea_emb, emb, [lows[0], highs[0]], None)
     middle = list(range(1, dp_count - 1))
     texts = [part for mask in middle for part in (lows[mask], highs[mask])]
-    image_part, grads = early(tea_emb, emb, texts, image_part, chunk)
+    image_part, grads = early(tea_emb, emb, texts, image_part)
     for k, mask in enumerate(middle):
         text_grads[mask] = grads[k * share : (k + 1) * share]
     last = dp_count - 1
     first_masks = list(range(pairs // 2, pairs))[::-1]
     second_masks = list(range(pairs // 2))[::-1]
     orders = [
-        jnp.stack([rank ^ (2 * k + place) for k in masks for place in (1, 0)]).astype(jnp.int32)
+        jnp.stack([(rank // 2) ^ k for k in masks] + [rank % 2]).astype(jnp.int32)
         for masks in (first_masks, second_masks)
     ]
     texts = [lows[last], highs[last]]

time: 150 us -> 130 us (0.87)
  Pallas kernels: 59.6 us -> 39 us
  starting transfers between devices: 30.1 us -> 33.5 us
    pallas_call x3, Pallas kernels: 22.9 us -> 12.2 us  [the longest x2 9.8 us: late(): pl.pallas_call(functools.partial(late_kernel, count, masks, summed), in_s...]
    pallas_call x2, Pallas kernels: 24.2 us -> 15.9 us  [early(): pl.pallas_call(functools.partial(early_kernel, count, before is not None)...]
    ppermute x25, starting transfers between devices: 30.1 us -> 33.5 us  [swap(): lax.ppermute(value, axis, [(source, source ^ mask) for source in range(co...]
    unnamed x12 -> x10, local copies, waits for them, and re-layouts: 5.73 us -> 4.93 us
  transfers between devices with their start and end apart: 25 -> 25, of which waited for: 8 -> 7; matrix products, arithmetic and copies ran while one was open for 2% -> 3% of each run, Pallas kernels for 29% -> 26%
where the time goes in v2:
time: 130 us
  waiting for transfers between devices  46.7 us (36%)
  Pallas kernels  39 us (30%)
  starting transfers between devices  33.5 us (26%)
  local copies, waits for them, and re-layouts  5.1 us (4%)
  other arithmetic  4.42 us (3%)
    ppermute x25, waiting for transfers between devices, swap(): lax.ppermute(value, axis, [(source, source ^ mask) for source in range(co...  46.7 us
    ppermute x25, starting transfers between devices, swap(): lax.ppermute(value, axis, [(source, source ^ mask) for source in range(co...  33.5 us
    pallas_call x2, Pallas kernels, early(): pl.pallas_call(functools.partial(early_kernel, count, before is not None)...  15.9 us
    pallas_call x2, Pallas kernels, late(): pl.pallas_call(functools.partial(late_kernel, count, masks, summed), in_s...  9.8 us
    pallas_call x1, Pallas kernels, projections(): pl.pallas_call(proj_kernel, grid_spec=pltpu.PrefetchScalarGridSpec(num_sc...  6.26 us
    unnamed x10, local copies, waits for them, and re-layouts  4.93 us
    pallas_call x1, Pallas kernels, head_parts(): pl.pallas_call(functools.partial(head_kernel, count), grid_spec=pltpu.Pre...  2.83 us
  transfers between devices with their start and end apart: 25, of which 7 were waited for; matrix products, arithmetic and copies ran while one was open for 3% of the time, Pallas kernels for 26%

profile of v2, /device:TPU:0, one launch (start us, length us, event | category | flops | bytes accessed | tf_op | source)
XLA Modules:
  0.0 129.6 jit_solution(1057935338726302153)
XLA Ops:
  0.6 3.1 %collective-permute-start = (bf16[96,768]{1,0:T(8,128)(2,1)}, bf16[96,768]{1,0:T(8,128)(2,1)S(1)}, u32[]{:S(2)}, u32[]{:S(2)}) collective-permute-start(bf16[96,768]{1,0:T(8,128)(2,1)} %bitcast.59), channel_id=1, source_target_pairs={{0,2},{1,3},{2,0},{3,1},{4,6},{5,7},{6,4},{7,5},{8,10},{9,11},{10,... | collective-permute-start | bytes 442376 | tf_op jit(solution)/shard_map/ppermute | solution.py:38
  3.7 2.6 %collective-permute-start.1 = (bf16[96,768]{1,0:T(8,128)(2,1)}, bf16[96,768]{1,0:T(8,128)(2,1)S(1)}, u32[]{:S(2)}, u32[]{:S(2)}) collective-permute-start(bf16[96,768]{1,0:T(8,128)(2,1)} %bitcast.60), channel_id=1, source_target_pairs={{0,4},{1,5},{2,6},{3,7},{4,0},{5,1},{6,2},{7,3},{8,12},{9,13},{10,... | collective-permute-start | bytes 442376 | tf_op jit(solution)/shard_map/ppermute | solution.py:38
  6.3 0.0 collective-permute-start.2
  6.3 1.0 copy-done.1
  7.3 1.1 copy-done.4
  8.4 0.4 shard_map.78
  8.8 1.8 %collective-permute-start.4 = (bf16[128,2304]{1,0:T(8,128)(2,1)S(1)}, bf16[128,2304]{1,0:T(8,128)(2,1)S(1)}, u32[]{:S(2)}, u32[]{:S(2)}) collective-permute-start(bf16[128,2304]{1,0:T(8,128)(2,1)S(1)} %get-tuple-element.24.refs_2_), channel_id=1, source_target_pairs={{0,8},{8,0},{16,24},{24,16},{1,9},{9,1},{17,25},{25,17},{2,10},{10... | collective-permute-start | bytes 1769480 | tf_op jit(solution)/shard_map/ppermute | solution.py:38
  10.6 1.5 %collective-permute-start.7 = (bf16[128,2304]{1,0:T(8,128)(2,1)S(1)}, bf16[128,2304]{1,0:T(8,128)(2,1)S(1)}, u32[]{:S(2)}, u32[]{:S(2)}) collective-permute-start(bf16[128,2304]{1,0:T(8,128)(2,1)S(1)} %get-tuple-element.25.refs_3_), channel_id=1, source_target_pairs={{0,16},{8,24},{16,0},{24,8},{1,17},{9,25},{17,1},{25,9},{2,18},{10... | collective-permute-start | bytes 1769480 | tf_op jit(solution)/shard_map/ppermute | solution.py:38
  12.1 5.8 %collective-permute-done.1 = bf16[96,768]{1,0:T(8,128)(2,1)S(1)} collective-permute-done((bf16[96,768]{1,0:T(8,128)(2,1)}, bf16[96,768]{1,0:T(8,128)(2,1)S(1)}, u32[]{:S(2)}, u32[]{:S(2)}) %collective-permute-start.1) | collective-permute-done | bytes 147488 | tf_op jit(solution)/shard_map/ppermute | solution.py:38
  17.9 1.0 pad_maximum_fusion.near_ref
  18.9 0.1 collective-permute-start.3
  19.0 1.6 %collective-permute-start.5 = (bf16[128,2304]{1,0:T(8,128)(2,1)S(1)}, bf16[128,2304]{1,0:T(8,128)(2,1)S(1)}, u32[]{:S(2)}, u32[]{:S(2)}) collective-permute-start(bf16[128,2304]{1,0:T(8,128)(2,1)S(1)} %get-tuple-element.25.refs_3_), channel_id=1, source_target_pairs={{0,8},{8,0},{16,24},{24,16},{1,9},{9,1},{17,25},{25,17},{2,10},{10... | collective-permute-start | bytes 1769480 | tf_op jit(solution)/shard_map/ppermute | solution.py:38
  20.6 1.5 %collective-permute-start.6 = (bf16[128,2304]{1,0:T(8,128)(2,1)S(1)}, bf16[128,2304]{1,0:T(8,128)(2,1)}, u32[]{:S(2)}, u32[]{:S(2)}) collective-permute-start(bf16[128,2304]{1,0:T(8,128)(2,1)S(1)} %get-tuple-element.24.refs_2_), channel_id=1, source_target_pairs={{0,16},{8,24},{16,0},{24,8},{1,17},{9,25},{17,1},{25,9},{2,18},{10... | collective-permute-start | bytes 1769480 | tf_op jit(solution)/shard_map/ppermute | solution.py:38
  22.1 0.1 stack.102.order_ref
  22.2 2.8 %copy-done = bf16[2048,1536]{1,0:T(8,128)(2,1)S(1)} copy-done((bf16[2048,1536]{1,0:T(8,128)(2,1)S(1)}, bf16[2048,1536]{1,0:T(8,128)(2,1)}, u32[]{:S(2)}) %copy-start) | copy-done | bytes 6291480
  24.9 2.4 %shard_map.76.refs_0_ = bf16[2048,1536]{1,0:T(8,128)(2,1)S(1)} custom-call(bf16[2048,1536]{1,0:T(8,128)(2,1)S(1)} %copy-done), custom_call_target="tpu_custom_call" | custom-call | flops 12582912 | bytes 6291456 | tf_op jit(solution)/shard_map/pallas_call | solution.py:77
  27.4 0.1 add_add_fusion
  27.5 0.5 collective-permute-start.8
  28.0 0.0 collective-permute-done.7.refs_5_
  28.0 0.5 collective-permute-start.9
  28.6 6.3 %shard_map.77 = (bf16[2048,768]{1,0:T(8,128)(2,1)S(1)}, bf16[2048,768]{1,0:T(8,128)(2,1)S(1)}, bf16[768,768]{1,0:T(8,128)(2,1)S(1)}) custom-call(s32[8]{0:T(128)S(1)} %stack.102.order_ref, bf16[2048,768]{1,0:T(8,128)(2,1)S(1)} %copy-done.3, bf16[4,96,768]{2,1,0:T(8,128)(2,1)S(1)} %pad_maximum_fusion.near_ref, bf16[4,96,768]{2,1,0:T(8,128)(2,1)} %collective-permute-done.3.far_ref), custom_call_target="tpu_custom_call" | custom-call | flops 2415919104 | bytes 3145728 | tf_op jit(solution)/shard_map/pallas_call | solution.py:111
  34.8 5.7 %shard_map.79 = (f32[2048,768]{1,0:T(8,128)S(1)}, f32[256,768]{1,0:T(8,128)S(1)}) custom-call(bf16[2048,1536]{1,0:T(8,128)(2,1)S(1)} %shard_map.76.refs_0_, bf16[2048,768]{1,0:T(8,128)(2,1)S(1)} %get-tuple-element.22.refs_1_, bf16[128,2304]{1,0:T(8,128)(2,1)S(1)} %get-tuple-element.24.refs_2_, bf16[128,2304]{1,0:T(8,128)(2,1)S(1)} %get-tuple-element.25.refs_3_), custom_call_target="tpu_custom_call" | custom-call | flops 4026531840 | bytes 1966080 | tf_op jit(solution)/shard_map/pallas_call | solution.py:165
  40.5 0.0 collective-permute-done.5.refs_3_
  40.5 10.2 %shard_map.80 = (f32[2048,768]{1,0:T(8,128)S(1)}, f32[512,768]{1,0:T(8,128)S(1)}) custom-call(bf16[2048,1536]{1,0:T(8,128)(2,1)S(1)} %shard_map.76.refs_0_, bf16[2048,768]{1,0:T(8,128)(2,1)S(1)} %get-tuple-element.22.refs_1_, bf16[128,2304]{1,0:T(8,128)(2,1)S(1)} %collective-permute-done.4.refs_2_, ...), custom_call_target="tpu_custom_call", output_to_operand_aliasing={{0}: (6, {})} | custom-call | flops 8053063680 | bytes 3932160 | tf_op jit(solution)/shard_map/pallas_call | solution.py:165
  50.7 0.1 convert.22
  50.8 0.0 collective-permute-done.9.refs_5_
  50.8 5.0 %shard_map.81 = (bf16[512,768]{1,0:T(8,128)(2,1)S(1)}, bf16[256,768]{1,0:T(8,128)(2,1)S(1)}, bf16[256,768]{1,0:T(8,128)(2,1)S(1)}, f32[256,768]{1,0:T(8,128)S(1)}) custom-call(s32[3]{0:T(128)S(1)} %get-tuple-element.57.order_ref, bf16[2048,1536]{1,0:T(8,128)(2,1)S(1)} %shard_map.76.refs_0_, bf16[2048,768]{1,0:T(8,128)(2,1)S(1)} %get-tuple-element.22.refs_1_, ...), custom_call_target="tpu_custom_call" | custom-call | flops 2013265920 | bytes 1572864 | tf_op jit(solution)/shard_map/pallas_call | solution.py:214
  55.8 0.1 collective-permute-start.11
  55.9 4.8 %shard_map.82 = (bf16[512,768]{1,0:T(8,128)(2,1)S(1)}, bf16[256,768]{1,0:T(8,128)(2,1)S(1)}, bf16[256,768]{1,0:T(8,128)(2,1)S(1)}, f32[256,768]{1,0:T(8,128)S(1)}) custom-call(s32[3]{0:T(128)S(1)} %get-tuple-element.56.order_ref, bf16[2048,1536]{1,0:T(8,128)(2,1)S(1)} %shard_map.76.refs_0_, bf16[2048,768]{1,0:T(8,128)(2,1)S(1)} %get-tuple-element.22.refs_1_, ...), custom_call_target="tpu_custom_call" | custom-call | flops 2013265920 | bytes 1572864 | tf_op jit(solution)/shard_map/pallas_call | solution.py:214
  60.7 0.6 collective-permute-start.10
  61.5 1.6 %collective-permute-start.23 = (bf16[2,128,768]{2,1,0:T(8,128)(2,1)S(1)}, bf16[2,128,768]{2,1,0:T(8,128)(2,1)S(1)}, u32[]{:S(2)}, u32[]{:S(2)}) collective-permute-start(bf16[2,128,768]{2,1,0:T(8,128)(2,1)S(1)} %pad_maximum_fusion.2), channel_id=1, source_target_pairs={{0,8},{8,0},{16,24},{24,16},{1,9},{9,1},{17,25},{25,17},{2,10},{10... | collective-permute-start | bytes 1179656 | tf_op jit(solution)/shard_map/ppermute | solution.py:38
  63.1 1.6 %collective-permute-start.21 = (bf16[2,128,768]{2,1,0:T(8,128)(2,1)S(1)}, bf16[2,128,768]{2,1,0:T(8,128)(2,1)S(1)}, u32[]{:S(2)}, u32[]{:S(2)}) collective-permute-start(bf16[2,128,768]{2,1,0:T(8,128)(2,1)S(1)} %pad_maximum_fusion.1), channel_id=1, source_target_pairs={{0,16},{8,24},{16,0},{24,8},{1,17},{9,25},{17,1},{25,9},{2,18},{10... | collective-permute-start | bytes 1179656 | tf_op jit(solution)/shard_map/ppermute | solution.py:38
  64.6 0.0 collective-permute-done.11
  64.6 0.1 slice_add_fusion.1
  64.7 0.0 collective-permute-done.10
  64.8 0.0 copy-start.2
  64.8 0.1 slice_add_fusion
  64.9 2.8 %shard_map.84 = (bf16[384,768]{1,0:T(8,128)(2,1)S(1)}, bf16[384,768]{1,0:T(8,128)(2,1)S(1)}) custom-call(s32[8]{0:T(128)S(1)} %stack.102.order_ref, bf16[2048,768]{1,0:T(8,128)(2,1)S(1)} %copy-done.3, bf16[256,768]{1,0:T(8,128)(2,1)S(1)} %get-tuple-element.48.refs_0_, bf16[256,768]{1,0:T(8,128)(2,1)S(1)} %get-tuple-element.47.refs_1_, ...), custom_call_target="tpu_custom_call" | custom-call | flops 1207959552 | bytes 3145728 | tf_op jit(solution)/shard_map/pallas_call | solution.py:262
  67.7 0.1 collective-permute-start.15
  67.8 0.2 fusion.5
  68.0 4.6 %collective-permute-done.23 = bf16[2,128,768]{2,1,0:T(8,128)(2,1)S(1)} collective-permute-done((bf16[2,128,768]{2,1,0:T(8,128)(2,1)S(1)}, bf16[2,128,768]{2,1,0:T(8,128)(2,1)S(1)}, u32[]{:S(2)}, u32[]{:S(2)}) %collective-permute-start.23) | collective-permute-done | bytes 393248 | tf_op jit(solution)/shard_map/ppermute | solution.py:38
  72.6 1.3 %collective-permute-done.21 = bf16[2,128,768]{2,1,0:T(8,128)(2,1)S(1)} collective-permute-done((bf16[2,128,768]{2,1,0:T(8,128)(2,1)S(1)}, bf16[2,128,768]{2,1,0:T(8,128)(2,1)S(1)}, u32[]{:S(2)}, u32[]{:S(2)}) %collective-permute-start.21) | collective-permute-done | bytes 393248 | tf_op jit(solution)/shard_map/ppermute | solution.py:38
  73.9 0.1 fusion.8
  74.0 0.6 collective-permute-start.22
  74.6 1.5 %collective-permute-start.24 = (bf16[1,128,768]{2,1,0:T(8,128)(2,1)S(1)}, bf16[1,128,768]{2,1,0:T(8,128)(2,1)S(1)}, u32[]{:S(2)}, u32[]{:S(2)}) collective-permute-start(bf16[1,128,768]{2,1,0:T(8,128)(2,1)S(1)} %get-tuple-element.42), channel_id=1, source_target_pairs={{0,16},{8,24},{16,0},{24,8},{1,17},{9,25},{17,1},{25,9},{2,18},{10... | collective-permute-start | bytes 589832 | tf_op jit(solution)/shard_map/ppermute | solution.py:38
  76.1 0.1 add.70
  76.3 2.4 %collective-permute-start.16 = (bf16[96,768]{1,0:T(8,128)(2,1)S(1)}, bf16[96,768]{1,0:T(8,128)(2,1)S(1)}, u32[]{:S(2)}, u32[]{:S(2)}) collective-permute-start(bf16[96,768]{1,0:T(8,128)(2,1)S(1)} %get-tuple-element.51), channel_id=1, source_target_pairs={{0,2},{1,3},{2,0},{3,1},{4,6},{5,7},{6,4},{7,5},{8,10},{9,11},{10,... | collective-permute-start | bytes 442376 | tf_op jit(solution)/shard_map/ppermute | solution.py:38
  78.6 1.1 collective-permute-start.17
  79.7 1.4 %collective-permute-start.18 = (bf16[96,768]{1,0:T(8,128)(2,1)S(1)}, bf16[96,768]{1,0:T(8,128)(2,1)S(1)}, u32[]{:S(2)}, u32[]{:S(2)}) collective-permute-start(bf16[96,768]{1,0:T(8,128)(2,1)S(1)} %get-tuple-element.52), channel_id=1, source_target_pairs={{0,6},{1,7},{2,4},{3,5},{4,2},{5,3},{6,0},{7,1},{8,14},{9,15},{10,... | collective-permute-start | bytes 442376 | tf_op jit(solution)/shard_map/ppermute | solution.py:38
  81.1 0.1 convert_add_fusion.3
  81.2 2.1 %collective-permute-done.16 = bf16[96,768]{1,0:T(8,128)(2,1)S(1)} collective-permute-done((bf16[96,768]{1,0:T(8,128)(2,1)S(1)}, bf16[96,768]{1,0:T(8,128)(2,1)S(1)}, u32[]{:S(2)}, u32[]{:S(2)}) %collective-permute-start.16) | collective-permute-done | bytes 147488 | tf_op jit(solution)/shard_map/ppermute | solution.py:38
  83.3 7.9 %collective-permute-done.17 = bf16[96,768]{1,0:T(8,128)(2,1)S(1)} collective-permute-done((bf16[96,768]{1,0:T(8,128)(2,1)S(1)}, bf16[96,768]{1,0:T(8,128)(2,1)S(1)}, u32[]{:S(2)}, u32[]{:S(2)}) %collective-permute-start.17) | collective-permute-done | bytes 147488 | tf_op jit(solution)/shard_map/ppermute | solution.py:38
  91.2 0.1 fusion.11
  91.3 1.6 %collective-permute-start.19 = (bf16[96,768]{1,0:T(8,128)(2,1)S(1)}, bf16[96,768]{1,0:T(8,128)(2,1)S(1)}, u32[]{:S(2)}, u32[]{:S(2)}) collective-permute-start(bf16[96,768]{1,0:T(8,128)(2,1)S(1)} %fusion.11), channel_id=1, source_target_pairs={{0,8},{8,0},{16,24},{24,16},{1,9},{9,1},{17,25},{25,17},{2,10},{10... | collective-permute-start | bytes 442376 | tf_op jit(solution)/shard_map/ppermute | solution.py:38
  92.9 0.3 fusion.2
  93.2 2.1 %collective-permute-start.12 = (bf16[256,768]{1,0:T(8,128)(2,1)S(1)}, bf16[256,768]{1,0:T(8,128)(2,1)S(1)}, u32[]{:S(2)}, u32[]{:S(2)}) collective-permute-start(bf16[256,768]{1,0:T(8,128)(2,1)S(1)} %get-tuple-element.50.refs_3_), channel_id=1, source_target_pairs={{0,6},{1,7},{2,4},{3,5},{4,2},{5,3},{6,0},{7,1},{8,14},{9,15},{10,... | collective-permute-start | bytes 1179656 | tf_op jit(solution)/shard_map/ppermute | solution.py:38
  95.3 5.8 %collective-permute-start.13 = (bf16[256,768]{1,0:T(8,128)(2,1)S(1)}, bf16[256,768]{1,0:T(8,128)(2,1)S(1)}, u32[]{:S(2)}, u32[]{:S(2)}) collective-permute-start(bf16[256,768]{1,0:T(8,128)(2,1)S(1)} %get-tuple-element.49.refs_2_), channel_id=1, source_target_pairs={{0,4},{1,5},{2,6},{3,7},{4,0},{5,1},{6,2},{7,3},{8,12},{9,13},{10,... | collective-permute-start | bytes 1179656 | tf_op jit(solution)/shard_map/ppermute | solution.py:38
  101.0 0.1 fusion.10
  101.2 0.1 collective-permute-start.20
  101.2 1.1 fusion.4
  102.3 4.6 %collective-permute-done.12.refs_1_ = bf16[256,768]{1,0:T(8,128)(2,1)S(1)} collective-permute-done((bf16[256,768]{1,0:T(8,128)(2,1)S(1)}, bf16[256,768]{1,0:T(8,128)(2,1)S(1)}, u32[]{:S(2)}, u32[]{:S(2)}) %collective-permute-start.12) | collective-permute-done | bytes 393248 | tf_op jit(solution)/shard_map/ppermute | solution.py:38
  106.9 20.4 %collective-permute-done.13.refs_2_ = bf16[256,768]{1,0:T(8,128)(2,1)S(1)} collective-permute-done((bf16[256,768]{1,0:T(8,128)(2,1)S(1)}, bf16[256,768]{1,0:T(8,128)(2,1)S(1)}, u32[]{:S(2)}, u32[]{:S(2)}) %collective-permute-start.13) | collective-permute-done | bytes 393248 | tf_op jit(solution)/shard_map/ppermute | solution.py:38
  127.3 1.5 %shard_map.83 = f32[256,768]{1,0:T(8,128)} custom-call(bf16[256,768]{1,0:T(8,128)(2,1)S(1)} %get-tuple-element.48.refs_0_, bf16[256,768]{1,0:T(8,128)(2,1)S(1)} %collective-permute-done.12.refs_1_, bf16[256,768]{1,0:T(8,128)(2,1)S(1)} %collective-permute-done.13.refs_2_, bf16[256,768]{1,0:T(8,128)(2,1)S(1)} %collective-permute-done.14.refs_3_, ...), custom_call_target="tpu_custom_call" | custom-call | flops 301989888 | bytes 786432 | tf_op jit(solution)/shard_map/pallas_call | solution.py:289
  128.8 0.9 multiply_bitcast_fusion
  (27 shorter events, 0.3 us)
Async XLA Ops:
  0.6 11.5 %collective-permute-start = (bf16[96,768]{1,0:T(8,128)(2,1)}, bf16[96,768]{1,0:T(8,128)(2,1)S(1)}, u32[]{:S(2)}, u32[]{:S(2)}) collective-permute-start(bf16[96,768]{1,0:T(8,128)(2,1)} %bitcast.59), channel_id=1, source_target_pairs={{0,2},{1,3},{2,0},{3,1},{4,6},{5,7},{6,4},{7,5},{8,10},{9,11},{10,... | collective-permute-start | bytes 442376 | tf_op jit(solution)/shard_map/ppermute | solution.py:38
  3.7 14.2 %collective-permute-start.1 = (bf16[96,768]{1,0:T(8,128)(2,1)}, bf16[96,768]{1,0:T(8,128)(2,1)S(1)}, u32[]{:S(2)}, u32[]{:S(2)}) collective-permute-start(bf16[96,768]{1,0:T(8,128)(2,1)} %bitcast.60), channel_id=1, source_target_pairs={{0,4},{1,5},{2,6},{3,7},{4,0},{5,1},{6,2},{7,3},{8,12},{9,13},{10,... | collective-permute-start | bytes 442376 | tf_op jit(solution)/shard_map/ppermute | solution.py:38
  6.3 11.6 %collective-permute-start.2 = (bf16[96,768]{1,0:T(8,128)(2,1)}, bf16[96,768]{1,0:T(8,128)(2,1)S(1)}, u32[]{:S(2)}, u32[]{:S(2)}) collective-permute-start(bf16[96,768]{1,0:T(8,128)(2,1)} %bitcast.61), channel_id=1, source_target_pairs={{0,6},{1,7},{2,4},{3,5},{4,2},{5,3},{6,0},{7,1},{8,14},{9,15},{10,... | collective-permute-start | bytes 442376 | tf_op jit(solution)/shard_map/ppermute | solution.py:38
  6.3 1.0 copy-start.1
  7.3 1.1 copy-start.4
  8.8 18.7 %collective-permute-start.4 = (bf16[128,2304]{1,0:T(8,128)(2,1)S(1)}, bf16[128,2304]{1,0:T(8,128)(2,1)S(1)}, u32[]{:S(2)}, u32[]{:S(2)}) collective-permute-start(bf16[128,2304]{1,0:T(8,128)(2,1)S(1)} %get-tuple-element.24.refs_2_), channel_id=1, source_target_pairs={{0,8},{8,0},{16,24},{24,16},{1,9},{9,1},{17,25},{25,17},{2,10},{10... | collective-permute-start | bytes 1769480 | tf_op jit(solution)/shard_map/ppermute | solution.py:38
  10.6 17.4 %collective-permute-start.7 = (bf16[128,2304]{1,0:T(8,128)(2,1)S(1)}, bf16[128,2304]{1,0:T(8,128)(2,1)S(1)}, u32[]{:S(2)}, u32[]{:S(2)}) collective-permute-start(bf16[128,2304]{1,0:T(8,128)(2,1)S(1)} %get-tuple-element.25.refs_3_), channel_id=1, source_target_pairs={{0,16},{8,24},{16,0},{24,8},{1,17},{9,25},{17,1},{25,9},{2,18},{10... | collective-permute-start | bytes 1769480 | tf_op jit(solution)/shard_map/ppermute | solution.py:38
  18.9 9.6 %collective-permute-start.3 = (bf16[4,96,768]{2,1,0:T(8,128)(2,1)S(1)}, bf16[4,96,768]{2,1,0:T(8,128)(2,1)}, u32[]{:S(2)}, u32[]{:S(2)}) collective-permute-start(bf16[4,96,768]{2,1,0:T(8,128)(2,1)S(1)} %pad_maximum_fusion.near_ref), channel_id=1, source_target_pairs={{0,1},{1,0},{2,3},{3,2},{4,5},{5,4},{6,7},{7,6},{8,9},{9,8},{10,11... | collective-permute-start | bytes 1769480 | tf_op jit(solution)/shard_map/ppermute | solution.py:38
  19.0 21.5 %collective-permute-start.5 = (bf16[128,2304]{1,0:T(8,128)(2,1)S(1)}, bf16[128,2304]{1,0:T(8,128)(2,1)S(1)}, u32[]{:S(2)}, u32[]{:S(2)}) collective-permute-start(bf16[128,2304]{1,0:T(8,128)(2,1)S(1)} %get-tuple-element.25.refs_3_), channel_id=1, source_target_pairs={{0,8},{8,0},{16,24},{24,16},{1,9},{9,1},{17,25},{25,17},{2,10},{10... | collective-permute-start | bytes 1769480 | tf_op jit(solution)/shard_map/ppermute | solution.py:38
  20.6 19.9 %collective-permute-start.6 = (bf16[128,2304]{1,0:T(8,128)(2,1)S(1)}, bf16[128,2304]{1,0:T(8,128)(2,1)}, u32[]{:S(2)}, u32[]{:S(2)}) collective-permute-start(bf16[128,2304]{1,0:T(8,128)(2,1)S(1)} %get-tuple-element.24.refs_2_), channel_id=1, source_target_pairs={{0,16},{8,24},{16,0},{24,8},{1,17},{9,25},{17,1},{25,9},{2,18},{10... | collective-permute-start | bytes 1769480 | tf_op jit(solution)/shard_map/ppermute | solution.py:38
  22.2 2.8 %copy-start = (bf16[2048,1536]{1,0:T(8,128)(2,1)S(1)}, bf16[2048,1536]{1,0:T(8,128)(2,1)}, u32[]{:S(2)}) copy-start(bf16[2048,1536]{1,0:T(8,128)(2,1)} %tea_ref.2) | copy-start | bytes 18874372
  24.9 3.6 %copy-start.3 = (bf16[2048,768]{1,0:T(8,128)(2,1)S(1)}, bf16[2048,768]{1,0:T(8,128)(2,1)}, u32[]{:S(2)}) copy-start(bf16[2048,768]{1,0:T(8,128)(2,1)} %images_ref.3) | copy-start | bytes 9437188
  27.5 23.3 %collective-permute-start.8 = (bf16[128,2304]{1,0:T(8,128)(2,1)S(1)}, bf16[128,2304]{1,0:T(8,128)(2,1)S(1)}, u32[]{:S(2)}, u32[]{:S(2)}) collective-permute-start(bf16[128,2304]{1,0:T(8,128)(2,1)S(1)} %collective-permute-done.4.refs_2_), channel_id=1, source_target_pairs={{0,16},{8,24},{16,0},{24,8},{1,17},{9,25},{17,1},{25,9},{2,18},{10... | collective-permute-start | bytes 1769480 | tf_op jit(solution)/shard_map/ppermute | solution.py:38
  28.0 22.8 %collective-permute-start.9 = (bf16[128,2304]{1,0:T(8,128)(2,1)S(1)}, bf16[128,2304]{1,0:T(8,128)(2,1)S(1)}, u32[]{:S(2)}, u32[]{:S(2)}) collective-permute-start(bf16[128,2304]{1,0:T(8,128)(2,1)S(1)} %collective-permute-done.7.refs_5_), channel_id=1, source_target_pairs={{0,8},{8,0},{16,24},{24,16},{1,9},{9,1},{17,25},{25,17},{2,10},{10... | collective-permute-start | bytes 1769480 | tf_op jit(solution)/shard_map/ppermute | solution.py:38
  55.8 8.8 %collective-permute-start.11 = (bf16[512,768]{1,0:T(8,128)(2,1)S(1)}, bf16[512,768]{1,0:T(8,128)(2,1)S(1)}, u32[]{:S(2)}, u32[]{:S(2)}) collective-permute-start(bf16[512,768]{1,0:T(8,128)(2,1)S(1)} %get-tuple-element.32), channel_id=1, source_target_pairs={{0,1},{1,0},{2,3},{3,2},{4,5},{5,4},{6,7},{7,6},{8,9},{9,8},{10,11... | collective-permute-start | bytes 2359304 | tf_op jit(solution)/shard_map/ppermute | solution.py:38
  60.7 4.0 %collective-permute-start.10 = (bf16[512,768]{1,0:T(8,128)(2,1)S(1)}, bf16[512,768]{1,0:T(8,128)(2,1)S(1)}, u32[]{:S(2)}, u32[]{:S(2)}) collective-permute-start(bf16[512,768]{1,0:T(8,128)(2,1)S(1)} %get-tuple-element.30), channel_id=1, source_target_pairs={{0,1},{1,0},{2,3},{3,2},{4,5},{5,4},{6,7},{7,6},{8,9},{9,8},{10,11... | collective-permute-start | bytes 2359304 | tf_op jit(solution)/shard_map/ppermute | solution.py:38
  61.5 11.1 %collective-permute-start.23 = (bf16[2,128,768]{2,1,0:T(8,128)(2,1)S(1)}, bf16[2,128,768]{2,1,0:T(8,128)(2,1)S(1)}, u32[]{:S(2)}, u32[]{:S(2)}) collective-permute-start(bf16[2,128,768]{2,1,0:T(8,128)(2,1)S(1)} %pad_maximum_fusion.2), channel_id=1, source_target_pairs={{0,8},{8,0},{16,24},{24,16},{1,9},{9,1},{17,25},{25,17},{2,10},{10... | collective-permute-start | bytes 1179656 | tf_op jit(solution)/shard_map/ppermute | solution.py:38
  63.1 10.8 %collective-permute-start.21 = (bf16[2,128,768]{2,1,0:T(8,128)(2,1)S(1)}, bf16[2,128,768]{2,1,0:T(8,128)(2,1)S(1)}, u32[]{:S(2)}, u32[]{:S(2)}) collective-permute-start(bf16[2,128,768]{2,1,0:T(8,128)(2,1)S(1)} %pad_maximum_fusion.1), channel_id=1, source_target_pairs={{0,16},{8,24},{16,0},{24,8},{1,17},{9,25},{17,1},{25,9},{2,18},{10... | collective-permute-start | bytes 1179656 | tf_op jit(solution)/shard_map/ppermute | solution.py:38
  64.8 3.0 %copy-start.2 = (bf16[256,768]{1,0:T(8,128)(2,1)S(1)}, bf16[256,768]{1,0:T(8,128)(2,1)}, u32[]{:S(2)}) copy-start(bf16[256,768]{1,0:T(8,128)(2,1)} %stu_ref.1) | copy-start | bytes 1179652
  67.7 8.4 %collective-permute-start.15 = (bf16[384,768]{1,0:T(8,128)(2,1)S(1)}, bf16[384,768]{1,0:T(8,128)(2,1)S(1)}, u32[]{:S(2)}, u32[]{:S(2)}) collective-permute-start(bf16[384,768]{1,0:T(8,128)(2,1)S(1)} %get-tuple-element.37), channel_id=1, source_target_pairs={{0,1},{1,0},{2,3},{3,2},{4,5},{5,4},{6,7},{7,6},{8,9},{9,8},{10,11... | collective-permute-start | bytes 1769480 | tf_op jit(solution)/shard_map/ppermute | solution.py:38
  74.0 7.2 %collective-permute-start.22 = (bf16[1,128,768]{2,1,0:T(8,128)(2,1)S(1)}, bf16[1,128,768]{2,1,0:T(8,128)(2,1)S(1)}, u32[]{:S(2)}, u32[]{:S(2)}) collective-permute-start(bf16[1,128,768]{2,1,0:T(8,128)(2,1)S(1)} %get-tuple-element.41), channel_id=1, source_target_pairs={{0,8},{8,0},{16,24},{24,16},{1,9},{9,1},{17,25},{25,17},{2,10},{10... | collective-permute-start | bytes 589832 | tf_op jit(solution)/shard_map/ppermute | solution.py:38
  74.6 6.6 %collective-permute-start.24 = (bf16[1,128,768]{2,1,0:T(8,128)(2,1)S(1)}, bf16[1,128,768]{2,1,0:T(8,128)(2,1)S(1)}, u32[]{:S(2)}, u32[]{:S(2)}) collective-permute-start(bf16[1,128,768]{2,1,0:T(8,128)(2,1)S(1)} %get-tuple-element.42), channel_id=1, source_target_pairs={{0,16},{8,24},{16,0},{24,8},{1,17},{9,25},{17,1},{25,9},{2,18},{10... | collective-permute-start | bytes 589832 | tf_op jit(solution)/shard_map/ppermute | solution.py:38
  76.3 7.1 %collective-permute-start.16 = (bf16[96,768]{1,0:T(8,128)(2,1)S(1)}, bf16[96,768]{1,0:T(8,128)(2,1)S(1)}, u32[]{:S(2)}, u32[]{:S(2)}) collective-permute-start(bf16[96,768]{1,0:T(8,128)(2,1)S(1)} %get-tuple-element.51), channel_id=1, source_target_pairs={{0,2},{1,3},{2,0},{3,1},{4,6},{5,7},{6,4},{7,5},{8,10},{9,11},{10,... | collective-permute-start | bytes 442376 | tf_op jit(solution)/shard_map/ppermute | solution.py:38
  78.6 12.6 %collective-permute-start.17 = (bf16[96,768]{1,0:T(8,128)(2,1)S(1)}, bf16[96,768]{1,0:T(8,128)(2,1)S(1)}, u32[]{:S(2)}, u32[]{:S(2)}) collective-permute-start(bf16[96,768]{1,0:T(8,128)(2,1)S(1)} %get-tuple-element.53), channel_id=1, source_target_pairs={{0,4},{1,5},{2,6},{3,7},{4,0},{5,1},{6,2},{7,3},{8,12},{9,13},{10,... | collective-permute-start | bytes 442376 | tf_op jit(solution)/shard_map/ppermute | solution.py:38
  79.7 11.5 %collective-permute-start.18 = (bf16[96,768]{1,0:T(8,128)(2,1)S(1)}, bf16[96,768]{1,0:T(8,128)(2,1)S(1)}, u32[]{:S(2)}, u32[]{:S(2)}) collective-permute-start(bf16[96,768]{1,0:T(8,128)(2,1)S(1)} %get-tuple-element.52), channel_id=1, source_target_pairs={{0,6},{1,7},{2,4},{3,5},{4,2},{5,3},{6,0},{7,1},{8,14},{9,15},{10,... | collective-permute-start | bytes 442376 | tf_op jit(solution)/shard_map/ppermute | solution.py:38
  91.3 9.7 %collective-permute-start.19 = (bf16[96,768]{1,0:T(8,128)(2,1)S(1)}, bf16[96,768]{1,0:T(8,128)(2,1)S(1)}, u32[]{:S(2)}, u32[]{:S(2)}) collective-permute-start(bf16[96,768]{1,0:T(8,128)(2,1)S(1)} %fusion.11), channel_id=1, source_target_pairs={{0,8},{8,0},{16,24},{24,16},{1,9},{9,1},{17,25},{25,17},{2,10},{10... | collective-permute-start | bytes 442376 | tf_op jit(solution)/shard_map/ppermute | solution.py:38
  93.2 13.8 %collective-permute-start.12 = (bf16[256,768]{1,0:T(8,128)(2,1)S(1)}, bf16[256,768]{1,0:T(8,128)(2,1)S(1)}, u32[]{:S(2)}, u32[]{:S(2)}) collective-permute-start(bf16[256,768]{1,0:T(8,128)(2,1)S(1)} %get-tuple-element.50.refs_3_), channel_id=1, source_target_pairs={{0,6},{1,7},{2,4},{3,5},{4,2},{5,3},{6,0},{7,1},{8,14},{9,15},{10,... | collective-permute-start | bytes 1179656 | tf_op jit(solution)/shard_map/ppermute | solution.py:38
  95.3 32.1 %collective-permute-start.13 = (bf16[256,768]{1,0:T(8,128)(2,1)S(1)}, bf16[256,768]{1,0:T(8,128)(2,1)S(1)}, u32[]{:S(2)}, u32[]{:S(2)}) collective-permute-start(bf16[256,768]{1,0:T(8,128)(2,1)S(1)} %get-tuple-element.49.refs_2_), channel_id=1, source_target_pairs={{0,4},{1,5},{2,6},{3,7},{4,0},{5,1},{6,2},{7,3},{8,12},{9,13},{10,... | collective-permute-start | bytes 1179656 | tf_op jit(solution)/shard_map/ppermute | solution.py:38
  101.0 26.3 %collective-permute-start.14 = (bf16[256,768]{1,0:T(8,128)(2,1)S(1)}, bf16[256,768]{1,0:T(8,128)(2,1)S(1)}, u32[]{:S(2)}, u32[]{:S(2)}) collective-permute-start(bf16[256,768]{1,0:T(8,128)(2,1)S(1)} %get-tuple-element.47.refs_1_), channel_id=1, source_target_pairs={{0,2},{1,3},{2,0},{3,1},{4,6},{5,7},{6,4},{7,5},{8,10},{9,11},{10,... | collective-permute-start | bytes 1179656 | tf_op jit(solution)/shard_map/ppermute | solution.py:38
  101.2 27.6 %collective-permute-start.20 = (bf16[96,768]{1,0:T(8,128)(2,1)S(1)}, bf16[96,768]{1,0:T(8,128)(2,1)S(1)}, u32[]{:S(2)}, u32[]{:S(2)}) collective-permute-start(bf16[96,768]{1,0:T(8,128)(2,1)S(1)} %fusion.10), channel_id=1, source_target_pairs={{0,16},{8,24},{16,0},{24,8},{1,17},{9,25},{17,1},{25,9},{2,18},{10... | collective-permute-start | bytes 442376 | tf_op jit(solution)/shard_map/ppermute | solution.py:38

commit v3 on v0

v3 whole, which is shorter than its diff:
```python
import functools
import math
import jax
import jax.numpy as jnp
from jax import lax
from jax.experimental import pallas as pl
from jax.experimental.pallas import tpu as pltpu
from jax.sharding import PartitionSpec as P

logit_scale = 64.0
logit_bias = -2.0
loss_scale = 65536.0
half_scale = 0.5 * logit_scale
half_bias = 0.5 * logit_bias
bf16 = jnp.bfloat16
f32 = jnp.float32
NT = (((1,), (1,)), ((), ()))
TN = (((0,), (0,)), ((), ()))


def params(held=0):
    return pltpu.CompilerParams(vmem_limit_bytes=held + 10 * 1024 * 1024)


resident = pl.BlockSpec(memory_space=pltpu.VMEM)


def pinned(value):
    return pltpu.with_memory_space_constraint(value, pltpu.VMEM)


def cost(flops, moved, trans=0):
    return pl.CostEstimate(flops=int(flops), bytes_accessed=int(moved), transcendentals=int(trans))


def swap(value, axis, mask):
    count = lax.axis_size(axis)
    return lax.ppermute(value, axis, [(source, source ^ mask) for source in range(count)])


def inverse_length(floats):
    return lax.rsqrt(jnp.sum(floats * floats, axis=1, keepdims=True) + 1e-06)


def in_hbm(value):
    return pltpu.with_memory_space_constraint(value, pltpu.HBM)


def stack_kernel(*refs):
    piece_refs, out_ref = refs[:-1], refs[-1]
    for k, ref in enumerate(piece_refs):
        out_ref[k, :, :] = ref[...]


def stacked(pieces):
    shape = (len(pieces), *pieces[0].shape)
    return pl.pallas_call(
        stack_kernel,
        in_specs=[resident] * len(pieces),
        out_specs=resident,
        out_shape=jax.ShapeDtypeStruct(shape, pieces[0].dtype),
        compiler_params=params(),
        cost_estimate=cost(0, 4 * math.prod(shape)),
    )(*pieces)


def sum_kernel(groups, *refs):
    start = 0
    for terms, out_ref in zip(groups, refs[-len(groups) :]):
        total = refs[start][...].astype(f32)
        for ref in refs[start + 1 : start + terms]:
            total += ref[...].astype(f32)
        out_ref[...] = total.astype(bf16)
        start += terms


def sums(groups, gates):
    given = [term for group in groups for term in group]
    size = sum(math.prod(term.shape) for term in given)
    return pl.pallas_call(
        functools.partial(sum_kernel, [len(group) for group in groups]),
        in_specs=[resident] * len(given) + [pl.BlockSpec(memory_space=pl.ANY)] * len(gates),
        out_specs=[resident] * len(groups),
        out_shape=[jax.ShapeDtypeStruct(group[0].shape, bf16) for group in groups],
        compiler_params=params(),
        cost_estimate=cost(0, 0),
    )(*given, *gates)


def fold_kernel(*refs):
    terms, (low_ref, high_ref) = refs[:-2], refs[-2:]
    half = low_ref.shape[0]
    for k, out_ref in enumerate((low_ref, high_ref)):
        total = terms[0][k * half : (k + 1) * half].astype(f32)
        for ref in terms[1:]:
            total += ref[k * half : (k + 1) * half].astype(f32)
        out_ref[...] = total.astype(bf16)


def folded(terms):
    count, *rest = terms[0].shape
    size = len(terms) * math.prod(terms[0].shape)
    return pl.pallas_call(
        fold_kernel,
        in_specs=[resident] * len(terms),
        out_specs=[resident] * 2,
        out_shape=[jax.ShapeDtypeStruct((count // 2, *rest), bf16)] * 2,
        compiler_params=params(),
        cost_estimate=cost(0, 0),
    )(*terms)


def text_kernel(tea_ref, stu_ref, low_ref, high_ref):
    tea_width = tea_ref.shape[1]
    for place, out_ref in enumerate((low_ref, high_ref)):

        @pl.when(pl.program_id(0) == place)
        def _(out_ref=out_ref):
            tea = tea_ref[...].astype(f32)
            out_ref[:, :tea_width] = (tea * inverse_length(tea)).astype(bf16)
            stu = stu_ref[...].astype(f32)
            out_ref[:, tea_width:] = (stu * inverse_length(stu)).astype(bf16)


def text_halves(tea_txt, stu_txt):
    share, tea_width = tea_txt.shape
    stu_width = stu_txt.shape[1]
    half = share // 2
    part = jax.ShapeDtypeStruct((half, tea_width + stu_width), bf16)
    row = lambda width: pl.BlockSpec((half, width), lambda i: (i, 0))
    return pl.pallas_call(
        text_kernel,
        grid=(2,),
        in_specs=[row(tea_width), row(stu_width)],
        out_specs=[resident] * 2,
        out_shape=(part, part),
        compiler_params=params(),
        cost_estimate=cost(4 * share * tea_width, 4 * share * tea_width),
    )(in_hbm(tea_txt), in_hbm(stu_txt))


def teacher_kernel(tea_ref, images_ref, low_ref, high_ref, emb_ref, target_ref, held_ref):
    chunk, width = tea_ref.shape
    rows = pl.ds(pl.multiple_of(pl.program_id(0) * chunk, chunk), chunk)
    tea = tea_ref[...].astype(f32)
    emb = (tea * inverse_length(tea)).astype(bf16) * half_scale
    emb_ref[rows, :] = emb
    half = low_ref.shape[0]
    for place, ref in enumerate((low_ref, high_ref)):
        target = lax.dot_general(emb, ref[:, :width], NT, preferred_element_type=f32)
        target_ref[rows, pl.ds(place * half, half)] = jnp.tanh(target + half_bias)
    held_ref[rows, :] = images_ref[...]


def teacher_emb(tea_img, images, low, high):
    rows, width = tea_img.shape
    depth = images.shape[1]
    chunk = math.gcd(rows, 512)
    size = 2 * low.shape[0]
    row = lambda width: pl.BlockSpec((chunk, width), lambda i: (i, 0))
    return pl.pallas_call(
        teacher_kernel,
        grid=(rows // chunk,),
        in_specs=[row(width), row(depth), resident, resident],
        out_specs=[resident] * 3,
        out_shape=(
            pltpu.VMEM((rows, width), bf16),
            pltpu.VMEM((rows, size), f32),
            pltpu.VMEM((rows, depth), bf16),
        ),
        compiler_params=params(),
        cost_estimate=cost(2 * rows * width * size, 2 * rows * width),
    )(in_hbm(tea_img), in_hbm(images), low, high)


def proj_kernel(order_ref, images_ref, near_ref, far_ref, _tea_ref, _target_ref, proj_ref, emb_ref, head_ref):
    count, columns = near_ref.shape[:2]
    size = images_ref.shape[0]
    chunk = math.gcd(size, 512)
    for k in range(count):
        for place, ref in enumerate((near_ref, far_ref)):
            start = pl.multiple_of(order_ref[2 * k + place] * columns, columns)
            head_ref[pl.ds(start, columns), :] = ref[k]
    for k in range(size // chunk):
        rows = pl.ds(k * chunk, chunk)
        proj = lax.dot_general(images_ref[rows, :], head_ref[...], NT, preferred_element_type=f32).astype(bf16)
        floats = proj.astype(f32)
        proj_ref[rows, :] = proj
        emb_ref[rows, :] = (floats * inverse_length(floats)).astype(bf16) * half_scale


def projections(order, images, near, far, *held):
    rows, depth = images.shape
    count, columns, _ = near.shape
    width = 2 * count * columns
    return pl.pallas_call(
        proj_kernel,
        in_specs=[pl.BlockSpec(memory_space=pltpu.SMEM)] + [resident] * (3 + len(held)),
        out_specs=[resident, resident, resident],
        out_shape=(
            pltpu.VMEM((rows, width), bf16),
            pltpu.VMEM((rows, width), bf16),
            jax.ShapeDtypeStruct((width, depth), bf16),
        ),
        compiler_params=params(),
        cost_estimate=cost(2 * rows * depth * width, 2 * rows * depth),
    )(order, pinned(images), near, far, *map(pinned, held))


def pair_tile(tea, emb, texts, grads_ref, target=None):
    stu = texts[:, -emb.shape[1] :]
    if target is None:
        target = lax.dot_general(tea, texts[:, : tea.shape[1]], NT, preferred_element_type=f32)
        target = jnp.tanh(target + half_bias)
    student = lax.dot_general(emb, stu, NT, preferred_element_type=f32)
    coef = (jnp.tanh(student + half_bias) - target).astype(bf16)
    part = jnp.dot(coef, stu, preferred_element_type=f32)
    grads_ref[...] += lax.dot_general(coef, emb, TN, preferred_element_type=f32)
    return part


def own_kernel(target_ref, emb_ref, low_ref, high_ref, _tea_ref, out_ref, grads_ref, texts_ref):
    width = emb_ref.shape[1]
    half = low_ref.shape[0]
    texts_ref[pl.ds(0, half), :] = low_ref[:, -width:]
    texts_ref[pl.ds(half, half), :] = high_ref[:, -width:]
    size = emb_ref.shape[0]
    chunk = math.gcd(size, 512)
    grads_ref[...] = jnp.zeros_like(grads_ref)
    for k in range(size // chunk):
        rows = pl.ds(k * chunk, chunk)
        out_ref[rows, :] = pair_tile(None, emb_ref[rows, :], texts_ref, grads_ref, target_ref[rows, :])


def own_texts(target, emb, low, high, tea_emb):
    rows, width = emb.shape
    size = target.shape[1]
    return pl.pallas_call(
        own_kernel,
        in_specs=[resident] * 5,
        out_specs=[resident, resident],
        out_shape=(pltpu.VMEM((rows, width), f32), jax.ShapeDtypeStruct((size, width), f32)),
        scratch_shapes=[pltpu.VMEM((size, width), bf16)],
        compiler_params=params(),
        cost_estimate=cost(6 * rows * size * width, 6 * size * width),
    )(pinned(target), pinned(emb), low, high, pinned(tea_emb))


def join(text_refs, out_ref):
    start = 0
    for ref in text_refs:
        out_ref[pl.ds(start, ref.shape[0]), :] = ref[...]
        start += ref.shape[0]


def early_kernel(count, *refs):
    tea_ref, emb_ref = refs[:2]
    text_refs = refs[2 : 2 + count]
    before_ref, out_ref, *sum_refs, grads_ref, texts_ref = refs[2 + count :]
    size = tea_ref.shape[0]
    chunk = math.gcd(size, 512)
    join(text_refs, texts_ref)
    grads_ref[...] = jnp.zeros_like(grads_ref)
    for k in range(size // chunk):
        rows = pl.ds(k * chunk, chunk)
        part = pair_tile(tea_ref[rows, :], emb_ref[rows, :], texts_ref, grads_ref)
        out_ref[rows, :] = part + before_ref[rows, :]
    share = grads_ref.shape[0] // len(sum_refs)
    for k, ref in enumerate(sum_refs):
        ref[...] = grads_ref[pl.ds(k * share, share), :].astype(bf16)


def early(tea_emb, emb, texts, before, share):
    rows = tea_emb.shape[0]
    emb_width = emb.shape[1]
    width = texts[0].shape[1]
    count = len(texts)
    size = sum(part.shape[0] for part in texts)
    given = [pinned(tea_emb), pinned(emb), *texts, pinned(before)]
    return pl.pallas_call(
        functools.partial(early_kernel, count),
        in_specs=[resident] * len(given),
        out_specs=[resident] * (1 + size // share),
        out_shape=[pltpu.VMEM((rows, emb_width), f32)]
        + [jax.ShapeDtypeStruct((share, emb_width), bf16)] * (size // share),
        input_output_aliases={len(given) - 1: 0},
        scratch_shapes=[pltpu.VMEM((size, emb_width), f32), pltpu.VMEM((size, width), bf16)],
        compiler_params=params(4 * size * width + 4 * size * emb_width),
        cost_estimate=cost(2 * rows * size * (width + 2 * emb_width), 2 * size * (width + 2 * emb_width)),
    )(*given)


def late_kernel(count, masks, summed, order_ref, *refs):
    tea_ref, emb_ref, proj_ref, before_ref = refs[:4]
    text_refs = refs[4 : 4 + count]
    refs = refs[4 + count :]
    if summed:
        texts_before_ref, refs = refs[0], refs[1:]
    give_ref, *keep_refs, out_ref, grads_ref, texts_ref = refs
    share = keep_refs[0].shape[0]
    join(text_refs, texts_ref)
    grads_ref[...] = texts_before_ref[...] if summed else jnp.zeros_like(grads_ref)
    for k in range(masks):
        blocks = [pl.ds(pl.multiple_of(order_ref[2 * k + place] * share, share), share) for place in range(2)]
        joined = [jnp.concatenate([ref[rows, :] for rows in blocks]) for ref in (tea_ref, emb_ref)]
        grads = pair_tile(*joined, texts_ref, grads_ref)
        for place, rows in enumerate(blocks):
            whole = grads[place * share : (place + 1) * share] + before_ref[rows, :]
            floats = proj_ref[rows, :].astype(f32)
            inverse = inverse_length(floats)
            unit = floats * inverse
            along = jnp.sum(unit * whole, axis=1, keepdims=True)
            part = ((whole - unit * along) * inverse).astype(bf16)
            if place == 0:
                give_ref[pl.ds(k * share, share), :] = part
            else:
                keep_refs[k][...] = part
    out_ref[...] = grads_ref[...].astype(out_ref.dtype)


def late(order, tea_emb, emb, proj, before, texts, texts_before, share):
    tea_width, emb_width = tea_emb.shape[1], emb.shape[1]
    width = texts[0].shape[1]
    count = len(texts)
    size = sum(part.shape[0] for part in texts)
    masks = order.shape[0] // 2
    summed = texts_before is not None
    given = [pinned(tea_emb), pinned(emb), pinned(proj), pinned(before), *texts]
    given += [texts_before] if summed else []
    return pl.pallas_call(
        functools.partial(late_kernel, count, masks, summed),
        in_specs=[pl.BlockSpec(memory_space=pltpu.SMEM)] + [resident] * len(given),
        out_specs=[resident] * (masks + 2),
        out_shape=[jax.ShapeDtypeStruct((masks * share, emb_width), bf16)]
        + [jax.ShapeDtypeStruct((share, emb_width), bf16)] * masks
        + [jax.ShapeDtypeStruct((size, emb_width), bf16 if summed else f32)],
        scratch_shapes=[pltpu.VMEM((size, emb_width), f32), pltpu.VMEM((size, width), bf16)],
        compiler_params=params(),
        cost_estimate=cost(
            4 * masks * share * size * (width + 2 * emb_width), 4 * masks * share * emb_width
        ),
    )(order, *given)


def merge_kernel(take_ref, *refs):
    for k in range(len(refs) // 2):
        rows = refs[k].shape[0]
        refs[k + len(refs) // 2][...] = refs[k][...] + take_ref[pl.ds(k * rows, rows), :]


def merged(take, keeps):
    size = take.size
    return pl.pallas_call(
        merge_kernel,
        out_shape=[jax.ShapeDtypeStruct(keep.shape, keep.dtype) for keep in keeps],
        compiler_params=params(),
        cost_estimate=cost(0, 0),
    )(take, *keeps)


def head_kernel(order_ref, images_ref, *refs):
    (near_ref, far_ref, total_ref), part_refs = refs[-3:], refs[:-3]
    count, dp_count, rows, _ = near_ref.shape
    columns = dp_count * rows
    share = part_refs[0].shape[0]
    total = None
    for k in range(count):
        places = pl.ds(pl.multiple_of(order_ref[2 * k] * share, share), share)
        term = lax.dot_general(part_refs[k][...], images_ref[places, :], TN, preferred_element_type=f32)
        total = term if total is None else total + term
    total_ref[...] = total
    for k in range(count):
        for place, ref in enumerate((near_ref, far_ref)):
            start = pl.multiple_of(order_ref[2 * k + place] * columns, columns)
            block = total_ref[pl.ds(start, columns), :]
            for j in range(dp_count):
                ref[k, j, :, :] = block[j * rows : (j + 1) * rows].astype(bf16)


def head_parts(order, images, parts, columns, dp_count):
    share, width = parts[0].shape
    depth = images.shape[1]
    count = len(parts)
    piece = jax.ShapeDtypeStruct((count, dp_count, columns // dp_count, depth), bf16)
    return pl.pallas_call(
        head_kernel,
        in_specs=[pl.BlockSpec(memory_space=pltpu.SMEM)] + [resident] * (1 + count),
        out_specs=[resident] * 2,
        out_shape=(piece, piece),
        scratch_shapes=[pltpu.VMEM((width, depth), f32)],
        compiler_params=params(),
        cost_estimate=cost(0, 0),
    )(order, pinned(images), *parts)


def split_kernel(gates, order_ref, near_ref, far_ref, *refs):
    for k, ref in enumerate(refs[gates:]):
        for j in range(near_ref.shape[0]):
            ref[j, :, :] = near_ref[j, order_ref[k]] + far_ref[j, order_ref[k]]


def split(order, near, far, gates):
    count, dp_count, rows, depth = near.shape
    return pl.pallas_call(
        functools.partial(split_kernel, len(gates)),
        in_specs=[pl.BlockSpec(memory_space=pltpu.SMEM)]
        + [resident] * 2
        + [pl.BlockSpec(memory_space=pl.ANY)] * len(gates),
        out_specs=[resident] * dp_count,
        out_shape=[jax.ShapeDtypeStruct((count, rows, depth), bf16)] * dp_count,
        compiler_params=params(),
        cost_estimate=cost(0, 0),
    )(order, near, far, *gates)


def head_result_kernel(scale, order_ref, *refs):
    pieces, (out_ref, total_ref) = refs[:-2], refs[-2:]
    for k, ref in enumerate(pieces):
        total_ref[order_ref[k]] = ref[...].astype(f32)
    rows = total_ref.shape[1]
    total = jnp.concatenate([total_ref[k] for k in range(len(pieces))])
    out_ref[...] = total.T * scale


def head_result(order, pieces, scale):
    rows, depth = pieces[0].shape
    count = len(pieces)
    return pl.pallas_call(
        functools.partial(head_result_kernel, scale),
        in_specs=[pl.BlockSpec(memory_space=pltpu.SMEM)] + [resident] * count,
        out_specs=resident,
        out_shape=jax.ShapeDtypeStruct((depth, count * rows), f32),
        scratch_shapes=[pltpu.VMEM((count, rows, depth), f32)],
        compiler_params=params(),
        cost_estimate=cost(0, 0),
    )(order, *pieces)


def text_result_kernel(scale, stu_ref, own_ref, *refs):
    total = own_ref[...]
    for ref in refs[:-1]:
        total += ref[...].astype(f32)
    stu = stu_ref[...].astype(f32)
    inverse = inverse_length(stu)
    unit = stu * inverse
    along = jnp.sum(unit * total, axis=1, keepdims=True)
    refs[-1][...] = (total - unit * along) * (inverse * scale)


def text_result(stu_txt, own, got, scale):
    rows, width = own.shape
    return pl.pallas_call(
        functools.partial(text_result_kernel, scale),
        out_shape=jax.ShapeDtypeStruct((rows, width), f32),
        compiler_params=params(),
        cost_estimate=cost(0, 0),
    )(stu_txt, own, *got)


def images_kernel(scale, *refs):
    part_refs, head_ref, out_ref, mark_ref = refs[:-3], *refs[-3:]
    total = part_refs[0][...].astype(f32)
    for ref in part_refs[1:]:
        total += ref[...].astype(f32)
    out_ref[...] = scale * jnp.dot(total.astype(bf16), head_ref[...], preferred_element_type=f32)
    mark_ref[...] = jnp.zeros_like(mark_ref)


def image_grads(parts, head, scale):
    share, width = parts[0].shape
    depth = head.shape[1]
    return pl.pallas_call(
        functools.partial(images_kernel, scale),
        out_shape=(jax.ShapeDtypeStruct((share, depth), f32), jax.ShapeDtypeStruct((8, 128), f32)),
        compiler_params=params(),
        cost_estimate=cost(0, 0),
    )(*parts, head)


def per_device(images, head, tea_img, stu_txt, tea_txt):
    dp_count = lax.axis_size("dp")
    tensor_count = lax.axis_size("tensor")
    rank = lax.axis_index("tensor")
    rows = images.shape[0]
    columns = head.shape[1]
    share = rows // tensor_count
    half = share // 2
    pairs = tensor_count // 2
    bits = dp_count.bit_length() - 1
    factor = 0.5 * logit_scale * loss_scale / (rows * dp_count)

    texts = {0: text_halves(tea_txt, stu_txt)}
    for mask in sorted(range(1, dp_count), key=lambda m: (m.bit_count(), m)):
        first, last = mask & -mask, 1 << (mask.bit_length() - 1)
        texts[mask] = [swap(texts[mask ^ last][0], "dp", last), swap(texts[mask ^ first][1], "dp", first)]

    head_t = head.T
    tea_emb, target, held_images = teacher_emb(tea_img, images, *texts[0])
    near = stacked([head_t] + [swap(head_t, "tensor", 2 * k) for k in range(1, pairs)])
    far = swap(near, "tensor", 1)
    order = jnp.stack([rank ^ (2 * k + place) for k in range(pairs) for place in range(2)]).astype(jnp.int32)
    proj, emb, head_full = projections(order, held_images, near, far, tea_emb, target)

    text_grads = {}
    image_part, text_grads[0] = own_texts(target, emb, *texts[0], tea_emb)
    middle = list(range(1, dp_count - 1))
    given = [part for mask in middle for part in texts[mask]]
    image_part, *block_sums = early(tea_emb, emb, given, image_part, share)
    text_grads.update(zip(middle, block_sums))
    last = dp_count - 1
    grads = None
    parts = {}
    for masks in (list(range(pairs // 2, pairs))[::-1], list(range(pairs // 2))[::-1]):
        chosen = jnp.stack([order[2 * k + place] for k in masks for place in (1, 0)])
        give, *keeps, grads = late(chosen, tea_emb, emb, proj, image_part, texts[last], grads, share)
        parts.update(zip(masks, merged(swap(give, "tensor", 1), keeps)))
    text_grads[last] = grads

    near, far = head_parts(order, held_images, [parts[mask] for mask in range(pairs)], columns, dp_count)
    far = swap(far, "tensor", 1)
    dp_order = jnp.stack([lax.axis_index("dp") ^ mask for mask in range(dp_count)]).astype(jnp.int32)
    got = {mask: swap(text_grads[mask], "dp", mask) for mask in range(1, dp_count)}
    pieces = split(dp_order, near, far, [])
    pieces = [pieces[0]] + [swap(pieces[mask], "dp", mask) for mask in range(1, dp_count)]

    for bit in range(pairs.bit_length() - 1):
        sent = [mask for mask in sorted(parts) if mask >> bit & 1 and mask != 1 << bit]
        passed = [swap(parts.pop(mask), "tensor", 2 << bit) for mask in sent]
        targets = [mask ^ 1 << bit for mask in sent]
        if targets:
            parts.update(zip(targets, sums([[parts[mask], block] for mask, block in zip(targets, passed)], [far])))
    arrived = [swap(parts[1 << bit], "tensor", 2 << bit) for bit in range(pairs.bit_length() - 1)]
    grad_images, images_mark = image_grads([parts[0]] + arrived, head_full, factor)

    held, count = pieces, pairs
    while count > 1:
        low, high = folded(held)
        held = [low, swap(high, "tensor", count)]
        count //= 2
    (own,) = sums([held], arrived + [got[mask] for mask in middle])
    own = own[0]
    shares = [own] + [swap(own, "dp", mask) for mask in range(1, dp_count)]
    grad_head = head_result(dp_order, shares, factor)

    grad_text = text_result(stu_txt, text_grads[0], list(got.values()), factor / half_scale)
    return (grad_images, grad_head, grad_text)


def solution(mesh):
    placed = (
        P("dp", None),
        P(None, "tensor"),
        P("dp", None),
        P(("dp", "tensor"), None),
        P(("dp", "tensor"), None),
    )
    return jax.shard_map(
        per_device,
        mesh=mesh,
        in_specs=placed,
        out_specs=(P(("dp", "tensor"), None), P(None, "tensor"), P(("dp", "tensor"), None)),
        check_vma=False,
    )
```

time: 341 us -> 113 us (0.33)
  waiting for transfers between devices: 232 us -> 30.6 us
  matrix products: 46.6 us -> 0 us
  Pallas kernels: 0 us -> 45 us
  other arithmetic: 26.2 us -> 0.23 us
  starting transfers between devices: 10 us -> 33.4 us
  between operations: 14.2 us -> 0.87 us
  local copies, waits for them, and re-layouts: 11.8 us -> 2.66 us
    psum x2 -> x0, waiting for transfers between devices: 113 us -> none  [the longest x1 72.6 us: per_device(): summed = lax.psum(img_grads, 'tensor')]
    ppermute x10 -> x27, waiting for transfers between devices: 105 us -> 30.6 us  [swap(): lax.ppermute(value, axis, [(source, source ^ mask) for source in range(co...]
    dot_general x19 -> x0, matrix products: 46.6 us -> none  [the longest x4 13.6 us: affinity_tile(): lax.dot_general(tea_img_emb, tea_piece, contract, preferred_element_type=...]
    pallas_call x0 -> x19, Pallas kernels: none -> 45 us  [the longest x1 11 us: early(): pl.pallas_call(functools.partial(early_kernel, count), in_specs=[resident...]
    ppermute x10 -> x27, starting transfers between devices: 9.83 us -> 33.4 us  [swap(): lax.ppermute(value, axis, [(source, source ^ mask) for source in range(co...]
    reduce_sum x6 -> x0, other arithmetic: 15.1 us -> none  [the longest x4 8.96 us: normalize(): length = jnp.sqrt(jnp.sum(floats * floats, axis=1, keepdims=True) + 1e-06)]
    all_gather x2 -> x0, waiting for transfers between devices: 13.5 us -> none  [the longest x1 13.5 us: per_device(): head_full = lax.all_gather(head, 'tensor', axis=1, tiled=True)]
    unnamed x57 -> x19, local copies, waits for them, and re-layouts: 11.8 us -> 2.57 us
  transfers between devices with their start and end apart: 14 -> 27, of which waited for: 11 -> 11; matrix products, arithmetic and copies ran while one was open for 18% -> 0% of each run, Pallas kernels for 0% -> 28%
where the time goes in v3:
time: 113 us
  Pallas kernels  45 us (40%)
  starting transfers between devices  33.4 us (30%)
  waiting for transfers between devices  30.6 us (27%)
  local copies, waits for them, and re-layouts  2.66 us (2%)
    ppermute x27, starting transfers between devices, swap(): lax.ppermute(value, axis, [(source, source ^ mask) for source in range(co...  33.4 us
    ppermute x27, waiting for transfers between devices, swap(): lax.ppermute(value, axis, [(source, source ^ mask) for source in range(co...  30.6 us
    pallas_call x1, Pallas kernels, early(): pl.pallas_call(functools.partial(early_kernel, count), in_specs=[resident...  11 us
    pallas_call x2, Pallas kernels, late(): pl.pallas_call(functools.partial(late_kernel, count, masks, summed), in_s...  8.58 us
    pallas_call x1, Pallas kernels, teacher_emb(): pl.pallas_call(teacher_kernel, grid=(rows // chunk,), in_specs=[row(width...  7.31 us
    pallas_call x1, Pallas kernels, projections(): pl.pallas_call(proj_kernel, in_specs=[pl.BlockSpec(memory_space=pltpu.SME...  3.77 us
    pallas_call x1, Pallas kernels, head_parts(): pl.pallas_call(head_kernel, in_specs=[pl.BlockSpec(memory_space=pltpu.SME...  3.38 us
    pallas_call x1, Pallas kernels, own_texts(): pl.pallas_call(own_kernel, in_specs=[resident] * 5, out_specs=[resident,...  3.29 us
  transfers between devices with their start and end apart: 27, of which 11 were waited for; matrix products, arithmetic and copies ran while one was open for 0% of the time, Pallas kernels for 28%

profile of v3, /device:TPU:0, one launch (start us, length us, event | category | flops | bytes accessed | tf_op | source)
XLA Modules:
  0.0 112.8 jit_solution(7293837044591670055)
XLA Ops:
  0.6 3.1 %collective-permute-start = (bf16[96,768]{1,0:T(8,128)(2,1)}, bf16[96,768]{1,0:T(8,128)(2,1)S(1)}, u32[]{:S(2)}, u32[]{:S(2)}) collective-permute-start(bf16[96,768]{1,0:T(8,128)(2,1)} %bitcast.14), channel_id=1, source_target_pairs={{0,2},{1,3},{2,0},{3,1},{4,6},{5,7},{6,4},{7,5},{8,10},{9,11},{10,... | collective-permute-start | bytes 442376 | tf_op jit(solution)/shard_map/ppermute | solution.py:38
  3.7 2.6 %collective-permute-start.1 = (bf16[96,768]{1,0:T(8,128)(2,1)}, bf16[96,768]{1,0:T(8,128)(2,1)S(1)}, u32[]{:S(2)}, u32[]{:S(2)}) collective-permute-start(bf16[96,768]{1,0:T(8,128)(2,1)} %bitcast.15), channel_id=1, source_target_pairs={{0,4},{1,5},{2,6},{3,7},{4,0},{5,1},{6,2},{7,3},{8,12},{9,13},{10,... | collective-permute-start | bytes 442376 | tf_op jit(solution)/shard_map/ppermute | solution.py:38
  6.3 0.0 collective-permute-start.2
  6.3 1.5 %shard_map.76 = (bf16[128,2304]{1,0:T(8,128)(2,1)S(1)}, bf16[128,2304]{1,0:T(8,128)(2,1)S(1)}) custom-call(bf16[256,1536]{1,0:T(8,128)(2,1)} %tea_ref.2, bf16[256,768]{1,0:T(8,128)(2,1)} %stu_ref.3), custom_call_target="tpu_custom_call" | custom-call | flops 1572864 | bytes 1572864 | tf_op jit(solution)/shard_map/pallas_call | solution.py:131
  7.8 1.8 %collective-permute-start.4 = (bf16[128,2304]{1,0:T(8,128)(2,1)S(1)}, bf16[128,2304]{1,0:T(8,128)(2,1)}, u32[]{:S(2)}, u32[]{:S(2)}) collective-permute-start(bf16[128,2304]{1,0:T(8,128)(2,1)S(1)} %get-tuple-element.39.low_ref), channel_id=1, source_target_pairs={{0,8},{8,0},{16,24},{24,16},{1,9},{9,1},{17,25},{25,17},{2,10},{10... | collective-permute-start | bytes 1769480 | tf_op jit(solution)/shard_map/ppermute | solution.py:38
  9.6 1.5 %collective-permute-start.7 = (bf16[128,2304]{1,0:T(8,128)(2,1)S(1)}, bf16[128,2304]{1,0:T(8,128)(2,1)}, u32[]{:S(2)}, u32[]{:S(2)}) collective-permute-start(bf16[128,2304]{1,0:T(8,128)(2,1)S(1)} %get-tuple-element.40.high_ref), channel_id=1, source_target_pairs={{0,16},{8,24},{16,0},{24,8},{1,17},{9,25},{17,1},{25,9},{2,18},{10... | collective-permute-start | bytes 1769480 | tf_op jit(solution)/shard_map/ppermute | solution.py:38
  11.1 6.8 %collective-permute-done.1.refs_2_ = bf16[96,768]{1,0:T(8,128)(2,1)S(1)} collective-permute-done((bf16[96,768]{1,0:T(8,128)(2,1)}, bf16[96,768]{1,0:T(8,128)(2,1)S(1)}, u32[]{:S(2)}, u32[]{:S(2)}) %collective-permute-start.1) | collective-permute-done | bytes 147488 | tf_op jit(solution)/shard_map/ppermute | solution.py:38
  17.9 0.0 collective-permute-done.2.refs_3_
  17.9 0.9 copy-done.4
  18.9 0.1 collective-permute-start.3
  19.0 1.6 %collective-permute-start.5 = (bf16[128,2304]{1,0:T(8,128)(2,1)S(1)}, bf16[128,2304]{1,0:T(8,128)(2,1)}, u32[]{:S(2)}, u32[]{:S(2)}) collective-permute-start(bf16[128,2304]{1,0:T(8,128)(2,1)S(1)} %get-tuple-element.40.high_ref), channel_id=1, source_target_pairs={{0,8},{8,0},{16,24},{24,16},{1,9},{9,1},{17,25},{25,17},{2,10},{10... | collective-permute-start | bytes 1769480 | tf_op jit(solution)/shard_map/ppermute | solution.py:38
  20.5 1.5 %collective-permute-start.6 = (bf16[128,2304]{1,0:T(8,128)(2,1)S(1)}, bf16[128,2304]{1,0:T(8,128)(2,1)}, u32[]{:S(2)}, u32[]{:S(2)}) collective-permute-start(bf16[128,2304]{1,0:T(8,128)(2,1)S(1)} %get-tuple-element.39.low_ref), channel_id=1, source_target_pairs={{0,16},{8,24},{16,0},{24,8},{1,17},{9,25},{17,1},{25,9},{2,18},{10... | collective-permute-start | bytes 1769480 | tf_op jit(solution)/shard_map/ppermute | solution.py:38
  22.0 0.1 stack.57.order_ref
  22.1 0.1 pad_add_fusion.order_ref
  22.2 0.1 pad_add_fusion.1.order_ref
  22.3 7.3 %shard_map.77 = (bf16[2048,1536]{1,0:T(8,128)(2,1)S(1)}, f32[2048,256]{1,0:T(8,128)S(1)}, bf16[2048,768]{1,0:T(8,128)(2,1)S(1)}) custom-call(bf16[2048,1536]{1,0:T(8,128)(2,1)} %tea_ref.3, bf16[2048,768]{1,0:T(8,128)(2,1)} %images_ref.1, bf16[128,2304]{1,0:T(8,128)(2,1)S(1)} %get-tuple-element.39.low_ref, bf16[128,2304]{1,0:T(8,128)(2,1)S(1)} %get-tuple-element.40.high_ref), custom_call_target="tpu_custom_call" | custom-call | flops 1610612736 | bytes 6291456 | tf_op jit(solution)/shard_map/pallas_call | solution.py:161
  29.6 0.6 collective-permute-start.8
  30.2 0.5 collective-permute-start.9
  30.7 3.8 %shard_map.79 = (bf16[2048,768]{1,0:T(8,128)(2,1)S(1)}, bf16[2048,768]{1,0:T(8,128)(2,1)S(1)}, bf16[768,768]{1,0:T(8,128)(2,1)S(1)}) custom-call(s32[8]{0:T(128)S(1)} %stack.57.order_ref, bf16[2048,768]{1,0:T(8,128)(2,1)S(1)} %get-tuple-element.42.images_ref, bf16[4,96,768]{2,1,0:T(8,128)(2,1)S(1)} %shard_map.78.near_ref, ...), custom_call_target="tpu_custom_call" | custom-call | flops 2415919104 | bytes 3145728 | tf_op jit(solution)/shard_map/pallas_call | solution.py:196
  34.5 3.3 %shard_map.80 = (f32[2048,768]{1,0:T(8,128)S(1)}, f32[256,768]{1,0:T(8,128)S(1)}) custom-call(f32[2048,256]{1,0:T(8,128)S(1)} %get-tuple-element.43._target_ref.target_ref, bf16[2048,768]{1,0:T(8,128)(2,1)S(1)} %get-tuple-element.44.emb_ref.refs_1_, bf16[128,2304]{1,0:T(8,128)(2,1)S(1)} %get-tuple-element.39.low_ref, ...), custom_call_target="tpu_custom_call" | custom-call | flops 2415919104 | bytes 1179648 | tf_op jit(solution)/shard_map/pallas_call | solution.py:238
  37.8 0.0 copy-start.1
  37.8 0.0 collective-permute-done.5.refs_3_
  37.8 11.0 %shard_map.81 = (f32[2048,768]{1,0:T(8,128)S(1)}, bf16[256,768]{1,0:T(8,128)(2,1)S(1)}, bf16[256,768]{1,0:T(8,128)(2,1)S(1)}) custom-call(bf16[2048,1536]{1,0:T(8,128)(2,1)S(1)} %get-tuple-element.41._tea_ref.refs_0_, bf16[2048,768]{1,0:T(8,128)(2,1)S(1)} %get-tuple-element.44.emb_ref.refs_1_, ...), custom_call_target="tpu_custom_call", output_to_operand_aliasing={{0}: (6, {})} | custom-call | flops 8053063680 | bytes 3932160 | tf_op jit(solution)/shard_map/pallas_call | solution.py:280
  48.9 0.0 collective-permute-done.8.refs_4_
  48.9 4.3 %shard_map.82 = (bf16[512,768]{1,0:T(8,128)(2,1)S(1)}, bf16[256,768]{1,0:T(8,128)(2,1)S(1)}, bf16[256,768]{1,0:T(8,128)(2,1)S(1)}, f32[256,768]{1,0:T(8,128)S(1)}) custom-call(s32[4]{0:T(128)S(1)} %pad_add_fusion.1.order_ref, bf16[2048,1536]{1,0:T(8,128)(2,1)S(1)} %get-tuple-element.41._tea_ref.refs_0_, ...), custom_call_target="tpu_custom_call" | custom-call | flops 2013265920 | bytes 1572864 | tf_op jit(solution)/shard_map/pallas_call | solution.py:330
  53.3 4.2 %shard_map.83 = (bf16[512,768]{1,0:T(8,128)(2,1)S(1)}, bf16[256,768]{1,0:T(8,128)(2,1)S(1)}, bf16[256,768]{1,0:T(8,128)(2,1)S(1)}, bf16[256,768]{1,0:T(8,128)(2,1)S(1)}) custom-call(s32[4]{0:T(128)S(1)} %pad_add_fusion.order_ref, bf16[2048,1536]{1,0:T(8,128)(2,1)S(1)} %get-tuple-element.41._tea_ref.refs_0_, ...), custom_call_target="tpu_custom_call" | custom-call | flops 2013265920 | bytes 1572864 | tf_op jit(solution)/shard_map/pallas_call | solution.py:330
  57.5 0.8 copy-done.5
  58.3 0.5 collective-permute-start.12
  58.8 1.8 %collective-permute-done.10.take_ref = bf16[512,768]{1,0:T(8,128)(2,1)S(1)} collective-permute-done((bf16[512,768]{1,0:T(8,128)(2,1)S(1)}, bf16[512,768]{1,0:T(8,128)(2,1)S(1)}, u32[]{:S(2)}, u32[]{:S(2)}) %collective-permute-start.10) | collective-permute-done | bytes 786464 | tf_op jit(solution)/shard_map/ppermute | solution.py:38
  60.6 0.1 shard_map.84
  60.7 1.0 collective-permute-done.12.take_ref
  61.7 0.8 shard_map.85
  62.5 3.4 %shard_map.86 = (bf16[4,4,24,768]{3,2,1,0:T(8,128)(2,1)S(1)}, bf16[4,4,24,768]{3,2,1,0:T(8,128)(2,1)}) custom-call(s32[8]{0:T(128)S(1)} %stack.57.order_ref, bf16[2048,768]{1,0:T(8,128)(2,1)S(1)} %get-tuple-element.42.images_ref, bf16[256,768]{1,0:T(8,128)(2,1)S(1)} %get-tuple-element.52.refs_0_, bf16[256,768]{1,0:T(8,128)(2,1)S(1)} %get-tuple-element.53.refs_1_, ...), custom_call_target="tpu_custom_call" | custom-call | tf_op jit(solution)/shard_map/pallas_call | solution.py:385
  65.9 0.1 collective-permute-start.14
  66.0 2.3 %collective-permute-start.13 = (bf16[256,768]{1,0:T(8,128)(2,1)}, bf16[256,768]{1,0:T(8,128)(2,1)}, u32[]{:S(2)}, u32[]{:S(2)}) collective-permute-start(bf16[256,768]{1,0:T(8,128)(2,1)} %get-tuple-element.58.refs_3_), channel_id=1, source_target_pairs={{0,2},{1,3},{2,0},{3,1},{4,6},{5,7},{6,4},{7,5},{8,10},{9,11},{10,... | collective-permute-start | bytes 1179656 | tf_op jit(solution)/shard_map/ppermute | solution.py:38
  68.4 0.1 pad_add_fusion.2.order_ref
  68.5 0.6 shard_map.89
  69.1 1.6 %collective-permute-start.16 = (bf16[4,24,768]{2,1,0:T(8,128)(2,1)S(1)}, bf16[4,24,768]{2,1,0:T(8,128)(2,1)S(1)}, u32[]{:S(2)}, u32[]{:S(2)}) collective-permute-start(bf16[4,24,768]{2,1,0:T(8,128)(2,1)S(1)} %get-tuple-element.64), channel_id=1, source_target_pairs={{0,8},{8,0},{16,24},{24,16},{1,9},{9,1},{17,25},{25,17},{2,10},{10... | collective-permute-start | bytes 442376 | tf_op jit(solution)/shard_map/ppermute | solution.py:38
  70.7 1.5 %collective-permute-start.17 = (bf16[4,24,768]{2,1,0:T(8,128)(2,1)S(1)}, bf16[4,24,768]{2,1,0:T(8,128)(2,1)S(1)}, u32[]{:S(2)}, u32[]{:S(2)}) collective-permute-start(bf16[4,24,768]{2,1,0:T(8,128)(2,1)S(1)} %get-tuple-element.65), channel_id=1, source_target_pairs={{0,16},{8,24},{16,0},{24,8},{1,17},{9,25},{17,1},{25,9},{2,18},{10... | collective-permute-start | bytes 442376 | tf_op jit(solution)/shard_map/ppermute | solution.py:38
  72.2 0.5 collective-permute-start.18
  72.6 1.5 %collective-permute-start.21 = (bf16[256,768]{1,0:T(8,128)(2,1)}, bf16[256,768]{1,0:T(8,128)(2,1)S(1)}, u32[]{:S(2)}, u32[]{:S(2)}) collective-permute-start(bf16[256,768]{1,0:T(8,128)(2,1)} %copy-done.8), channel_id=1, source_target_pairs={{0,8},{8,0},{16,24},{24,16},{1,9},{9,1},{17,25},{25,17},{2,10},{10... | collective-permute-start | bytes 1179656 | tf_op jit(solution)/shard_map/ppermute | solution.py:38
  74.1 1.5 %collective-permute-done.16.refs_1_ = bf16[4,24,768]{2,1,0:T(8,128)(2,1)S(1)} collective-permute-done((bf16[4,24,768]{2,1,0:T(8,128)(2,1)S(1)}, bf16[4,24,768]{2,1,0:T(8,128)(2,1)S(1)}, u32[]{:S(2)}, u32[]{:S(2)}) %collective-permute-start.16) | collective-permute-done | bytes 147488 | tf_op jit(solution)/shard_map/ppermute | solution.py:38
  75.7 3.2 %collective-permute-done.17.refs_2_ = bf16[4,24,768]{2,1,0:T(8,128)(2,1)S(1)} collective-permute-done((bf16[4,24,768]{2,1,0:T(8,128)(2,1)S(1)}, bf16[4,24,768]{2,1,0:T(8,128)(2,1)S(1)}, u32[]{:S(2)}, u32[]{:S(2)}) %collective-permute-start.17) | collective-permute-done | bytes 147488 | tf_op jit(solution)/shard_map/ppermute | solution.py:38
  78.8 1.1 collective-permute-done.18.refs_3_
  79.9 0.1 shard_map.90
  80.0 3.0 %collective-permute-start.19 = (bf16[2,24,768]{2,1,0:T(8,128)(2,1)S(1)}, bf16[2,24,768]{2,1,0:T(8,128)(2,1)S(1)}, u32[]{:S(2)}, u32[]{:S(2)}) collective-permute-start(bf16[2,24,768]{2,1,0:T(8,128)(2,1)S(1)} %get-tuple-element.68), channel_id=1, source_target_pairs={{0,4},{1,5},{2,6},{3,7},{4,0},{5,1},{6,2},{7,3},{8,12},{9,13},{10,... | collective-permute-start | bytes 221192 | tf_op jit(solution)/shard_map/ppermute | solution.py:38
  83.0 1.0 collective-permute-start.22
  84.0 0.3 collective-permute-start.11
  84.4 1.1 shard_map.87
  85.5 1.7 %collective-permute-start.15 = (bf16[256,768]{1,0:T(8,128)(2,1)S(1)}, bf16[256,768]{1,0:T(8,128)(2,1)S(1)}, u32[]{:S(2)}, u32[]{:S(2)}) collective-permute-start(bf16[256,768]{1,0:T(8,128)(2,1)S(1)} %shard_map.87), channel_id=1, source_target_pairs={{0,4},{1,5},{2,6},{3,7},{4,0},{5,1},{6,2},{7,3},{8,12},{9,13},{10,... | collective-permute-start | bytes 1179656 | tf_op jit(solution)/shard_map/ppermute | solution.py:38
  87.2 2.0 %collective-permute-start.26 = (bf16[256,768]{1,0:T(8,128)(2,1)S(1)}, bf16[256,768]{1,0:T(8,128)(2,1)S(1)}, u32[]{:S(2)}, u32[]{:S(2)}) collective-permute-start(bf16[256,768]{1,0:T(8,128)(2,1)S(1)} %copy-done.6), channel_id=1, source_target_pairs={{0,24},{8,16},{16,8},{24,0},{1,25},{9,17},{17,9},{25,1},{2,26},{10... | collective-permute-start | bytes 1179656 | tf_op jit(solution)/shard_map/ppermute | solution.py:38
  89.2 0.5 collective-permute-start.20
  89.7 11.4 %collective-permute-done.22.refs_5_.refs_1_ = bf16[256,768]{1,0:T(8,128)(2,1)S(1)} collective-permute-done((bf16[256,768]{1,0:T(8,128)(2,1)}, bf16[256,768]{1,0:T(8,128)(2,1)S(1)}, u32[]{:S(2)}, u32[]{:S(2)}) %collective-permute-start.22) | collective-permute-done | bytes 393248 | tf_op jit(solution)/shard_map/ppermute | solution.py:38
  101.1 0.1 collective-permute-done.11.refs_1_.refs_2_
  101.2 0.4 collective-permute-done.20.refs_1_
  101.6 2.4 %collective-permute-done.15.refs_2_.refs_3_ = bf16[256,768]{1,0:T(8,128)(2,1)S(1)} collective-permute-done((bf16[256,768]{1,0:T(8,128)(2,1)S(1)}, bf16[256,768]{1,0:T(8,128)(2,1)S(1)}, u32[]{:S(2)}, u32[]{:S(2)}) %collective-permute-start.15) | collective-permute-done | bytes 393248 | tf_op jit(solution)/shard_map/ppermute | solution.py:38
  104.0 1.4 %collective-permute-start.23 = (bf16[24,768]{1,0:T(8,128)(2,1)S(1)}, bf16[24,768]{1,0:T(8,128)(2,1)S(1)}, u32[]{:S(2)}, u32[]{:S(2)}) collective-permute-start(bf16[24,768]{1,0:T(8,128)(2,1)S(1)} %bitcast.18), channel_id=1, source_target_pairs={{0,8},{8,0},{16,24},{24,16},{1,9},{9,1},{17,25},{25,17},{2,10},{10... | collective-permute-start | bytes 110600 | tf_op jit(solution)/shard_map/ppermute | solution.py:38
  105.4 1.0 collective-permute-start.24
  106.4 1.2 %collective-permute-start.25 = (bf16[24,768]{1,0:T(8,128)(2,1)S(1)}, bf16[24,768]{1,0:T(8,128)(2,1)S(1)}, u32[]{:S(2)}, u32[]{:S(2)}) collective-permute-start(bf16[24,768]{1,0:T(8,128)(2,1)S(1)} %bitcast.20), channel_id=1, source_target_pairs={{0,24},{8,16},{16,8},{24,0},{1,25},{9,17},{17,9},{25,1},{2,26},{10... | collective-permute-start | bytes 110600 | tf_op jit(solution)/shard_map/ppermute | solution.py:38
  107.6 1.3 %shard_map.94 = f32[256,768]{1,0:T(8,128)} custom-call(bf16[256,768]{1,0:T(8,128)(2,1)S(1)} %copy-done, f32[256,768]{1,0:T(8,128)S(1)} %copy-done.2, bf16[256,768]{1,0:T(8,128)(2,1)S(1)} %collective-permute-done.21.refs_4_.refs_0_, bf16[256,768]{1,0:T(8,128)(2,1)S(1)} %collective-permute-done.22.refs_5_.refs_1_, ...), custom_call_target="tpu_custom_call" | custom-call | tf_op jit(solution)/shard_map/pallas_call | solution.py:452
  108.9 1.4 %shard_map.88 = (f32[256,768]{1,0:T(8,128)}, f32[8,128]{1,0:T(8,128)}) custom-call(bf16[256,768]{1,0:T(8,128)(2,1)S(1)} %get-tuple-element.52.refs_0_, bf16[256,768]{1,0:T(8,128)(2,1)S(1)} %collective-permute-done.11.refs_1_.refs_2_, bf16[256,768]{1,0:T(8,128)(2,1)S(1)} %collective-permute-done.15.refs_2_.refs_3_, bf16[768,768]{1,0:T(8,128)(2,1)S(1)} %get-tuple-element.60.refs_3_), custom_call_target="tpu_custom_call" | custom-call | tf_op jit(solution)/shard_map/pallas_call | solution.py:472
  110.3 0.9 collective-permute-done.25.refs_3_
  111.2 0.7 shard_map.93
  112.0 0.9 copy.9
  (32 shorter events, 0.1 us)
Async XLA Ops:
  0.6 10.5 %collective-permute-start = (bf16[96,768]{1,0:T(8,128)(2,1)}, bf16[96,768]{1,0:T(8,128)(2,1)S(1)}, u32[]{:S(2)}, u32[]{:S(2)}) collective-permute-start(bf16[96,768]{1,0:T(8,128)(2,1)} %bitcast.14), channel_id=1, source_target_pairs={{0,2},{1,3},{2,0},{3,1},{4,6},{5,7},{6,4},{7,5},{8,10},{9,11},{10,... | collective-permute-start | bytes 442376 | tf_op jit(solution)/shard_map/ppermute | solution.py:38
  3.7 14.2 %collective-permute-start.1 = (bf16[96,768]{1,0:T(8,128)(2,1)}, bf16[96,768]{1,0:T(8,128)(2,1)S(1)}, u32[]{:S(2)}, u32[]{:S(2)}) collective-permute-start(bf16[96,768]{1,0:T(8,128)(2,1)} %bitcast.15), channel_id=1, source_target_pairs={{0,4},{1,5},{2,6},{3,7},{4,0},{5,1},{6,2},{7,3},{8,12},{9,13},{10,... | collective-permute-start | bytes 442376 | tf_op jit(solution)/shard_map/ppermute | solution.py:38
  6.3 11.6 %collective-permute-start.2 = (bf16[96,768]{1,0:T(8,128)(2,1)}, bf16[96,768]{1,0:T(8,128)(2,1)S(1)}, u32[]{:S(2)}, u32[]{:S(2)}) collective-permute-start(bf16[96,768]{1,0:T(8,128)(2,1)} %bitcast.16), channel_id=1, source_target_pairs={{0,6},{1,7},{2,4},{3,5},{4,2},{5,3},{6,0},{7,1},{8,14},{9,15},{10,... | collective-permute-start | bytes 442376 | tf_op jit(solution)/shard_map/ppermute | solution.py:38
  7.8 21.8 %collective-permute-start.4 = (bf16[128,2304]{1,0:T(8,128)(2,1)S(1)}, bf16[128,2304]{1,0:T(8,128)(2,1)}, u32[]{:S(2)}, u32[]{:S(2)}) collective-permute-start(bf16[128,2304]{1,0:T(8,128)(2,1)S(1)} %get-tuple-element.39.low_ref), channel_id=1, source_target_pairs={{0,8},{8,0},{16,24},{24,16},{1,9},{9,1},{17,25},{25,17},{2,10},{10... | collective-permute-start | bytes 1769480 | tf_op jit(solution)/shard_map/ppermute | solution.py:38
  9.6 20.6 %collective-permute-start.7 = (bf16[128,2304]{1,0:T(8,128)(2,1)S(1)}, bf16[128,2304]{1,0:T(8,128)(2,1)}, u32[]{:S(2)}, u32[]{:S(2)}) collective-permute-start(bf16[128,2304]{1,0:T(8,128)(2,1)S(1)} %get-tuple-element.40.high_ref), channel_id=1, source_target_pairs={{0,16},{8,24},{16,0},{24,8},{1,17},{9,25},{17,1},{25,9},{2,18},{10... | collective-permute-start | bytes 1769480 | tf_op jit(solution)/shard_map/ppermute | solution.py:38
  17.9 0.9 copy-start.4
  18.9 11.8 %collective-permute-start.3 = (bf16[4,96,768]{2,1,0:T(8,128)(2,1)S(1)}, bf16[4,96,768]{2,1,0:T(8,128)(2,1)S(1)}, u32[]{:S(2)}, u32[]{:S(2)}) collective-permute-start(bf16[4,96,768]{2,1,0:T(8,128)(2,1)S(1)} %shard_map.78.near_ref), channel_id=1, source_target_pairs={{0,1},{1,0},{2,3},{3,2},{4,5},{5,4},{6,7},{7,6},{8,9},{9,8},{10,11... | collective-permute-start | bytes 1769480 | tf_op jit(solution)/shard_map/ppermute | solution.py:38
  19.0 18.9 %collective-permute-start.5 = (bf16[128,2304]{1,0:T(8,128)(2,1)S(1)}, bf16[128,2304]{1,0:T(8,128)(2,1)}, u32[]{:S(2)}, u32[]{:S(2)}) collective-permute-start(bf16[128,2304]{1,0:T(8,128)(2,1)S(1)} %get-tuple-element.40.high_ref), channel_id=1, source_target_pairs={{0,8},{8,0},{16,24},{24,16},{1,9},{9,1},{17,25},{25,17},{2,10},{10... | collective-permute-start | bytes 1769480 | tf_op jit(solution)/shard_map/ppermute | solution.py:38
  20.5 17.3 %collective-permute-start.6 = (bf16[128,2304]{1,0:T(8,128)(2,1)S(1)}, bf16[128,2304]{1,0:T(8,128)(2,1)}, u32[]{:S(2)}, u32[]{:S(2)}) collective-permute-start(bf16[128,2304]{1,0:T(8,128)(2,1)S(1)} %get-tuple-element.39.low_ref), channel_id=1, source_target_pairs={{0,16},{8,24},{16,0},{24,8},{1,17},{9,25},{17,1},{25,9},{2,18},{10... | collective-permute-start | bytes 1769480 | tf_op jit(solution)/shard_map/ppermute | solution.py:38
  29.6 19.3 %collective-permute-start.8 = (bf16[128,2304]{1,0:T(8,128)(2,1)}, bf16[128,2304]{1,0:T(8,128)(2,1)S(1)}, u32[]{:S(2)}, u32[]{:S(2)}) collective-permute-start(bf16[128,2304]{1,0:T(8,128)(2,1)} %collective-permute-done.4.refs_2_), channel_id=1, source_target_pairs={{0,16},{8,24},{16,0},{24,8},{1,17},{9,25},{17,1},{25,9},{2,18},{10... | collective-permute-start | bytes 1769480 | tf_op jit(solution)/shard_map/ppermute | solution.py:38
  30.2 18.7 %collective-permute-start.9 = (bf16[128,2304]{1,0:T(8,128)(2,1)}, bf16[128,2304]{1,0:T(8,128)(2,1)S(1)}, u32[]{:S(2)}, u32[]{:S(2)}) collective-permute-start(bf16[128,2304]{1,0:T(8,128)(2,1)} %collective-permute-done.7.refs_5_), channel_id=1, source_target_pairs={{0,8},{8,0},{16,24},{24,16},{1,9},{9,1},{17,25},{25,17},{2,10},{10... | collective-permute-start | bytes 1769480 | tf_op jit(solution)/shard_map/ppermute | solution.py:38
  37.8 11.1 %copy-start.1 = (f32[256,768]{1,0:T(8,128)}, f32[256,768]{1,0:T(8,128)S(1)}, u32[]{:S(2)}) copy-start(f32[256,768]{1,0:T(8,128)S(1)} %get-tuple-element.73.own_ref) | copy-start | bytes 2359300
  48.9 4.4 %copy-start.7 = (bf16[256,768]{1,0:T(8,128)(2,1)}, bf16[256,768]{1,0:T(8,128)(2,1)S(1)}, u32[]{:S(2)}) copy-start(bf16[256,768]{1,0:T(8,128)(2,1)S(1)} %get-tuple-element.72) | copy-start | bytes 1179652
  48.9 4.4 %copy-start.8 = (bf16[256,768]{1,0:T(8,128)(2,1)}, bf16[256,768]{1,0:T(8,128)(2,1)S(1)}, u32[]{:S(2)}) copy-start(bf16[256,768]{1,0:T(8,128)(2,1)S(1)} %get-tuple-element.71) | copy-start | bytes 1179652
  57.5 0.8 copy-start.5
  58.3 2.3 %collective-permute-start.10 = (bf16[512,768]{1,0:T(8,128)(2,1)S(1)}, bf16[512,768]{1,0:T(8,128)(2,1)S(1)}, u32[]{:S(2)}, u32[]{:S(2)}) collective-permute-start(bf16[512,768]{1,0:T(8,128)(2,1)S(1)} %get-tuple-element.49), channel_id=1, source_target_pairs={{0,1},{1,0},{2,3},{3,2},{4,5},{5,4},{6,7},{7,6},{8,9},{9,8},{10,11... | collective-permute-start | bytes 2359304 | tf_op jit(solution)/shard_map/ppermute | solution.py:38
  58.3 3.4 %collective-permute-start.12 = (bf16[512,768]{1,0:T(8,128)(2,1)S(1)}, bf16[512,768]{1,0:T(8,128)(2,1)S(1)}, u32[]{:S(2)}, u32[]{:S(2)}) collective-permute-start(bf16[512,768]{1,0:T(8,128)(2,1)S(1)} %get-tuple-element.54), channel_id=1, source_target_pairs={{0,1},{1,0},{2,3},{3,2},{4,5},{5,4},{6,7},{7,6},{8,9},{9,8},{10,11... | collective-permute-start | bytes 2359304 | tf_op jit(solution)/shard_map/ppermute | solution.py:38
  60.7 5.3 %copy-start.3 = (bf16[256,768]{1,0:T(8,128)(2,1)}, bf16[256,768]{1,0:T(8,128)(2,1)S(1)}, u32[]{:S(2)}) copy-start(bf16[256,768]{1,0:T(8,128)(2,1)S(1)} %get-tuple-element.53.refs_1_) | copy-start | bytes 1179652
  65.9 41.7 %copy-start = (bf16[256,768]{1,0:T(8,128)(2,1)S(1)}, bf16[256,768]{1,0:T(8,128)(2,1)}, u32[]{:S(2)}) copy-start(bf16[256,768]{1,0:T(8,128)(2,1)} %stu_ref.3) | copy-start | bytes 1179652
  65.9 2.5 %collective-permute-start.14 = (bf16[4,4,24,768]{3,2,1,0:T(8,128)(2,1)}, bf16[4,4,24,768]{3,2,1,0:T(8,128)(2,1)S(1)}, u32[]{:S(2)}, u32[]{:S(2)}) collective-permute-start(bf16[4,4,24,768]{3,2,1,0:T(8,128)(2,1)} %get-tuple-element.59), channel_id=1, source_target_pairs={{0,1},{1,0},{2,3},{3,2},{4,5},{5,4},{6,7},{7,6},{8,9},{9,8},{10,11... | collective-permute-start | bytes 1769480 | tf_op jit(solution)/shard_map/ppermute | solution.py:38
  66.0 18.3 %collective-permute-start.13 = (bf16[256,768]{1,0:T(8,128)(2,1)}, bf16[256,768]{1,0:T(8,128)(2,1)}, u32[]{:S(2)}, u32[]{:S(2)}) collective-permute-start(bf16[256,768]{1,0:T(8,128)(2,1)} %get-tuple-element.58.refs_3_), channel_id=1, source_target_pairs={{0,2},{1,3},{2,0},{3,1},{4,6},{5,7},{6,4},{7,5},{8,10},{9,11},{10,... | collective-permute-start | bytes 1179656 | tf_op jit(solution)/shard_map/ppermute | solution.py:38
  68.4 18.8 %copy-start.6 = (bf16[256,768]{1,0:T(8,128)(2,1)S(1)}, bf16[256,768]{1,0:T(8,128)(2,1)}, u32[]{:S(2)}) copy-start(bf16[256,768]{1,0:T(8,128)(2,1)} %copy-done.5) | copy-start | bytes 1179652
  68.4 39.2 %copy-start.2 = (f32[256,768]{1,0:T(8,128)S(1)}, f32[256,768]{1,0:T(8,128)}, u32[]{:S(2)}) copy-start(f32[256,768]{1,0:T(8,128)} %copy-done.1) | copy-start | bytes 2359300
  69.1 6.6 %collective-permute-start.16 = (bf16[4,24,768]{2,1,0:T(8,128)(2,1)S(1)}, bf16[4,24,768]{2,1,0:T(8,128)(2,1)S(1)}, u32[]{:S(2)}, u32[]{:S(2)}) collective-permute-start(bf16[4,24,768]{2,1,0:T(8,128)(2,1)S(1)} %get-tuple-element.64), channel_id=1, source_target_pairs={{0,8},{8,0},{16,24},{24,16},{1,9},{9,1},{17,25},{25,17},{2,10},{10... | collective-permute-start | bytes 442376 | tf_op jit(solution)/shard_map/ppermute | solution.py:38
  70.7 8.2 %collective-permute-start.17 = (bf16[4,24,768]{2,1,0:T(8,128)(2,1)S(1)}, bf16[4,24,768]{2,1,0:T(8,128)(2,1)S(1)}, u32[]{:S(2)}, u32[]{:S(2)}) collective-permute-start(bf16[4,24,768]{2,1,0:T(8,128)(2,1)S(1)} %get-tuple-element.65), channel_id=1, source_target_pairs={{0,16},{8,24},{16,0},{24,8},{1,17},{9,25},{17,1},{25,9},{2,18},{10... | collective-permute-start | bytes 442376 | tf_op jit(solution)/shard_map/ppermute | solution.py:38
  72.2 7.7 %collective-permute-start.18 = (bf16[4,24,768]{2,1,0:T(8,128)(2,1)S(1)}, bf16[4,24,768]{2,1,0:T(8,128)(2,1)S(1)}, u32[]{:S(2)}, u32[]{:S(2)}) collective-permute-start(bf16[4,24,768]{2,1,0:T(8,128)(2,1)S(1)} %get-tuple-element.66), channel_id=1, source_target_pairs={{0,24},{8,16},{16,8},{24,0},{1,25},{9,17},{17,9},{25,1},{2,26},{10... | collective-permute-start | bytes 442376 | tf_op jit(solution)/shard_map/ppermute | solution.py:38
  72.6 16.5 %collective-permute-start.21 = (bf16[256,768]{1,0:T(8,128)(2,1)}, bf16[256,768]{1,0:T(8,128)(2,1)S(1)}, u32[]{:S(2)}, u32[]{:S(2)}) collective-permute-start(bf16[256,768]{1,0:T(8,128)(2,1)} %copy-done.8), channel_id=1, source_target_pairs={{0,8},{8,0},{16,24},{24,16},{1,9},{9,1},{17,25},{25,17},{2,10},{10... | collective-permute-start | bytes 1179656 | tf_op jit(solution)/shard_map/ppermute | solution.py:38
  80.0 7.2 %collective-permute-start.19 = (bf16[2,24,768]{2,1,0:T(8,128)(2,1)S(1)}, bf16[2,24,768]{2,1,0:T(8,128)(2,1)S(1)}, u32[]{:S(2)}, u32[]{:S(2)}) collective-permute-start(bf16[2,24,768]{2,1,0:T(8,128)(2,1)S(1)} %get-tuple-element.68), channel_id=1, source_target_pairs={{0,4},{1,5},{2,6},{3,7},{4,0},{5,1},{6,2},{7,3},{8,12},{9,13},{10,... | collective-permute-start | bytes 221192 | tf_op jit(solution)/shard_map/ppermute | solution.py:38
  83.0 18.1 %collective-permute-start.22 = (bf16[256,768]{1,0:T(8,128)(2,1)}, bf16[256,768]{1,0:T(8,128)(2,1)S(1)}, u32[]{:S(2)}, u32[]{:S(2)}) collective-permute-start(bf16[256,768]{1,0:T(8,128)(2,1)} %copy-done.7), channel_id=1, source_target_pairs={{0,16},{8,24},{16,0},{24,8},{1,17},{9,25},{17,1},{25,9},{2,18},{10... | collective-permute-start | bytes 1179656 | tf_op jit(solution)/shard_map/ppermute | solution.py:38
  84.0 17.2 %collective-permute-start.11 = (bf16[256,768]{1,0:T(8,128)(2,1)}, bf16[256,768]{1,0:T(8,128)(2,1)S(1)}, u32[]{:S(2)}, u32[]{:S(2)}) collective-permute-start(bf16[256,768]{1,0:T(8,128)(2,1)} %copy-done.3), channel_id=1, source_target_pairs={{0,2},{1,3},{2,0},{3,1},{4,6},{5,7},{6,4},{7,5},{8,10},{9,11},{10,... | collective-permute-start | bytes 1179656 | tf_op jit(solution)/shard_map/ppermute | solution.py:38
  85.5 18.5 %collective-permute-start.15 = (bf16[256,768]{1,0:T(8,128)(2,1)S(1)}, bf16[256,768]{1,0:T(8,128)(2,1)S(1)}, u32[]{:S(2)}, u32[]{:S(2)}) collective-permute-start(bf16[256,768]{1,0:T(8,128)(2,1)S(1)} %shard_map.87), channel_id=1, source_target_pairs={{0,4},{1,5},{2,6},{3,7},{4,0},{5,1},{6,2},{7,3},{8,12},{9,13},{10,... | collective-permute-start | bytes 1179656 | tf_op jit(solution)/shard_map/ppermute | solution.py:38
  87.2 20.4 %collective-permute-start.26 = (bf16[256,768]{1,0:T(8,128)(2,1)S(1)}, bf16[256,768]{1,0:T(8,128)(2,1)S(1)}, u32[]{:S(2)}, u32[]{:S(2)}) collective-permute-start(bf16[256,768]{1,0:T(8,128)(2,1)S(1)} %copy-done.6), channel_id=1, source_target_pairs={{0,24},{8,16},{16,8},{24,0},{1,25},{9,17},{17,9},{25,1},{2,26},{10... | collective-permute-start | bytes 1179656 | tf_op jit(solution)/shard_map/ppermute | solution.py:38
  89.2 12.4 %collective-permute-start.20 = (bf16[1,24,768]{2,1,0:T(8,128)(2,1)S(1)}, bf16[1,24,768]{2,1,0:T(8,128)(2,1)S(1)}, u32[]{:S(2)}, u32[]{:S(2)}) collective-permute-start(bf16[1,24,768]{2,1,0:T(8,128)(2,1)S(1)} %get-tuple-element.70), channel_id=1, source_target_pairs={{0,2},{1,3},{2,0},{3,1},{4,6},{5,7},{6,4},{7,5},{8,10},{9,11},{10,... | collective-permute-start | bytes 110600 | tf_op jit(solution)/shard_map/ppermute | solution.py:38
  104.0 6.3 %collective-permute-start.23 = (bf16[24,768]{1,0:T(8,128)(2,1)S(1)}, bf16[24,768]{1,0:T(8,128)(2,1)S(1)}, u32[]{:S(2)}, u32[]{:S(2)}) collective-permute-start(bf16[24,768]{1,0:T(8,128)(2,1)S(1)} %bitcast.18), channel_id=1, source_target_pairs={{0,8},{8,0},{16,24},{24,16},{1,9},{9,1},{17,25},{25,17},{2,10},{10... | collective-permute-start | bytes 110600 | tf_op jit(solution)/shard_map/ppermute | solution.py:38
  105.4 4.9 %collective-permute-start.24 = (bf16[24,768]{1,0:T(8,128)(2,1)S(1)}, bf16[24,768]{1,0:T(8,128)(2,1)S(1)}, u32[]{:S(2)}, u32[]{:S(2)}) collective-permute-start(bf16[24,768]{1,0:T(8,128)(2,1)S(1)} %bitcast.19), channel_id=1, source_target_pairs={{0,16},{8,24},{16,0},{24,8},{1,17},{9,25},{17,1},{25,9},{2,18},{10... | collective-permute-start | bytes 110600 | tf_op jit(solution)/shard_map/ppermute | solution.py:38
  106.4 4.9 %collective-permute-start.25 = (bf16[24,768]{1,0:T(8,128)(2,1)S(1)}, bf16[24,768]{1,0:T(8,128)(2,1)S(1)}, u32[]{:S(2)}, u32[]{:S(2)}) collective-permute-start(bf16[24,768]{1,0:T(8,128)(2,1)S(1)} %bitcast.20), channel_id=1, source_target_pairs={{0,24},{8,16},{16,8},{24,0},{1,25},{9,17},{17,9},{25,1},{2,26},{10... | collective-permute-start | bytes 110600 | tf_op jit(solution)/shard_map/ppermute | solution.py:38

commit v4 on v3

--- a/solution.py
+++ b/solution.py
@@ -333,7 +333,7 @@
         out_specs=[resident] * (masks + 2),
         out_shape=[jax.ShapeDtypeStruct((masks * share, emb_width), bf16)]
         + [jax.ShapeDtypeStruct((share, emb_width), bf16)] * masks
-        + [jax.ShapeDtypeStruct((size, emb_width), bf16 if summed else f32)],
+        + [jax.ShapeDtypeStruct((size, emb_width), bf16)],
         scratch_shapes=[pltpu.VMEM((size, emb_width), f32), pltpu.VMEM((size, width), bf16)],
         compiler_params=params(),
         cost_estimate=cost(
@@ -342,31 +342,18 @@
     )(order, *given)
 
 
-def merge_kernel(take_ref, *refs):
-    for k in range(len(refs) // 2):
-        rows = refs[k].shape[0]
-        refs[k + len(refs) // 2][...] = refs[k][...] + take_ref[pl.ds(k * rows, rows), :]
-
-
-def merged(take, keeps):
-    size = take.size
-    return pl.pallas_call(
-        merge_kernel,
-        out_shape=[jax.ShapeDtypeStruct(keep.shape, keep.dtype) for keep in keeps],
-        compiler_params=params(),
-        cost_estimate=cost(0, 0),
-    )(take, *keeps)
-
-
-def head_kernel(order_ref, images_ref, *refs):
-    (near_ref, far_ref, total_ref), part_refs = refs[-3:], refs[:-3]
-    count, dp_count, rows, _ = near_ref.shape
+def head_kernel(order_ref, images_ref, take_ref, *refs):
+    count = (len(refs) - 3) // 2
+    keep_refs, (near_ref, far_ref), part_refs, total_ref = refs[:count], refs[count : count + 2], refs[count + 2 : -1], refs[-1]
+    _, dp_count, rows, _ = near_ref.shape
     columns = dp_count * rows
-    share = part_refs[0].shape[0]
+    share = keep_refs[0].shape[0]
     total = None
     for k in range(count):
         places = pl.ds(pl.multiple_of(order_ref[2 * k] * share, share), share)
-        term = lax.dot_general(part_refs[k][...], images_ref[places, :], TN, preferred_element_type=f32)
+        part = keep_refs[k][...] + take_ref[pl.ds((count - 1 - k) * share, share), :]
+        part_refs[k][...] = part
+        term = lax.dot_general(part, images_ref[places, :], TN, preferred_element_type=f32)
         total = term if total is None else total + term
     total_ref[...] = total
     for k in range(count):
@@ -377,20 +364,20 @@
                 ref[k, j, :, :] = block[j * rows : (j + 1) * rows].astype(bf16)
 
 
-def head_parts(order, images, parts, columns, dp_count):
-    share, width = parts[0].shape
+def head_parts(order, images, take, keeps, columns, dp_count):
+    share, width = keeps[0].shape
     depth = images.shape[1]
-    count = len(parts)
+    count = len(keeps)
     piece = jax.ShapeDtypeStruct((count, dp_count, columns // dp_count, depth), bf16)
     return pl.pallas_call(
         head_kernel,
-        in_specs=[pl.BlockSpec(memory_space=pltpu.SMEM)] + [resident] * (1 + count),
-        out_specs=[resident] * 2,
-        out_shape=(piece, piece),
+        in_specs=[pl.BlockSpec(memory_space=pltpu.SMEM)] + [resident] * (2 + count),
+        out_specs=[resident] * (2 + count),
+        out_shape=[piece] * 2 + [jax.ShapeDtypeStruct((share, width), bf16)] * count,
         scratch_shapes=[pltpu.VMEM((width, depth), f32)],
         compiler_params=params(),
-        cost_estimate=cost(0, 0),
-    )(order, pinned(images), *parts)
+        cost_estimate=cost(2 * count * share * width * depth, 4 * count * share * width),
+    )(order, pinned(images), take, *keeps)
 
 
 def split_kernel(gates, order_ref, near_ref, far_ref, *refs):
@@ -508,18 +495,16 @@
     image_part, *block_sums = early(tea_emb, emb, given, image_part, share)
     text_grads.update(zip(middle, block_sums))
     last = dp_count - 1
-    grads = None
-    parts = {}
-    for masks in (list(range(pairs // 2, pairs))[::-1], list(range(pairs // 2))[::-1]):
-        chosen = jnp.stack([order[2 * k + place] for k in masks for place in (1, 0)])
-        give, *keeps, grads = late(chosen, tea_emb, emb, proj, image_part, texts[last], grads, share)
-        parts.update(zip(masks, merged(swap(give, "tensor", 1), keeps)))
+    chosen = jnp.stack([order[2 * k + place] for k in range(pairs)[::-1] for place in (1, 0)])
+    give, *keeps, grads = late(chosen, tea_emb, emb, proj, image_part, texts[last], None, share)
+    keeps = dict(zip(range(pairs)[::-1], keeps))
+    take = swap(give, "tensor", 1)
     text_grads[last] = grads
 
-    near, far = head_parts(order, held_images, [parts[mask] for mask in range(pairs)], columns, dp_count)
+    near, far, *parts = head_parts(order, held_images, take, [keeps[mask] for mask in range(pairs)], columns, dp_count)
+    parts = dict(enumerate(parts))
     far = swap(far, "tensor", 1)
     dp_order = jnp.stack([lax.axis_index("dp") ^ mask for mask in range(dp_count)]).astype(jnp.int32)
-    got = {mask: swap(text_grads[mask], "dp", mask) for mask in range(1, dp_count)}
     pieces = split(dp_order, near, far, [])
     pieces = [pieces[0]] + [swap(pieces[mask], "dp", mask) for mask in range(1, dp_count)]
 
@@ -529,6 +514,8 @@
         targets = [mask ^ 1 << bit for mask in sent]
         if targets:
             parts.update(zip(targets, sums([[parts[mask], block] for mask, block in zip(targets, passed)], [far])))
+    leaving = sums([[text_grads[mask]] for mask in range(1, dp_count)], [parts[pairs // 2]])
+    got = {mask: swap(block, "dp", mask) for mask, block in zip(range(1, dp_count), leaving)}
     arrived = [swap(parts[1 << bit], "tensor", 2 << bit) for bit in range(pairs.bit_length() - 1)]
     grad_images, images_mark = image_grads([parts[0]] + arrived, head_full, factor)
 
@@ -537,7 +524,7 @@
         low, high = folded(held)
         held = [low, swap(high, "tensor", count)]
         count //= 2
-    (own,) = sums([held], arrived + [got[mask] for mask in middle])
+    (own,) = sums([held], arrived)
     own = own[0]
     shares = [own] + [swap(own, "dp", mask) for mask in range(1, dp_count)]
     grad_head = head_result(dp_order, shares, factor)

time: 113 us -> 111 us (0.982)
  waiting for transfers between devices: 30.6 us -> 26.4 us
  Pallas kernels: 45 us -> 41.9 us
  local copies, waits for them, and re-layouts: 2.66 us -> 5.58 us
  starting transfers between devices: 33.4 us -> 36 us
    ppermute x27 -> x26, waiting for transfers between devices: 30.6 us -> 26.4 us  [swap(): lax.ppermute(value, axis, [(source, source ^ mask) for source in range(co...]
    unnamed x19 -> x23, local copies, waits for them, and re-layouts: 2.57 us -> 5.41 us
    ppermute x27 -> x26, starting transfers between devices: 33.4 us -> 36 us  [swap(): lax.ppermute(value, axis, [(source, source ^ mask) for source in range(co...]
    pallas_call x2 -> x1, Pallas kernels: 8.58 us -> 7 us  [late(): pl.pallas_call(functools.partial(late_kernel, count, masks, summed), in_s...]
  transfers between devices with their start and end apart: 27 -> 26, of which waited for: 11 -> 9; matrix products, arithmetic and copies ran while one was open for 0% -> 0% of each run, Pallas kernels for 28% -> 28%
where the time goes in v4:
time: 111 us
  Pallas kernels  41.9 us (38%)
  starting transfers between devices  36 us (32%)
  waiting for transfers between devices  26.4 us (24%)
  local copies, waits for them, and re-layouts  5.58 us (5%)
    ppermute x26, starting transfers between devices, swap(): lax.ppermute(value, axis, [(source, source ^ mask) for source in range(co...  36 us
    ppermute x26, waiting for transfers between devices, swap(): lax.ppermute(value, axis, [(source, source ^ mask) for source in range(co...  26.4 us
    pallas_call x1, Pallas kernels, early(): pl.pallas_call(functools.partial(early_kernel, count), in_specs=[resident...  10.6 us
    pallas_call x1, Pallas kernels, teacher_emb(): pl.pallas_call(teacher_kernel, grid=(rows // chunk,), in_specs=[row(width...  7.32 us
    pallas_call x1, Pallas kernels, late(): pl.pallas_call(functools.partial(late_kernel, count, masks, summed), in_s...  7 us
    unnamed x23, local copies, waits for them, and re-layouts  5.41 us
    pallas_call x1, Pallas kernels, projections(): pl.pallas_call(proj_kernel, in_specs=[pl.BlockSpec(memory_space=pltpu.SME...  3.76 us
    pallas_call x1, Pallas kernels, own_texts(): pl.pallas_call(own_kernel, in_specs=[resident] * 5, out_specs=[resident,...  3.27 us
  transfers between devices with their start and end apart: 26, of which 9 were waited for; matrix products, arithmetic and copies ran while one was open for 0% of the time, Pallas kernels for 28%

profile of v4, /device:TPU:0, one launch (start us, length us, event | category | flops | bytes accessed | tf_op | source)
XLA Modules:
  0.0 110.8 jit_solution(13937128956895064999)
XLA Ops:
  0.6 3.1 %collective-permute-start = (bf16[96,768]{1,0:T(8,128)(2,1)}, bf16[96,768]{1,0:T(8,128)(2,1)S(1)}, u32[]{:S(2)}, u32[]{:S(2)}) collective-permute-start(bf16[96,768]{1,0:T(8,128)(2,1)} %bitcast.18), channel_id=1, source_target_pairs={{0,2},{1,3},{2,0},{3,1},{4,6},{5,7},{6,4},{7,5},{8,10},{9,11},{10,... | collective-permute-start | bytes 442376 | tf_op jit(solution)/shard_map/ppermute | solution.py:38
  3.7 2.6 %collective-permute-start.1 = (bf16[96,768]{1,0:T(8,128)(2,1)}, bf16[96,768]{1,0:T(8,128)(2,1)S(1)}, u32[]{:S(2)}, u32[]{:S(2)}) collective-permute-start(bf16[96,768]{1,0:T(8,128)(2,1)} %bitcast.19), channel_id=1, source_target_pairs={{0,4},{1,5},{2,6},{3,7},{4,0},{5,1},{6,2},{7,3},{8,12},{9,13},{10,... | collective-permute-start | bytes 442376 | tf_op jit(solution)/shard_map/ppermute | solution.py:38
  6.3 1.5 %shard_map.76 = (bf16[128,2304]{1,0:T(8,128)(2,1)S(1)}, bf16[128,2304]{1,0:T(8,128)(2,1)S(1)}) custom-call(bf16[256,1536]{1,0:T(8,128)(2,1)} %tea_ref.2, bf16[256,768]{1,0:T(8,128)(2,1)} %stu_ref.3), custom_call_target="tpu_custom_call" | custom-call | flops 1572864 | bytes 1572864 | tf_op jit(solution)/shard_map/pallas_call | solution.py:131
  7.8 1.8 %collective-permute-start.4 = (bf16[128,2304]{1,0:T(8,128)(2,1)S(1)}, bf16[128,2304]{1,0:T(8,128)(2,1)}, u32[]{:S(2)}, u32[]{:S(2)}) collective-permute-start(bf16[128,2304]{1,0:T(8,128)(2,1)S(1)} %get-tuple-element.40.low_ref), channel_id=1, source_target_pairs={{0,8},{8,0},{16,24},{24,16},{1,9},{9,1},{17,25},{25,17},{2,10},{10... | collective-permute-start | bytes 1769480 | tf_op jit(solution)/shard_map/ppermute | solution.py:38
  9.6 1.5 %collective-permute-start.7 = (bf16[128,2304]{1,0:T(8,128)(2,1)S(1)}, bf16[128,2304]{1,0:T(8,128)(2,1)}, u32[]{:S(2)}, u32[]{:S(2)}) collective-permute-start(bf16[128,2304]{1,0:T(8,128)(2,1)S(1)} %get-tuple-element.41.high_ref), channel_id=1, source_target_pairs={{0,16},{8,24},{16,0},{24,8},{1,17},{9,25},{17,1},{25,9},{2,18},{10... | collective-permute-start | bytes 1769480 | tf_op jit(solution)/shard_map/ppermute | solution.py:38
  11.1 0.0 collective-permute-done.refs_1_
  11.1 6.8 %collective-permute-done.1.refs_2_ = bf16[96,768]{1,0:T(8,128)(2,1)S(1)} collective-permute-done((bf16[96,768]{1,0:T(8,128)(2,1)}, bf16[96,768]{1,0:T(8,128)(2,1)S(1)}, u32[]{:S(2)}, u32[]{:S(2)}) %collective-permute-start.1) | collective-permute-done | bytes 147488 | tf_op jit(solution)/shard_map/ppermute | solution.py:38
  17.9 0.0 collective-permute-done.2.refs_3_
  17.9 0.9 copy-done.9
  18.9 0.1 collective-permute-start.3
  19.0 1.6 %collective-permute-start.5 = (bf16[128,2304]{1,0:T(8,128)(2,1)S(1)}, bf16[128,2304]{1,0:T(8,128)(2,1)}, u32[]{:S(2)}, u32[]{:S(2)}) collective-permute-start(bf16[128,2304]{1,0:T(8,128)(2,1)S(1)} %get-tuple-element.41.high_ref), channel_id=1, source_target_pairs={{0,8},{8,0},{16,24},{24,16},{1,9},{9,1},{17,25},{25,17},{2,10},{10... | collective-permute-start | bytes 1769480 | tf_op jit(solution)/shard_map/ppermute | solution.py:38
  20.5 1.5 %collective-permute-start.6 = (bf16[128,2304]{1,0:T(8,128)(2,1)S(1)}, bf16[128,2304]{1,0:T(8,128)(2,1)}, u32[]{:S(2)}, u32[]{:S(2)}) collective-permute-start(bf16[128,2304]{1,0:T(8,128)(2,1)S(1)} %get-tuple-element.40.low_ref), channel_id=1, source_target_pairs={{0,16},{8,24},{16,0},{24,8},{1,17},{9,25},{17,1},{25,9},{2,18},{10... | collective-permute-start | bytes 1769480 | tf_op jit(solution)/shard_map/ppermute | solution.py:38
  22.0 0.1 stack.53.order_ref
  22.1 0.1 stack.54.order_ref
  22.2 7.3 %shard_map.77 = (bf16[2048,1536]{1,0:T(8,128)(2,1)S(1)}, f32[2048,256]{1,0:T(8,128)S(1)}, bf16[2048,768]{1,0:T(8,128)(2,1)S(1)}) custom-call(bf16[2048,1536]{1,0:T(8,128)(2,1)} %tea_ref.3, bf16[2048,768]{1,0:T(8,128)(2,1)} %images_ref.1, bf16[128,2304]{1,0:T(8,128)(2,1)S(1)} %get-tuple-element.40.low_ref, bf16[128,2304]{1,0:T(8,128)(2,1)S(1)} %get-tuple-element.41.high_ref), custom_call_target="tpu_custom_call" | custom-call | flops 1610612736 | bytes 6291456 | tf_op jit(solution)/shard_map/pallas_call | solution.py:161
  29.5 0.6 collective-permute-start.8
  30.1 0.0 collective-permute-done.7.refs_5_
  30.1 0.5 collective-permute-start.9
  30.6 3.8 %shard_map.79 = (bf16[2048,768]{1,0:T(8,128)(2,1)S(1)}, bf16[2048,768]{1,0:T(8,128)(2,1)S(1)}, bf16[768,768]{1,0:T(8,128)(2,1)S(1)}) custom-call(s32[8]{0:T(128)S(1)} %stack.53.order_ref, bf16[2048,768]{1,0:T(8,128)(2,1)S(1)} %get-tuple-element.42.images_ref, bf16[4,96,768]{2,1,0:T(8,128)(2,1)S(1)} %shard_map.78.near_ref, ...), custom_call_target="tpu_custom_call" | custom-call | flops 2415919104 | bytes 3145728 | tf_op jit(solution)/shard_map/pallas_call | solution.py:196
  34.4 3.3 %shard_map.80 = (f32[2048,768]{1,0:T(8,128)S(1)}, f32[256,768]{1,0:T(8,128)S(1)}) custom-call(f32[2048,256]{1,0:T(8,128)S(1)} %get-tuple-element.44._target_ref.target_ref, bf16[2048,768]{1,0:T(8,128)(2,1)S(1)} %get-tuple-element.45.emb_ref.refs_1_, bf16[128,2304]{1,0:T(8,128)(2,1)S(1)} %get-tuple-element.40.low_ref, ...), custom_call_target="tpu_custom_call" | custom-call | flops 2415919104 | bytes 1179648 | tf_op jit(solution)/shard_map/pallas_call | solution.py:238
  37.7 0.0 copy-start.1
  37.7 0.9 copy-done.1
  38.6 0.0 collective-permute-done.6.refs_4_
  38.6 10.6 %shard_map.81 = (f32[2048,768]{1,0:T(8,128)S(1)}, bf16[256,768]{1,0:T(8,128)(2,1)S(1)}, bf16[256,768]{1,0:T(8,128)(2,1)S(1)}) custom-call(bf16[2048,1536]{1,0:T(8,128)(2,1)S(1)} %get-tuple-element.43._tea_ref.refs_0_, bf16[2048,768]{1,0:T(8,128)(2,1)S(1)} %get-tuple-element.45.emb_ref.refs_1_, ...), custom_call_target="tpu_custom_call", output_to_operand_aliasing={{0}: (6, {})} | custom-call | flops 8053063680 | bytes 3932160 | tf_op jit(solution)/shard_map/pallas_call | solution.py:280
  49.2 0.0 collective-permute-done.8.refs_4_
  49.2 0.0 collective-permute-done.9.refs_5_
  49.2 7.0 %shard_map.82 = (bf16[1024,768]{1,0:T(8,128)(2,1)S(1)}, bf16[256,768]{1,0:T(8,128)(2,1)S(1)}, bf16[256,768]{1,0:T(8,128)(2,1)S(1)}, bf16[256,768]{1,0:T(8,128)(2...) custom-call(s32[8]{0:T(128)S(1)} %stack.54.order_ref, ...), custom_call_target="tpu_custom_call" | custom-call | flops 4026531840 | bytes 3145728 | tf_op jit(solution)/shard_map/pallas_call | solution.py:330
  56.2 0.1 collective-permute-start.10
  56.3 3.4 %collective-permute-done.10.take_ref = bf16[1024,768]{1,0:T(8,128)(2,1)S(1)} collective-permute-done((bf16[1024,768]{1,0:T(8,128)(2,1)S(1)}, bf16[1024,768]{1,0:T(8,128)(2,1)S(1)}, u32[]{:S(2)}, u32[]{:S(2)}) %collective-permute-start.10) | collective-permute-done | bytes 1572896 | tf_op jit(solution)/shard_map/ppermute | solution.py:38
  59.7 3.1 %shard_map.83 = (bf16[4,4,24,768]{3,2,1,0:T(8,128)(2,1)S(1)}, bf16[4,4,24,768]{3,2,1,0:T(8,128)(2,1)}, bf16[256,768]{1,0:T(8,128)(2,1)S(1)}, bf16[256,768]{1,0:T...) custom-call(s32[8]{0:T(128)S(1)} %stack.53.order_ref, ...), custom_call_target="tpu_custom_call" | custom-call | flops 1207959552 | bytes 3145728 | tf_op jit(solution)/shard_map/pallas_call | solution.py:372
  62.8 0.7 copy-done.10
  63.5 0.1 collective-permute-start.13
  63.7 2.4 %collective-permute-start.12 = (bf16[256,768]{1,0:T(8,128)(2,1)}, bf16[256,768]{1,0:T(8,128)(2,1)}, u32[]{:S(2)}, u32[]{:S(2)}) collective-permute-start(bf16[256,768]{1,0:T(8,128)(2,1)} %get-tuple-element.57), channel_id=1, source_target_pairs={{0,2},{1,3},{2,0},{3,1},{4,6},{5,7},{6,4},{7,5},{8,10},{9,11},{10,... | collective-permute-start | bytes 1179656 | tf_op jit(solution)/shard_map/ppermute | solution.py:38
  66.0 0.1 pad_add_fusion.order_ref
  66.1 0.6 shard_map.86
  66.7 1.6 %collective-permute-start.15 = (bf16[4,24,768]{2,1,0:T(8,128)(2,1)S(1)}, bf16[4,24,768]{2,1,0:T(8,128)(2,1)S(1)}, u32[]{:S(2)}, u32[]{:S(2)}) collective-permute-start(bf16[4,24,768]{2,1,0:T(8,128)(2,1)S(1)} %get-tuple-element.63), channel_id=1, source_target_pairs={{0,8},{8,0},{16,24},{24,16},{1,9},{9,1},{17,25},{25,17},{2,10},{10... | collective-permute-start | bytes 442376 | tf_op jit(solution)/shard_map/ppermute | solution.py:38
  68.3 1.5 %collective-permute-start.16 = (bf16[4,24,768]{2,1,0:T(8,128)(2,1)S(1)}, bf16[4,24,768]{2,1,0:T(8,128)(2,1)S(1)}, u32[]{:S(2)}, u32[]{:S(2)}) collective-permute-start(bf16[4,24,768]{2,1,0:T(8,128)(2,1)S(1)} %get-tuple-element.64), channel_id=1, source_target_pairs={{0,16},{8,24},{16,0},{24,8},{1,17},{9,25},{17,1},{25,9},{2,18},{10... | collective-permute-start | bytes 442376 | tf_op jit(solution)/shard_map/ppermute | solution.py:38
  69.8 0.5 collective-permute-start.17
  70.3 2.0 %collective-permute-start.11 = (bf16[256,768]{1,0:T(8,128)(2,1)}, bf16[256,768]{1,0:T(8,128)(2,1)S(1)}, u32[]{:S(2)}, u32[]{:S(2)}) collective-permute-start(bf16[256,768]{1,0:T(8,128)(2,1)} %copy-done.10), channel_id=1, source_target_pairs={{0,2},{1,3},{2,0},{3,1},{4,6},{5,7},{6,4},{7,5},{8,10},{9,11},{10,... | collective-permute-start | bytes 1179656 | tf_op jit(solution)/shard_map/ppermute | solution.py:38
  72.3 1.1 collective-permute-done.15.refs_1_
  73.3 3.7 %collective-permute-done.16.refs_2_ = bf16[4,24,768]{2,1,0:T(8,128)(2,1)S(1)} collective-permute-done((bf16[4,24,768]{2,1,0:T(8,128)(2,1)S(1)}, bf16[4,24,768]{2,1,0:T(8,128)(2,1)S(1)}, u32[]{:S(2)}, u32[]{:S(2)}) %collective-permute-start.16) | collective-permute-done | bytes 147488 | tf_op jit(solution)/shard_map/ppermute | solution.py:38
  77.0 0.1 shard_map.87
  77.1 3.1 %collective-permute-start.18 = (bf16[2,24,768]{2,1,0:T(8,128)(2,1)S(1)}, bf16[2,24,768]{2,1,0:T(8,128)(2,1)S(1)}, u32[]{:S(2)}, u32[]{:S(2)}) collective-permute-start(bf16[2,24,768]{2,1,0:T(8,128)(2,1)S(1)} %get-tuple-element.67), channel_id=1, source_target_pairs={{0,4},{1,5},{2,6},{3,7},{4,0},{5,1},{6,2},{7,3},{8,12},{9,13},{10,... | collective-permute-start | bytes 221192 | tf_op jit(solution)/shard_map/ppermute | solution.py:38
  80.2 1.2 %shard_map.84.refs_3_ = bf16[256,768]{1,0:T(8,128)(2,1)S(1)} custom-call(bf16[256,768]{1,0:T(8,128)(2,1)S(1)} %get-tuple-element.56.refs_0_, bf16[256,768]{1,0:T(8,128)(2,1)} %collective-permute-done.12.refs_1_, bf16[4,4,24,768]{3,2,1,0:T(8,128)(2,1)S(1)} %collective-permute-done.13.refs_2_.far_ref), custom_call_target="tpu_custom_call" | custom-call | tf_op jit(solution)/shard_map/pallas_call | solution.py:80
  81.4 0.1 collective-permute-start.14
  81.5 1.0 copy-done.4
  82.5 1.0 copy-done.6
  83.5 0.1 shard_map.91
  83.6 1.3 %collective-permute-start.23 = (bf16[256,768]{1,0:T(8,128)(2,1)S(1)}, bf16[256,768]{1,0:T(8,128)(2,1)S(1)}, u32[]{:S(2)}, u32[]{:S(2)}) collective-permute-start(bf16[256,768]{1,0:T(8,128)(2,1)S(1)} %get-tuple-element.74), channel_id=1, source_target_pairs={{0,8},{8,0},{16,24},{24,16},{1,9},{9,1},{17,25},{25,17},{2,10},{10... | collective-permute-start | bytes 1179656 | tf_op jit(solution)/shard_map/ppermute | solution.py:38
  84.9 0.8 collective-permute-start.24
  85.7 0.1 collective-permute-done.18.refs_1_
  85.7 2.5 %collective-permute-start.25 = (bf16[256,768]{1,0:T(8,128)(2,1)S(1)}, bf16[256,768]{1,0:T(8,128)(2,1)S(1)}, u32[]{:S(2)}, u32[]{:S(2)}) collective-permute-start(bf16[256,768]{1,0:T(8,128)(2,1)S(1)} %get-tuple-element.76), channel_id=1, source_target_pairs={{0,24},{8,16},{16,8},{24,0},{1,25},{9,17},{17,9},{25,1},{2,26},{10... | collective-permute-start | bytes 1179656 | tf_op jit(solution)/shard_map/ppermute | solution.py:38
  88.2 0.3 collective-permute-done.11.refs_1_.refs_2_
  88.5 3.3 %collective-permute-start.19 = (bf16[1,24,768]{2,1,0:T(8,128)(2,1)S(1)}, bf16[1,24,768]{2,1,0:T(8,128)(2,1)S(1)}, u32[]{:S(2)}, u32[]{:S(2)}) collective-permute-start(bf16[1,24,768]{2,1,0:T(8,128)(2,1)S(1)} %get-tuple-element.69), channel_id=1, source_target_pairs={{0,2},{1,3},{2,0},{3,1},{4,6},{5,7},{6,4},{7,5},{8,10},{9,11},{10,... | collective-permute-start | bytes 110600 | tf_op jit(solution)/shard_map/ppermute | solution.py:38
  91.8 2.6 %collective-permute-done.19.refs_1_ = bf16[1,24,768]{2,1,0:T(8,128)(2,1)S(1)} collective-permute-done((bf16[1,24,768]{2,1,0:T(8,128)(2,1)S(1)}, bf16[1,24,768]{2,1,0:T(8,128)(2,1)S(1)}, u32[]{:S(2)}, u32[]{:S(2)}) %collective-permute-start.19) | collective-permute-done | bytes 36896 | tf_op jit(solution)/shard_map/ppermute | solution.py:38
  94.4 7.9 %collective-permute-done.14.refs_2_.refs_3_ = bf16[256,768]{1,0:T(8,128)(2,1)S(1)} collective-permute-done((bf16[256,768]{1,0:T(8,128)(2,1)S(1)}, bf16[256,768]{1,0:T(8,128)(2,1)S(1)}, u32[]{:S(2)}, u32[]{:S(2)}) %collective-permute-start.14) | collective-permute-done | bytes 393248 | tf_op jit(solution)/shard_map/ppermute | solution.py:38
  102.3 1.4 %collective-permute-start.20 = (bf16[24,768]{1,0:T(8,128)(2,1)S(1)}, bf16[24,768]{1,0:T(8,128)(2,1)S(1)}, u32[]{:S(2)}, u32[]{:S(2)}) collective-permute-start(bf16[24,768]{1,0:T(8,128)(2,1)S(1)} %bitcast.14), channel_id=1, source_target_pairs={{0,8},{8,0},{16,24},{24,16},{1,9},{9,1},{17,25},{25,17},{2,10},{10... | collective-permute-start | bytes 110600 | tf_op jit(solution)/shard_map/ppermute | solution.py:38
  103.8 0.6 collective-permute-start.21
  104.3 1.6 %collective-permute-start.22 = (bf16[24,768]{1,0:T(8,128)(2,1)S(1)}, bf16[24,768]{1,0:T(8,128)(2,1)S(1)}, u32[]{:S(2)}, u32[]{:S(2)}) collective-permute-start(bf16[24,768]{1,0:T(8,128)(2,1)S(1)} %bitcast.16), channel_id=1, source_target_pairs={{0,24},{8,16},{16,8},{24,0},{1,25},{9,17},{17,9},{25,1},{2,26},{10... | collective-permute-start | bytes 110600 | tf_op jit(solution)/shard_map/ppermute | solution.py:38
  105.9 1.4 %shard_map.85 = (f32[256,768]{1,0:T(8,128)}, f32[8,128]{1,0:T(8,128)}) custom-call(bf16[256,768]{1,0:T(8,128)(2,1)S(1)} %get-tuple-element.54.refs_0_, bf16[256,768]{1,0:T(8,128)(2,1)S(1)} %collective-permute-done.11.refs_1_.refs_2_, bf16[256,768]{1,0:T(8,128)(2,1)S(1)} %collective-permute-done.14.refs_2_.refs_3_, bf16[768,768]{1,0:T(8,128)(2,1)S(1)} %get-tuple-element.59.refs_3_), custom_call_target="tpu_custom_call" | custom-call | tf_op jit(solution)/shard_map/pallas_call | solution.py:459
  107.3 1.3 %shard_map.92 = f32[256,768]{1,0:T(8,128)} custom-call(bf16[256,768]{1,0:T(8,128)(2,1)S(1)} %copy-done, f32[256,768]{1,0:T(8,128)S(1)} %copy-done.2, bf16[256,768]{1,0:T(8,128)(2,1)S(1)} %collective-permute-done.23.refs_0_, bf16[256,768]{1,0:T(8,128)(2,1)S(1)} %collective-permute-done.24.refs_1_, bf16[256,768]{1,0:T(8,128)(2,1)S(1)} %collective-permute-done.25.refs_2_), custom_call_target="tpu_custom_call" | custom-call | tf_op jit(solution)/shard_map/pallas_call | solution.py:439
  108.6 0.6 collective-permute-done.22.refs_3_
  109.2 0.7 shard_map.90
  109.9 0.9 copy.9
  (31 shorter events, 0.1 us)
Async XLA Ops:
  0.6 10.5 %collective-permute-start = (bf16[96,768]{1,0:T(8,128)(2,1)}, bf16[96,768]{1,0:T(8,128)(2,1)S(1)}, u32[]{:S(2)}, u32[]{:S(2)}) collective-permute-start(bf16[96,768]{1,0:T(8,128)(2,1)} %bitcast.18), channel_id=1, source_target_pairs={{0,2},{1,3},{2,0},{3,1},{4,6},{5,7},{6,4},{7,5},{8,10},{9,11},{10,... | collective-permute-start | bytes 442376 | tf_op jit(solution)/shard_map/ppermute | solution.py:38
  3.7 14.2 %collective-permute-start.1 = (bf16[96,768]{1,0:T(8,128)(2,1)}, bf16[96,768]{1,0:T(8,128)(2,1)S(1)}, u32[]{:S(2)}, u32[]{:S(2)}) collective-permute-start(bf16[96,768]{1,0:T(8,128)(2,1)} %bitcast.19), channel_id=1, source_target_pairs={{0,4},{1,5},{2,6},{3,7},{4,0},{5,1},{6,2},{7,3},{8,12},{9,13},{10,... | collective-permute-start | bytes 442376 | tf_op jit(solution)/shard_map/ppermute | solution.py:38
  6.3 11.6 %collective-permute-start.2 = (bf16[96,768]{1,0:T(8,128)(2,1)}, bf16[96,768]{1,0:T(8,128)(2,1)S(1)}, u32[]{:S(2)}, u32[]{:S(2)}) collective-permute-start(bf16[96,768]{1,0:T(8,128)(2,1)} %bitcast.20), channel_id=1, source_target_pairs={{0,6},{1,7},{2,4},{3,5},{4,2},{5,3},{6,0},{7,1},{8,14},{9,15},{10,... | collective-permute-start | bytes 442376 | tf_op jit(solution)/shard_map/ppermute | solution.py:38
  7.8 21.7 %collective-permute-start.4 = (bf16[128,2304]{1,0:T(8,128)(2,1)S(1)}, bf16[128,2304]{1,0:T(8,128)(2,1)}, u32[]{:S(2)}, u32[]{:S(2)}) collective-permute-start(bf16[128,2304]{1,0:T(8,128)(2,1)S(1)} %get-tuple-element.40.low_ref), channel_id=1, source_target_pairs={{0,8},{8,0},{16,24},{24,16},{1,9},{9,1},{17,25},{25,17},{2,10},{10... | collective-permute-start | bytes 1769480 | tf_op jit(solution)/shard_map/ppermute | solution.py:38
  9.6 20.5 %collective-permute-start.7 = (bf16[128,2304]{1,0:T(8,128)(2,1)S(1)}, bf16[128,2304]{1,0:T(8,128)(2,1)}, u32[]{:S(2)}, u32[]{:S(2)}) collective-permute-start(bf16[128,2304]{1,0:T(8,128)(2,1)S(1)} %get-tuple-element.41.high_ref), channel_id=1, source_target_pairs={{0,16},{8,24},{16,0},{24,8},{1,17},{9,25},{17,1},{25,9},{2,18},{10... | collective-permute-start | bytes 1769480 | tf_op jit(solution)/shard_map/ppermute | solution.py:38
  17.9 0.9 copy-start.9
  18.9 11.8 %collective-permute-start.3 = (bf16[4,96,768]{2,1,0:T(8,128)(2,1)S(1)}, bf16[4,96,768]{2,1,0:T(8,128)(2,1)S(1)}, u32[]{:S(2)}, u32[]{:S(2)}) collective-permute-start(bf16[4,96,768]{2,1,0:T(8,128)(2,1)S(1)} %shard_map.78.near_ref), channel_id=1, source_target_pairs={{0,1},{1,0},{2,3},{3,2},{4,5},{5,4},{6,7},{7,6},{8,9},{9,8},{10,11... | collective-permute-start | bytes 1769480 | tf_op jit(solution)/shard_map/ppermute | solution.py:38
  19.0 19.6 %collective-permute-start.5 = (bf16[128,2304]{1,0:T(8,128)(2,1)S(1)}, bf16[128,2304]{1,0:T(8,128)(2,1)}, u32[]{:S(2)}, u32[]{:S(2)}) collective-permute-start(bf16[128,2304]{1,0:T(8,128)(2,1)S(1)} %get-tuple-element.41.high_ref), channel_id=1, source_target_pairs={{0,8},{8,0},{16,24},{24,16},{1,9},{9,1},{17,25},{25,17},{2,10},{10... | collective-permute-start | bytes 1769480 | tf_op jit(solution)/shard_map/ppermute | solution.py:38
  20.5 18.1 %collective-permute-start.6 = (bf16[128,2304]{1,0:T(8,128)(2,1)S(1)}, bf16[128,2304]{1,0:T(8,128)(2,1)}, u32[]{:S(2)}, u32[]{:S(2)}) collective-permute-start(bf16[128,2304]{1,0:T(8,128)(2,1)S(1)} %get-tuple-element.40.low_ref), channel_id=1, source_target_pairs={{0,16},{8,24},{16,0},{24,8},{1,17},{9,25},{17,1},{25,9},{2,18},{10... | collective-permute-start | bytes 1769480 | tf_op jit(solution)/shard_map/ppermute | solution.py:38
  29.5 19.6 %collective-permute-start.8 = (bf16[128,2304]{1,0:T(8,128)(2,1)}, bf16[128,2304]{1,0:T(8,128)(2,1)S(1)}, u32[]{:S(2)}, u32[]{:S(2)}) collective-permute-start(bf16[128,2304]{1,0:T(8,128)(2,1)} %collective-permute-done.4.refs_2_), channel_id=1, source_target_pairs={{0,16},{8,24},{16,0},{24,8},{1,17},{9,25},{17,1},{25,9},{2,18},{10... | collective-permute-start | bytes 1769480 | tf_op jit(solution)/shard_map/ppermute | solution.py:38
  30.1 19.0 %collective-permute-start.9 = (bf16[128,2304]{1,0:T(8,128)(2,1)}, bf16[128,2304]{1,0:T(8,128)(2,1)S(1)}, u32[]{:S(2)}, u32[]{:S(2)}) collective-permute-start(bf16[128,2304]{1,0:T(8,128)(2,1)} %collective-permute-done.7.refs_5_), channel_id=1, source_target_pairs={{0,8},{8,0},{16,24},{24,16},{1,9},{9,1},{17,25},{25,17},{2,10},{10... | collective-permute-start | bytes 1769480 | tf_op jit(solution)/shard_map/ppermute | solution.py:38
  37.7 0.9 copy-start.1
  49.1 7.0 %copy-start.3 = (bf16[256,768]{1,0:T(8,128)(2,1)}, bf16[256,768]{1,0:T(8,128)(2,1)S(1)}, u32[]{:S(2)}) copy-start(bf16[256,768]{1,0:T(8,128)(2,1)S(1)} %get-tuple-element.71.refs_0_) | copy-start | bytes 1179652
  49.1 7.0 %copy-start.5 = (bf16[256,768]{1,0:T(8,128)(2,1)}, bf16[256,768]{1,0:T(8,128)(2,1)S(1)}, u32[]{:S(2)}) copy-start(bf16[256,768]{1,0:T(8,128)(2,1)S(1)} %get-tuple-element.72.refs_1_) | copy-start | bytes 1179652
  56.2 6.6 %copy-start.7 = (bf16[256,768]{1,0:T(8,128)(2,1)}, bf16[256,768]{1,0:T(8,128)(2,1)S(1)}, u32[]{:S(2)}) copy-start(bf16[256,768]{1,0:T(8,128)(2,1)S(1)} %get-tuple-element.73.refs_2_) | copy-start | bytes 1179652
  56.2 3.5 %collective-permute-start.10 = (bf16[1024,768]{1,0:T(8,128)(2,1)S(1)}, bf16[1024,768]{1,0:T(8,128)(2,1)S(1)}, u32[]{:S(2)}, u32[]{:S(2)}) collective-permute-start(bf16[1024,768]{1,0:T(8,128)(2,1)S(1)} %get-tuple-element.49), channel_id=1, source_target_pairs={{0,1},{1,0},{2,3},{3,2},{4,5},{5,4},{6,7},{7,6},{8,9},{9,8},{10,11... | collective-permute-start | bytes 4718600 | tf_op jit(solution)/shard_map/ppermute | solution.py:38
  62.8 0.7 copy-start.10
  63.5 2.6 %collective-permute-start.13 = (bf16[4,4,24,768]{3,2,1,0:T(8,128)(2,1)}, bf16[4,4,24,768]{3,2,1,0:T(8,128)(2,1)S(1)}, u32[]{:S(2)}, u32[]{:S(2)}) collective-permute-start(bf16[4,4,24,768]{3,2,1,0:T(8,128)(2,1)} %get-tuple-element.58), channel_id=1, source_target_pairs={{0,1},{1,0},{2,3},{3,2},{4,5},{5,4},{6,7},{7,6},{8,9},{9,8},{10,11... | collective-permute-start | bytes 1769480 | tf_op jit(solution)/shard_map/ppermute | solution.py:38
  63.7 16.5 %collective-permute-start.12 = (bf16[256,768]{1,0:T(8,128)(2,1)}, bf16[256,768]{1,0:T(8,128)(2,1)}, u32[]{:S(2)}, u32[]{:S(2)}) collective-permute-start(bf16[256,768]{1,0:T(8,128)(2,1)} %get-tuple-element.57), channel_id=1, source_target_pairs={{0,2},{1,3},{2,0},{3,1},{4,6},{5,7},{6,4},{7,5},{8,10},{9,11},{10,... | collective-permute-start | bytes 1179656 | tf_op jit(solution)/shard_map/ppermute | solution.py:38
  66.0 15.5 %copy-start.8 = (bf16[256,768]{1,0:T(8,128)(2,1)S(1)}, bf16[256,768]{1,0:T(8,128)(2,1)}, u32[]{:S(2)}) copy-start(bf16[256,768]{1,0:T(8,128)(2,1)} %copy-done.7) | copy-start | bytes 1179652
  66.7 6.6 %collective-permute-start.15 = (bf16[4,24,768]{2,1,0:T(8,128)(2,1)S(1)}, bf16[4,24,768]{2,1,0:T(8,128)(2,1)S(1)}, u32[]{:S(2)}, u32[]{:S(2)}) collective-permute-start(bf16[4,24,768]{2,1,0:T(8,128)(2,1)S(1)} %get-tuple-element.63), channel_id=1, source_target_pairs={{0,8},{8,0},{16,24},{24,16},{1,9},{9,1},{17,25},{25,17},{2,10},{10... | collective-permute-start | bytes 442376 | tf_op jit(solution)/shard_map/ppermute | solution.py:38
  68.3 8.7 %collective-permute-start.16 = (bf16[4,24,768]{2,1,0:T(8,128)(2,1)S(1)}, bf16[4,24,768]{2,1,0:T(8,128)(2,1)S(1)}, u32[]{:S(2)}, u32[]{:S(2)}) collective-permute-start(bf16[4,24,768]{2,1,0:T(8,128)(2,1)S(1)} %get-tuple-element.64), channel_id=1, source_target_pairs={{0,16},{8,24},{16,0},{24,8},{1,17},{9,25},{17,1},{25,9},{2,18},{10... | collective-permute-start | bytes 442376 | tf_op jit(solution)/shard_map/ppermute | solution.py:38
  69.8 7.2 %collective-permute-start.17 = (bf16[4,24,768]{2,1,0:T(8,128)(2,1)S(1)}, bf16[4,24,768]{2,1,0:T(8,128)(2,1)S(1)}, u32[]{:S(2)}, u32[]{:S(2)}) collective-permute-start(bf16[4,24,768]{2,1,0:T(8,128)(2,1)S(1)} %get-tuple-element.65), channel_id=1, source_target_pairs={{0,24},{8,16},{16,8},{24,0},{1,25},{9,17},{17,9},{25,1},{2,26},{10... | collective-permute-start | bytes 442376 | tf_op jit(solution)/shard_map/ppermute | solution.py:38
  70.3 18.3 %collective-permute-start.11 = (bf16[256,768]{1,0:T(8,128)(2,1)}, bf16[256,768]{1,0:T(8,128)(2,1)S(1)}, u32[]{:S(2)}, u32[]{:S(2)}) collective-permute-start(bf16[256,768]{1,0:T(8,128)(2,1)} %copy-done.10), channel_id=1, source_target_pairs={{0,2},{1,3},{2,0},{3,1},{4,6},{5,7},{6,4},{7,5},{8,10},{9,11},{10,... | collective-permute-start | bytes 1179656 | tf_op jit(solution)/shard_map/ppermute | solution.py:38
  77.1 8.7 %collective-permute-start.18 = (bf16[2,24,768]{2,1,0:T(8,128)(2,1)S(1)}, bf16[2,24,768]{2,1,0:T(8,128)(2,1)S(1)}, u32[]{:S(2)}, u32[]{:S(2)}) collective-permute-start(bf16[2,24,768]{2,1,0:T(8,128)(2,1)S(1)} %get-tuple-element.67), channel_id=1, source_target_pairs={{0,4},{1,5},{2,6},{3,7},{4,0},{5,1},{6,2},{7,3},{8,12},{9,13},{10,... | collective-permute-start | bytes 221192 | tf_op jit(solution)/shard_map/ppermute | solution.py:38
  80.2 27.1 %copy-start = (bf16[256,768]{1,0:T(8,128)(2,1)S(1)}, bf16[256,768]{1,0:T(8,128)(2,1)}, u32[]{:S(2)}) copy-start(bf16[256,768]{1,0:T(8,128)(2,1)} %stu_ref.3) | copy-start | bytes 1179652
  80.2 27.1 %copy-start.2 = (f32[256,768]{1,0:T(8,128)S(1)}, f32[256,768]{1,0:T(8,128)}, u32[]{:S(2)}) copy-start(f32[256,768]{1,0:T(8,128)} %copy-done.1) | copy-start | bytes 2359300
  81.4 21.0 %collective-permute-start.14 = (bf16[256,768]{1,0:T(8,128)(2,1)S(1)}, bf16[256,768]{1,0:T(8,128)(2,1)S(1)}, u32[]{:S(2)}, u32[]{:S(2)}) collective-permute-start(bf16[256,768]{1,0:T(8,128)(2,1)S(1)} %shard_map.84.refs_3_), channel_id=1, source_target_pairs={{0,4},{1,5},{2,6},{3,7},{4,0},{5,1},{6,2},{7,3},{8,12},{9,13},{10,... | collective-permute-start | bytes 1179656 | tf_op jit(solution)/shard_map/ppermute | solution.py:38
  81.5 1.0 copy-start.4
  82.5 1.0 copy-start.6
  83.6 20.8 %collective-permute-start.23 = (bf16[256,768]{1,0:T(8,128)(2,1)S(1)}, bf16[256,768]{1,0:T(8,128)(2,1)S(1)}, u32[]{:S(2)}, u32[]{:S(2)}) collective-permute-start(bf16[256,768]{1,0:T(8,128)(2,1)S(1)} %get-tuple-element.74), channel_id=1, source_target_pairs={{0,8},{8,0},{16,24},{24,16},{1,9},{9,1},{17,25},{25,17},{2,10},{10... | collective-permute-start | bytes 1179656 | tf_op jit(solution)/shard_map/ppermute | solution.py:38
  84.9 22.4 %collective-permute-start.24 = (bf16[256,768]{1,0:T(8,128)(2,1)S(1)}, bf16[256,768]{1,0:T(8,128)(2,1)S(1)}, u32[]{:S(2)}, u32[]{:S(2)}) collective-permute-start(bf16[256,768]{1,0:T(8,128)(2,1)S(1)} %get-tuple-element.75), channel_id=1, source_target_pairs={{0,16},{8,24},{16,0},{24,8},{1,17},{9,25},{17,1},{25,9},{2,18},{10... | collective-permute-start | bytes 1179656 | tf_op jit(solution)/shard_map/ppermute | solution.py:38
  85.7 21.6 %collective-permute-start.25 = (bf16[256,768]{1,0:T(8,128)(2,1)S(1)}, bf16[256,768]{1,0:T(8,128)(2,1)S(1)}, u32[]{:S(2)}, u32[]{:S(2)}) collective-permute-start(bf16[256,768]{1,0:T(8,128)(2,1)S(1)} %get-tuple-element.76), channel_id=1, source_target_pairs={{0,24},{8,16},{16,8},{24,0},{1,25},{9,17},{17,9},{25,1},{2,26},{10... | collective-permute-start | bytes 1179656 | tf_op jit(solution)/shard_map/ppermute | solution.py:38
  88.5 5.9 %collective-permute-start.19 = (bf16[1,24,768]{2,1,0:T(8,128)(2,1)S(1)}, bf16[1,24,768]{2,1,0:T(8,128)(2,1)S(1)}, u32[]{:S(2)}, u32[]{:S(2)}) collective-permute-start(bf16[1,24,768]{2,1,0:T(8,128)(2,1)S(1)} %get-tuple-element.69), channel_id=1, source_target_pairs={{0,2},{1,3},{2,0},{3,1},{4,6},{5,7},{6,4},{7,5},{8,10},{9,11},{10,... | collective-permute-start | bytes 110600 | tf_op jit(solution)/shard_map/ppermute | solution.py:38
  102.3 6.3 %collective-permute-start.20 = (bf16[24,768]{1,0:T(8,128)(2,1)S(1)}, bf16[24,768]{1,0:T(8,128)(2,1)S(1)}, u32[]{:S(2)}, u32[]{:S(2)}) collective-permute-start(bf16[24,768]{1,0:T(8,128)(2,1)S(1)} %bitcast.14), channel_id=1, source_target_pairs={{0,8},{8,0},{16,24},{24,16},{1,9},{9,1},{17,25},{25,17},{2,10},{10... | collective-permute-start | bytes 110600 | tf_op jit(solution)/shard_map/ppermute | solution.py:38
  103.8 4.9 %collective-permute-start.21 = (bf16[24,768]{1,0:T(8,128)(2,1)S(1)}, bf16[24,768]{1,0:T(8,128)(2,1)S(1)}, u32[]{:S(2)}, u32[]{:S(2)}) collective-permute-start(bf16[24,768]{1,0:T(8,128)(2,1)S(1)} %bitcast.15), channel_id=1, source_target_pairs={{0,16},{8,24},{16,0},{24,8},{1,17},{9,25},{17,1},{25,9},{2,18},{10... | collective-permute-start | bytes 110600 | tf_op jit(solution)/shard_map/ppermute | solution.py:38
  104.3 4.9 %collective-permute-start.22 = (bf16[24,768]{1,0:T(8,128)(2,1)S(1)}, bf16[24,768]{1,0:T(8,128)(2,1)S(1)}, u32[]{:S(2)}, u32[]{:S(2)}) collective-permute-start(bf16[24,768]{1,0:T(8,128)(2,1)S(1)} %bitcast.16), channel_id=1, source_target_pairs={{0,24},{8,16},{16,8},{24,0},{1,25},{9,17},{17,9},{25,1},{2,26},{10... | collective-permute-start | bytes 110600 | tf_op jit(solution)/shard_map/ppermute | solution.py:38

commit v5 on v4

--- a/solution.py
+++ b/solution.py
@@ -406,7 +406,7 @@
         total_ref[order_ref[k]] = ref[...].astype(f32)
     rows = total_ref.shape[1]
     total = jnp.concatenate([total_ref[k] for k in range(len(pieces))])
-    out_ref[...] = total.T * scale
+    out_ref[...] = total * scale
 
 
 def head_result(order, pieces, scale):
@@ -416,7 +416,7 @@
         functools.partial(head_result_kernel, scale),
         in_specs=[pl.BlockSpec(memory_space=pltpu.SMEM)] + [resident] * count,
         out_specs=resident,
-        out_shape=jax.ShapeDtypeStruct((depth, count * rows), f32),
+        out_shape=jax.ShapeDtypeStruct((count * rows, depth), f32),
         scratch_shapes=[pltpu.VMEM((count, rows, depth), f32)],
         compiler_params=params(),
         cost_estimate=cost(0, 0),
@@ -527,7 +527,7 @@
     (own,) = sums([held], arrived)
     own = own[0]
     shares = [own] + [swap(own, "dp", mask) for mask in range(1, dp_count)]
-    grad_head = head_result(dp_order, shares, factor)
+    grad_head = head_result(dp_order, shares, factor).T
 
     grad_text = text_result(stu_txt, text_grads[0], list(got.values()), factor / half_scale)
     return (grad_images, grad_head, grad_text)

time: 111 us -> 111 us (level)
    unnamed x23 -> x22, local copies, waits for them, and re-layouts: 5.41 us -> 4.54 us
where the time goes in v5:
time: 111 us; the launch traced here: 110 us
  Pallas kernels  42.5 us (38%)
  starting transfers between devices  36 us (32%)
  waiting for transfers between devices  26.4 us (24%)
  local copies, waits for them, and re-layouts  4.71 us (4%)
    ppermute x26, starting transfers between devices, swap(): lax.ppermute(value, axis, [(source, source ^ mask) for source in range(co...  36 us
    ppermute x26, waiting for transfers between devices, swap(): lax.ppermute(value, axis, [(source, source ^ mask) for source in range(co...  26.4 us
    pallas_call x1, Pallas kernels, early(): pl.pallas_call(functools.partial(early_kernel, count), in_specs=[resident...  10.6 us
    pallas_call x1, Pallas kernels, teacher_emb(): pl.pallas_call(teacher_kernel, grid=(rows // chunk,), in_specs=[row(width...  7.32 us
    pallas_call x1, Pallas kernels, late(): pl.pallas_call(functools.partial(late_kernel, count, masks, summed), in_s...  7 us
    unnamed x22, local copies, waits for them, and re-layouts  4.54 us
    pallas_call x1, Pallas kernels, projections(): pl.pallas_call(proj_kernel, in_specs=[pl.BlockSpec(memory_space=pltpu.SME...  3.76 us
    pallas_call x1, Pallas kernels, own_texts(): pl.pallas_call(own_kernel, in_specs=[resident] * 5, out_specs=[resident,...  3.27 us
  transfers between devices with their start and end apart: 26, of which 9 were waited for; matrix products, arithmetic and copies ran while one was open for 0% of the time, Pallas kernels for 28%

profile of v5, /device:TPU:0, one launch (start us, length us, event | category | flops | bytes accessed | tf_op | source)
XLA Modules:
  0.0 110.5 jit_solution(9188534220222797310)
XLA Ops:
  0.6 3.1 %collective-permute-start = (bf16[96,768]{1,0:T(8,128)(2,1)}, bf16[96,768]{1,0:T(8,128)(2,1)S(1)}, u32[]{:S(2)}, u32[]{:S(2)}) collective-permute-start(bf16[96,768]{1,0:T(8,128)(2,1)} %bitcast.19), channel_id=1, source_target_pairs={{0,2},{1,3},{2,0},{3,1},{4,6},{5,7},{6,4},{7,5},{8,10},{9,11},{10,... | collective-permute-start | bytes 442376 | tf_op jit(solution)/shard_map/ppermute | solution.py:38
  3.7 2.6 %collective-permute-start.1 = (bf16[96,768]{1,0:T(8,128)(2,1)}, bf16[96,768]{1,0:T(8,128)(2,1)S(1)}, u32[]{:S(2)}, u32[]{:S(2)}) collective-permute-start(bf16[96,768]{1,0:T(8,128)(2,1)} %bitcast.20), channel_id=1, source_target_pairs={{0,4},{1,5},{2,6},{3,7},{4,0},{5,1},{6,2},{7,3},{8,12},{9,13},{10,... | collective-permute-start | bytes 442376 | tf_op jit(solution)/shard_map/ppermute | solution.py:38
  6.3 0.0 collective-permute-start.2
  6.3 1.5 %shard_map.76 = (bf16[128,2304]{1,0:T(8,128)(2,1)S(1)}, bf16[128,2304]{1,0:T(8,128)(2,1)S(1)}) custom-call(bf16[256,1536]{1,0:T(8,128)(2,1)} %tea_ref.2, bf16[256,768]{1,0:T(8,128)(2,1)} %stu_ref.3), custom_call_target="tpu_custom_call" | custom-call | flops 1572864 | bytes 1572864 | tf_op jit(solution)/shard_map/pallas_call | solution.py:131
  7.8 1.8 %collective-permute-start.4 = (bf16[128,2304]{1,0:T(8,128)(2,1)S(1)}, bf16[128,2304]{1,0:T(8,128)(2,1)}, u32[]{:S(2)}, u32[]{:S(2)}) collective-permute-start(bf16[128,2304]{1,0:T(8,128)(2,1)S(1)} %get-tuple-element.40.low_ref), channel_id=1, source_target_pairs={{0,8},{8,0},{16,24},{24,16},{1,9},{9,1},{17,25},{25,17},{2,10},{10... | collective-permute-start | bytes 1769480 | tf_op jit(solution)/shard_map/ppermute | solution.py:38
  9.6 1.5 %collective-permute-start.7 = (bf16[128,2304]{1,0:T(8,128)(2,1)S(1)}, bf16[128,2304]{1,0:T(8,128)(2,1)}, u32[]{:S(2)}, u32[]{:S(2)}) collective-permute-start(bf16[128,2304]{1,0:T(8,128)(2,1)S(1)} %get-tuple-element.41.high_ref), channel_id=1, source_target_pairs={{0,16},{8,24},{16,0},{24,8},{1,17},{9,25},{17,1},{25,9},{2,18},{10... | collective-permute-start | bytes 1769480 | tf_op jit(solution)/shard_map/ppermute | solution.py:38
  11.1 0.0 collective-permute-done.refs_1_
  11.1 6.8 %collective-permute-done.1.refs_2_ = bf16[96,768]{1,0:T(8,128)(2,1)S(1)} collective-permute-done((bf16[96,768]{1,0:T(8,128)(2,1)}, bf16[96,768]{1,0:T(8,128)(2,1)S(1)}, u32[]{:S(2)}, u32[]{:S(2)}) %collective-permute-start.1) | collective-permute-done | bytes 147488 | tf_op jit(solution)/shard_map/ppermute | solution.py:38
  17.9 0.9 copy-done.9
  18.9 0.1 collective-permute-start.3
  19.0 1.6 %collective-permute-start.5 = (bf16[128,2304]{1,0:T(8,128)(2,1)S(1)}, bf16[128,2304]{1,0:T(8,128)(2,1)}, u32[]{:S(2)}, u32[]{:S(2)}) collective-permute-start(bf16[128,2304]{1,0:T(8,128)(2,1)S(1)} %get-tuple-element.41.high_ref), channel_id=1, source_target_pairs={{0,8},{8,0},{16,24},{24,16},{1,9},{9,1},{17,25},{25,17},{2,10},{10... | collective-permute-start | bytes 1769480 | tf_op jit(solution)/shard_map/ppermute | solution.py:38
  20.5 1.5 %collective-permute-start.6 = (bf16[128,2304]{1,0:T(8,128)(2,1)S(1)}, bf16[128,2304]{1,0:T(8,128)(2,1)}, u32[]{:S(2)}, u32[]{:S(2)}) collective-permute-start(bf16[128,2304]{1,0:T(8,128)(2,1)S(1)} %get-tuple-element.40.low_ref), channel_id=1, source_target_pairs={{0,16},{8,24},{16,0},{24,8},{1,17},{9,25},{17,1},{25,9},{2,18},{10... | collective-permute-start | bytes 1769480 | tf_op jit(solution)/shard_map/ppermute | solution.py:38
  22.0 0.1 stack.53.order_ref
  22.1 0.1 stack.54.order_ref
  22.2 7.3 %shard_map.77 = (bf16[2048,1536]{1,0:T(8,128)(2,1)S(1)}, f32[2048,256]{1,0:T(8,128)S(1)}, bf16[2048,768]{1,0:T(8,128)(2,1)S(1)}) custom-call(bf16[2048,1536]{1,0:T(8,128)(2,1)} %tea_ref.3, bf16[2048,768]{1,0:T(8,128)(2,1)} %images_ref.1, bf16[128,2304]{1,0:T(8,128)(2,1)S(1)} %get-tuple-element.40.low_ref, bf16[128,2304]{1,0:T(8,128)(2,1)S(1)} %get-tuple-element.41.high_ref), custom_call_target="tpu_custom_call" | custom-call | flops 1610612736 | bytes 6291456 | tf_op jit(solution)/shard_map/pallas_call | solution.py:161
  29.5 0.0 collective-permute-done.4.refs_2_
  29.5 0.6 collective-permute-start.8
  30.1 0.5 collective-permute-start.9
  30.6 0.0 collective-permute-done.3.far_ref
  30.6 3.8 %shard_map.79 = (bf16[2048,768]{1,0:T(8,128)(2,1)S(1)}, bf16[2048,768]{1,0:T(8,128)(2,1)S(1)}, bf16[768,768]{1,0:T(8,128)(2,1)S(1)}) custom-call(s32[8]{0:T(128)S(1)} %stack.53.order_ref, bf16[2048,768]{1,0:T(8,128)(2,1)S(1)} %get-tuple-element.42.images_ref, bf16[4,96,768]{2,1,0:T(8,128)(2,1)S(1)} %shard_map.78.near_ref, ...), custom_call_target="tpu_custom_call" | custom-call | flops 2415919104 | bytes 3145728 | tf_op jit(solution)/shard_map/pallas_call | solution.py:196
  34.4 3.3 %shard_map.80 = (f32[2048,768]{1,0:T(8,128)S(1)}, f32[256,768]{1,0:T(8,128)S(1)}) custom-call(f32[2048,256]{1,0:T(8,128)S(1)} %get-tuple-element.44._target_ref.target_ref, bf16[2048,768]{1,0:T(8,128)(2,1)S(1)} %get-tuple-element.45.emb_ref.refs_1_, bf16[128,2304]{1,0:T(8,128)(2,1)S(1)} %get-tuple-element.40.low_ref, ...), custom_call_target="tpu_custom_call" | custom-call | flops 2415919104 | bytes 1179648 | tf_op jit(solution)/shard_map/pallas_call | solution.py:238
  37.7 0.0 copy-start.1
  37.7 0.9 copy-done.1
  38.6 0.0 collective-permute-done.5.refs_3_
  38.6 0.0 collective-permute-done.6.refs_4_
  38.6 10.6 %shard_map.81 = (f32[2048,768]{1,0:T(8,128)S(1)}, bf16[256,768]{1,0:T(8,128)(2,1)S(1)}, bf16[256,768]{1,0:T(8,128)(2,1)S(1)}) custom-call(bf16[2048,1536]{1,0:T(8,128)(2,1)S(1)} %get-tuple-element.43._tea_ref.refs_0_, bf16[2048,768]{1,0:T(8,128)(2,1)S(1)} %get-tuple-element.45.emb_ref.refs_1_, ...), custom_call_target="tpu_custom_call", output_to_operand_aliasing={{0}: (6, {})} | custom-call | flops 8053063680 | bytes 3932160 | tf_op jit(solution)/shard_map/pallas_call | solution.py:280
  49.2 0.0 collective-permute-done.9.refs_5_
  49.2 7.0 %shard_map.82 = (bf16[1024,768]{1,0:T(8,128)(2,1)S(1)}, bf16[256,768]{1,0:T(8,128)(2,1)S(1)}, bf16[256,768]{1,0:T(8,128)(2,1)S(1)}, bf16[256,768]{1,0:T(8,128)(2...) custom-call(s32[8]{0:T(128)S(1)} %stack.54.order_ref, ...), custom_call_target="tpu_custom_call" | custom-call | flops 4026531840 | bytes 3145728 | tf_op jit(solution)/shard_map/pallas_call | solution.py:330
  56.2 0.1 collective-permute-start.10
  56.3 3.4 %collective-permute-done.10.take_ref = bf16[1024,768]{1,0:T(8,128)(2,1)S(1)} collective-permute-done((bf16[1024,768]{1,0:T(8,128)(2,1)S(1)}, bf16[1024,768]{1,0:T(8,128)(2,1)S(1)}, u32[]{:S(2)}, u32[]{:S(2)}) %collective-permute-start.10) | collective-permute-done | bytes 1572896 | tf_op jit(solution)/shard_map/ppermute | solution.py:38
  59.7 3.1 %shard_map.83 = (bf16[4,4,24,768]{3,2,1,0:T(8,128)(2,1)S(1)}, bf16[4,4,24,768]{3,2,1,0:T(8,128)(2,1)}, bf16[256,768]{1,0:T(8,128)(2,1)S(1)}, bf16[256,768]{1,0:T...) custom-call(s32[8]{0:T(128)S(1)} %stack.53.order_ref, ...), custom_call_target="tpu_custom_call" | custom-call | flops 1207959552 | bytes 3145728 | tf_op jit(solution)/shard_map/pallas_call | solution.py:372
  62.8 0.7 copy-done.10
  63.5 0.1 collective-permute-start.13
  63.7 2.4 %collective-permute-start.12 = (bf16[256,768]{1,0:T(8,128)(2,1)}, bf16[256,768]{1,0:T(8,128)(2,1)}, u32[]{:S(2)}, u32[]{:S(2)}) collective-permute-start(bf16[256,768]{1,0:T(8,128)(2,1)} %get-tuple-element.57), channel_id=1, source_target_pairs={{0,2},{1,3},{2,0},{3,1},{4,6},{5,7},{6,4},{7,5},{8,10},{9,11},{10,... | collective-permute-start | bytes 1179656 | tf_op jit(solution)/shard_map/ppermute | solution.py:38
  66.0 0.1 pad_add_fusion.order_ref
  66.1 0.6 shard_map.86
  66.7 1.6 %collective-permute-start.15 = (bf16[4,24,768]{2,1,0:T(8,128)(2,1)S(1)}, bf16[4,24,768]{2,1,0:T(8,128)(2,1)S(1)}, u32[]{:S(2)}, u32[]{:S(2)}) collective-permute-start(bf16[4,24,768]{2,1,0:T(8,128)(2,1)S(1)} %get-tuple-element.63), channel_id=1, source_target_pairs={{0,8},{8,0},{16,24},{24,16},{1,9},{9,1},{17,25},{25,17},{2,10},{10... | collective-permute-start | bytes 442376 | tf_op jit(solution)/shard_map/ppermute | solution.py:38
  68.3 1.5 %collective-permute-start.16 = (bf16[4,24,768]{2,1,0:T(8,128)(2,1)S(1)}, bf16[4,24,768]{2,1,0:T(8,128)(2,1)S(1)}, u32[]{:S(2)}, u32[]{:S(2)}) collective-permute-start(bf16[4,24,768]{2,1,0:T(8,128)(2,1)S(1)} %get-tuple-element.64), channel_id=1, source_target_pairs={{0,16},{8,24},{16,0},{24,8},{1,17},{9,25},{17,1},{25,9},{2,18},{10... | collective-permute-start | bytes 442376 | tf_op jit(solution)/shard_map/ppermute | solution.py:38
  69.8 0.5 collective-permute-start.17
  70.3 2.0 %collective-permute-start.11 = (bf16[256,768]{1,0:T(8,128)(2,1)}, bf16[256,768]{1,0:T(8,128)(2,1)S(1)}, u32[]{:S(2)}, u32[]{:S(2)}) collective-permute-start(bf16[256,768]{1,0:T(8,128)(2,1)} %copy-done.10), channel_id=1, source_target_pairs={{0,2},{1,3},{2,0},{3,1},{4,6},{5,7},{6,4},{7,5},{8,10},{9,11},{10,... | collective-permute-start | bytes 1179656 | tf_op jit(solution)/shard_map/ppermute | solution.py:38
  72.3 1.1 collective-permute-done.15.refs_1_
  73.3 3.7 %collective-permute-done.16.refs_2_ = bf16[4,24,768]{2,1,0:T(8,128)(2,1)S(1)} collective-permute-done((bf16[4,24,768]{2,1,0:T(8,128)(2,1)S(1)}, bf16[4,24,768]{2,1,0:T(8,128)(2,1)S(1)}, u32[]{:S(2)}, u32[]{:S(2)}) %collective-permute-start.16) | collective-permute-done | bytes 147488 | tf_op jit(solution)/shard_map/ppermute | solution.py:38
  77.0 0.1 shard_map.87
  77.1 3.1 %collective-permute-start.18 = (bf16[2,24,768]{2,1,0:T(8,128)(2,1)S(1)}, bf16[2,24,768]{2,1,0:T(8,128)(2,1)S(1)}, u32[]{:S(2)}, u32[]{:S(2)}) collective-permute-start(bf16[2,24,768]{2,1,0:T(8,128)(2,1)S(1)} %get-tuple-element.67), channel_id=1, source_target_pairs={{0,4},{1,5},{2,6},{3,7},{4,0},{5,1},{6,2},{7,3},{8,12},{9,13},{10,... | collective-permute-start | bytes 221192 | tf_op jit(solution)/shard_map/ppermute | solution.py:38
  80.2 1.2 %shard_map.84.refs_3_ = bf16[256,768]{1,0:T(8,128)(2,1)S(1)} custom-call(bf16[256,768]{1,0:T(8,128)(2,1)S(1)} %get-tuple-element.56.refs_0_, bf16[256,768]{1,0:T(8,128)(2,1)} %collective-permute-done.12.refs_1_, bf16[4,4,24,768]{3,2,1,0:T(8,128)(2,1)S(1)} %collective-permute-done.13.refs_2_.far_ref), custom_call_target="tpu_custom_call" | custom-call | tf_op jit(solution)/shard_map/pallas_call | solution.py:80
  81.4 0.1 collective-permute-start.14
  81.5 1.0 copy-done.4
  82.5 1.0 copy-done.6
  83.5 0.1 shard_map.91
  83.6 1.3 %collective-permute-start.23 = (bf16[256,768]{1,0:T(8,128)(2,1)S(1)}, bf16[256,768]{1,0:T(8,128)(2,1)S(1)}, u32[]{:S(2)}, u32[]{:S(2)}) collective-permute-start(bf16[256,768]{1,0:T(8,128)(2,1)S(1)} %get-tuple-element.74), channel_id=1, source_target_pairs={{0,8},{8,0},{16,24},{24,16},{1,9},{9,1},{17,25},{25,17},{2,10},{10... | collective-permute-start | bytes 1179656 | tf_op jit(solution)/shard_map/ppermute | solution.py:38
  84.9 0.8 collective-permute-start.24
  85.7 0.1 collective-permute-done.18.refs_1_
  85.7 2.5 %collective-permute-start.25 = (bf16[256,768]{1,0:T(8,128)(2,1)S(1)}, bf16[256,768]{1,0:T(8,128)(2,1)S(1)}, u32[]{:S(2)}, u32[]{:S(2)}) collective-permute-start(bf16[256,768]{1,0:T(8,128)(2,1)S(1)} %get-tuple-element.76), channel_id=1, source_target_pairs={{0,24},{8,16},{16,8},{24,0},{1,25},{9,17},{17,9},{25,1},{2,26},{10... | collective-permute-start | bytes 1179656 | tf_op jit(solution)/shard_map/ppermute | solution.py:38
  88.2 0.3 collective-permute-done.11.refs_1_.refs_2_
  88.5 3.3 %collective-permute-start.19 = (bf16[1,24,768]{2,1,0:T(8,128)(2,1)S(1)}, bf16[1,24,768]{2,1,0:T(8,128)(2,1)S(1)}, u32[]{:S(2)}, u32[]{:S(2)}) collective-permute-start(bf16[1,24,768]{2,1,0:T(8,128)(2,1)S(1)} %get-tuple-element.69), channel_id=1, source_target_pairs={{0,2},{1,3},{2,0},{3,1},{4,6},{5,7},{6,4},{7,5},{8,10},{9,11},{10,... | collective-permute-start | bytes 110600 | tf_op jit(solution)/shard_map/ppermute | solution.py:38
  91.8 2.6 %collective-permute-done.19.refs_1_ = bf16[1,24,768]{2,1,0:T(8,128)(2,1)S(1)} collective-permute-done((bf16[1,24,768]{2,1,0:T(8,128)(2,1)S(1)}, bf16[1,24,768]{2,1,0:T(8,128)(2,1)S(1)}, u32[]{:S(2)}, u32[]{:S(2)}) %collective-permute-start.19) | collective-permute-done | bytes 36896 | tf_op jit(solution)/shard_map/ppermute | solution.py:38
  94.4 7.9 %collective-permute-done.14.refs_2_.refs_3_ = bf16[256,768]{1,0:T(8,128)(2,1)S(1)} collective-permute-done((bf16[256,768]{1,0:T(8,128)(2,1)S(1)}, bf16[256,768]{1,0:T(8,128)(2,1)S(1)}, u32[]{:S(2)}, u32[]{:S(2)}) %collective-permute-start.14) | collective-permute-done | bytes 393248 | tf_op jit(solution)/shard_map/ppermute | solution.py:38
  102.3 1.4 %collective-permute-start.20 = (bf16[24,768]{1,0:T(8,128)(2,1)S(1)}, bf16[24,768]{1,0:T(8,128)(2,1)S(1)}, u32[]{:S(2)}, u32[]{:S(2)}) collective-permute-start(bf16[24,768]{1,0:T(8,128)(2,1)S(1)} %bitcast.15), channel_id=1, source_target_pairs={{0,8},{8,0},{16,24},{24,16},{1,9},{9,1},{17,25},{25,17},{2,10},{10... | collective-permute-start | bytes 110600 | tf_op jit(solution)/shard_map/ppermute | solution.py:38
  103.8 0.6 collective-permute-start.21
  104.3 1.6 %collective-permute-start.22 = (bf16[24,768]{1,0:T(8,128)(2,1)S(1)}, bf16[24,768]{1,0:T(8,128)(2,1)S(1)}, u32[]{:S(2)}, u32[]{:S(2)}) collective-permute-start(bf16[24,768]{1,0:T(8,128)(2,1)S(1)} %bitcast.17), channel_id=1, source_target_pairs={{0,24},{8,16},{16,8},{24,0},{1,25},{9,17},{17,9},{25,1},{2,26},{10... | collective-permute-start | bytes 110600 | tf_op jit(solution)/shard_map/ppermute | solution.py:38
  105.9 1.4 %shard_map.85 = (f32[256,768]{1,0:T(8,128)}, f32[8,128]{1,0:T(8,128)}) custom-call(bf16[256,768]{1,0:T(8,128)(2,1)S(1)} %get-tuple-element.54.refs_0_, bf16[256,768]{1,0:T(8,128)(2,1)S(1)} %collective-permute-done.11.refs_1_.refs_2_, bf16[256,768]{1,0:T(8,128)(2,1)S(1)} %collective-permute-done.14.refs_2_.refs_3_, bf16[768,768]{1,0:T(8,128)(2,1)S(1)} %get-tuple-element.59.refs_3_), custom_call_target="tpu_custom_call" | custom-call | tf_op jit(solution)/shard_map/pallas_call | solution.py:459
  107.3 1.3 %shard_map.92 = f32[256,768]{1,0:T(8,128)} custom-call(bf16[256,768]{1,0:T(8,128)(2,1)S(1)} %copy-done, f32[256,768]{1,0:T(8,128)S(1)} %copy-done.2, bf16[256,768]{1,0:T(8,128)(2,1)S(1)} %collective-permute-done.23.refs_0_, bf16[256,768]{1,0:T(8,128)(2,1)S(1)} %collective-permute-done.24.refs_1_, bf16[256,768]{1,0:T(8,128)(2,1)S(1)} %collective-permute-done.25.refs_2_), custom_call_target="tpu_custom_call" | custom-call | tf_op jit(solution)/shard_map/pallas_call | solution.py:439
  108.6 0.6 collective-permute-done.22.refs_3_
  109.2 1.3 %shard_map.90 = f32[96,768]{1,0:T(8,128)} custom-call(s32[4]{0:T(128)S(1)} %pad_add_fusion.order_ref, bf16[24,768]{1,0:T(8,128)(2,1)S(1)} %bitcast.18, bf16[24,768]{1,0:T(8,128)(2,1)S(1)} %collective-permute-done.20.refs_1_, bf16[24,768]{1,0:T(8,128)(2,1)S(1)} %collective-permute-done.21.refs_2_, bf16[24,768]{1,0:T(8,128)(2,1)S(1)} %collective-permute-done.22.refs_3_), custom_call_target="tpu_custom_call" | custom-call | tf_op jit(solution)/shard_map/pallas_call | solution.py:415
  (30 shorter events, 0.1 us)
Async XLA Ops:
  0.6 10.5 %collective-permute-start = (bf16[96,768]{1,0:T(8,128)(2,1)}, bf16[96,768]{1,0:T(8,128)(2,1)S(1)}, u32[]{:S(2)}, u32[]{:S(2)}) collective-permute-start(bf16[96,768]{1,0:T(8,128)(2,1)} %bitcast.19), channel_id=1, source_target_pairs={{0,2},{1,3},{2,0},{3,1},{4,6},{5,7},{6,4},{7,5},{8,10},{9,11},{10,... | collective-permute-start | bytes 442376 | tf_op jit(solution)/shard_map/ppermute | solution.py:38
  3.7 14.2 %collective-permute-start.1 = (bf16[96,768]{1,0:T(8,128)(2,1)}, bf16[96,768]{1,0:T(8,128)(2,1)S(1)}, u32[]{:S(2)}, u32[]{:S(2)}) collective-permute-start(bf16[96,768]{1,0:T(8,128)(2,1)} %bitcast.20), channel_id=1, source_target_pairs={{0,4},{1,5},{2,6},{3,7},{4,0},{5,1},{6,2},{7,3},{8,12},{9,13},{10,... | collective-permute-start | bytes 442376 | tf_op jit(solution)/shard_map/ppermute | solution.py:38
  6.3 11.6 %collective-permute-start.2 = (bf16[96,768]{1,0:T(8,128)(2,1)}, bf16[96,768]{1,0:T(8,128)(2,1)S(1)}, u32[]{:S(2)}, u32[]{:S(2)}) collective-permute-start(bf16[96,768]{1,0:T(8,128)(2,1)} %bitcast.21), channel_id=1, source_target_pairs={{0,6},{1,7},{2,4},{3,5},{4,2},{5,3},{6,0},{7,1},{8,14},{9,15},{10,... | collective-permute-start | bytes 442376 | tf_op jit(solution)/shard_map/ppermute | solution.py:38
  7.8 21.7 %collective-permute-start.4 = (bf16[128,2304]{1,0:T(8,128)(2,1)S(1)}, bf16[128,2304]{1,0:T(8,128)(2,1)}, u32[]{:S(2)}, u32[]{:S(2)}) collective-permute-start(bf16[128,2304]{1,0:T(8,128)(2,1)S(1)} %get-tuple-element.40.low_ref), channel_id=1, source_target_pairs={{0,8},{8,0},{16,24},{24,16},{1,9},{9,1},{17,25},{25,17},{2,10},{10... | collective-permute-start | bytes 1769480 | tf_op jit(solution)/shard_map/ppermute | solution.py:38
  9.6 20.5 %collective-permute-start.7 = (bf16[128,2304]{1,0:T(8,128)(2,1)S(1)}, bf16[128,2304]{1,0:T(8,128)(2,1)}, u32[]{:S(2)}, u32[]{:S(2)}) collective-permute-start(bf16[128,2304]{1,0:T(8,128)(2,1)S(1)} %get-tuple-element.41.high_ref), channel_id=1, source_target_pairs={{0,16},{8,24},{16,0},{24,8},{1,17},{9,25},{17,1},{25,9},{2,18},{10... | collective-permute-start | bytes 1769480 | tf_op jit(solution)/shard_map/ppermute | solution.py:38
  17.9 0.9 copy-start.9
  18.9 11.8 %collective-permute-start.3 = (bf16[4,96,768]{2,1,0:T(8,128)(2,1)S(1)}, bf16[4,96,768]{2,1,0:T(8,128)(2,1)S(1)}, u32[]{:S(2)}, u32[]{:S(2)}) collective-permute-start(bf16[4,96,768]{2,1,0:T(8,128)(2,1)S(1)} %shard_map.78.near_ref), channel_id=1, source_target_pairs={{0,1},{1,0},{2,3},{3,2},{4,5},{5,4},{6,7},{7,6},{8,9},{9,8},{10,11... | collective-permute-start | bytes 1769480 | tf_op jit(solution)/shard_map/ppermute | solution.py:38
  19.0 19.6 %collective-permute-start.5 = (bf16[128,2304]{1,0:T(8,128)(2,1)S(1)}, bf16[128,2304]{1,0:T(8,128)(2,1)}, u32[]{:S(2)}, u32[]{:S(2)}) collective-permute-start(bf16[128,2304]{1,0:T(8,128)(2,1)S(1)} %get-tuple-element.41.high_ref), channel_id=1, source_target_pairs={{0,8},{8,0},{16,24},{24,16},{1,9},{9,1},{17,25},{25,17},{2,10},{10... | collective-permute-start | bytes 1769480 | tf_op jit(solution)/shard_map/ppermute | solution.py:38
  20.5 18.1 %collective-permute-start.6 = (bf16[128,2304]{1,0:T(8,128)(2,1)S(1)}, bf16[128,2304]{1,0:T(8,128)(2,1)}, u32[]{:S(2)}, u32[]{:S(2)}) collective-permute-start(bf16[128,2304]{1,0:T(8,128)(2,1)S(1)} %get-tuple-element.40.low_ref), channel_id=1, source_target_pairs={{0,16},{8,24},{16,0},{24,8},{1,17},{9,25},{17,1},{25,9},{2,18},{10... | collective-permute-start | bytes 1769480 | tf_op jit(solution)/shard_map/ppermute | solution.py:38
  29.5 19.6 %collective-permute-start.8 = (bf16[128,2304]{1,0:T(8,128)(2,1)}, bf16[128,2304]{1,0:T(8,128)(2,1)S(1)}, u32[]{:S(2)}, u32[]{:S(2)}) collective-permute-start(bf16[128,2304]{1,0:T(8,128)(2,1)} %collective-permute-done.4.refs_2_), channel_id=1, source_target_pairs={{0,16},{8,24},{16,0},{24,8},{1,17},{9,25},{17,1},{25,9},{2,18},{10... | collective-permute-start | bytes 1769480 | tf_op jit(solution)/shard_map/ppermute | solution.py:38
  30.1 19.0 %collective-permute-start.9 = (bf16[128,2304]{1,0:T(8,128)(2,1)}, bf16[128,2304]{1,0:T(8,128)(2,1)S(1)}, u32[]{:S(2)}, u32[]{:S(2)}) collective-permute-start(bf16[128,2304]{1,0:T(8,128)(2,1)} %collective-permute-done.7.refs_5_), channel_id=1, source_target_pairs={{0,8},{8,0},{16,24},{24,16},{1,9},{9,1},{17,25},{25,17},{2,10},{10... | collective-permute-start | bytes 1769480 | tf_op jit(solution)/shard_map/ppermute | solution.py:38
  37.7 0.9 copy-start.1
  49.1 7.0 %copy-start.3 = (bf16[256,768]{1,0:T(8,128)(2,1)}, bf16[256,768]{1,0:T(8,128)(2,1)S(1)}, u32[]{:S(2)}) copy-start(bf16[256,768]{1,0:T(8,128)(2,1)S(1)} %get-tuple-element.71.refs_0_) | copy-start | bytes 1179652
  49.1 7.0 %copy-start.5 = (bf16[256,768]{1,0:T(8,128)(2,1)}, bf16[256,768]{1,0:T(8,128)(2,1)S(1)}, u32[]{:S(2)}) copy-start(bf16[256,768]{1,0:T(8,128)(2,1)S(1)} %get-tuple-element.72.refs_1_) | copy-start | bytes 1179652
  56.2 6.6 %copy-start.7 = (bf16[256,768]{1,0:T(8,128)(2,1)}, bf16[256,768]{1,0:T(8,128)(2,1)S(1)}, u32[]{:S(2)}) copy-start(bf16[256,768]{1,0:T(8,128)(2,1)S(1)} %get-tuple-element.73.refs_2_) | copy-start | bytes 1179652
  56.2 3.5 %collective-permute-start.10 = (bf16[1024,768]{1,0:T(8,128)(2,1)S(1)}, bf16[1024,768]{1,0:T(8,128)(2,1)S(1)}, u32[]{:S(2)}, u32[]{:S(2)}) collective-permute-start(bf16[1024,768]{1,0:T(8,128)(2,1)S(1)} %get-tuple-element.49), channel_id=1, source_target_pairs={{0,1},{1,0},{2,3},{3,2},{4,5},{5,4},{6,7},{7,6},{8,9},{9,8},{10,11... | collective-permute-start | bytes 4718600 | tf_op jit(solution)/shard_map/ppermute | solution.py:38
  62.8 0.7 copy-start.10
  63.5 2.6 %collective-permute-start.13 = (bf16[4,4,24,768]{3,2,1,0:T(8,128)(2,1)}, bf16[4,4,24,768]{3,2,1,0:T(8,128)(2,1)S(1)}, u32[]{:S(2)}, u32[]{:S(2)}) collective-permute-start(bf16[4,4,24,768]{3,2,1,0:T(8,128)(2,1)} %get-tuple-element.58), channel_id=1, source_target_pairs={{0,1},{1,0},{2,3},{3,2},{4,5},{5,4},{6,7},{7,6},{8,9},{9,8},{10,11... | collective-permute-start | bytes 1769480 | tf_op jit(solution)/shard_map/ppermute | solution.py:38
  63.7 16.5 %collective-permute-start.12 = (bf16[256,768]{1,0:T(8,128)(2,1)}, bf16[256,768]{1,0:T(8,128)(2,1)}, u32[]{:S(2)}, u32[]{:S(2)}) collective-permute-start(bf16[256,768]{1,0:T(8,128)(2,1)} %get-tuple-element.57), channel_id=1, source_target_pairs={{0,2},{1,3},{2,0},{3,1},{4,6},{5,7},{6,4},{7,5},{8,10},{9,11},{10,... | collective-permute-start | bytes 1179656 | tf_op jit(solution)/shard_map/ppermute | solution.py:38
  66.0 15.5 %copy-start.8 = (bf16[256,768]{1,0:T(8,128)(2,1)S(1)}, bf16[256,768]{1,0:T(8,128)(2,1)}, u32[]{:S(2)}) copy-start(bf16[256,768]{1,0:T(8,128)(2,1)} %copy-done.7) | copy-start | bytes 1179652
  66.7 6.6 %collective-permute-start.15 = (bf16[4,24,768]{2,1,0:T(8,128)(2,1)S(1)}, bf16[4,24,768]{2,1,0:T(8,128)(2,1)S(1)}, u32[]{:S(2)}, u32[]{:S(2)}) collective-permute-start(bf16[4,24,768]{2,1,0:T(8,128)(2,1)S(1)} %get-tuple-element.63), channel_id=1, source_target_pairs={{0,8},{8,0},{16,24},{24,16},{1,9},{9,1},{17,25},{25,17},{2,10},{10... | collective-permute-start | bytes 442376 | tf_op jit(solution)/shard_map/ppermute | solution.py:38
  68.3 8.7 %collective-permute-start.16 = (bf16[4,24,768]{2,1,0:T(8,128)(2,1)S(1)}, bf16[4,24,768]{2,1,0:T(8,128)(2,1)S(1)}, u32[]{:S(2)}, u32[]{:S(2)}) collective-permute-start(bf16[4,24,768]{2,1,0:T(8,128)(2,1)S(1)} %get-tuple-element.64), channel_id=1, source_target_pairs={{0,16},{8,24},{16,0},{24,8},{1,17},{9,25},{17,1},{25,9},{2,18},{10... | collective-permute-start | bytes 442376 | tf_op jit(solution)/shard_map/ppermute | solution.py:38
  69.8 7.2 %collective-permute-start.17 = (bf16[4,24,768]{2,1,0:T(8,128)(2,1)S(1)}, bf16[4,24,768]{2,1,0:T(8,128)(2,1)S(1)}, u32[]{:S(2)}, u32[]{:S(2)}) collective-permute-start(bf16[4,24,768]{2,1,0:T(8,128)(2,1)S(1)} %get-tuple-element.65), channel_id=1, source_target_pairs={{0,24},{8,16},{16,8},{24,0},{1,25},{9,17},{17,9},{25,1},{2,26},{10... | collective-permute-start | bytes 442376 | tf_op jit(solution)/shard_map/ppermute | solution.py:38
  70.3 18.3 %collective-permute-start.11 = (bf16[256,768]{1,0:T(8,128)(2,1)}, bf16[256,768]{1,0:T(8,128)(2,1)S(1)}, u32[]{:S(2)}, u32[]{:S(2)}) collective-permute-start(bf16[256,768]{1,0:T(8,128)(2,1)} %copy-done.10), channel_id=1, source_target_pairs={{0,2},{1,3},{2,0},{3,1},{4,6},{5,7},{6,4},{7,5},{8,10},{9,11},{10,... | collective-permute-start | bytes 1179656 | tf_op jit(solution)/shard_map/ppermute | solution.py:38
  77.1 8.7 %collective-permute-start.18 = (bf16[2,24,768]{2,1,0:T(8,128)(2,1)S(1)}, bf16[2,24,768]{2,1,0:T(8,128)(2,1)S(1)}, u32[]{:S(2)}, u32[]{:S(2)}) collective-permute-start(bf16[2,24,768]{2,1,0:T(8,128)(2,1)S(1)} %get-tuple-element.67), channel_id=1, source_target_pairs={{0,4},{1,5},{2,6},{3,7},{4,0},{5,1},{6,2},{7,3},{8,12},{9,13},{10,... | collective-permute-start | bytes 221192 | tf_op jit(solution)/shard_map/ppermute | solution.py:38
  80.2 27.1 %copy-start = (bf16[256,768]{1,0:T(8,128)(2,1)S(1)}, bf16[256,768]{1,0:T(8,128)(2,1)}, u32[]{:S(2)}) copy-start(bf16[256,768]{1,0:T(8,128)(2,1)} %stu_ref.3) | copy-start | bytes 1179652
  80.2 27.1 %copy-start.2 = (f32[256,768]{1,0:T(8,128)S(1)}, f32[256,768]{1,0:T(8,128)}, u32[]{:S(2)}) copy-start(f32[256,768]{1,0:T(8,128)} %copy-done.1) | copy-start | bytes 2359300
  81.4 21.0 %collective-permute-start.14 = (bf16[256,768]{1,0:T(8,128)(2,1)S(1)}, bf16[256,768]{1,0:T(8,128)(2,1)S(1)}, u32[]{:S(2)}, u32[]{:S(2)}) collective-permute-start(bf16[256,768]{1,0:T(8,128)(2,1)S(1)} %shard_map.84.refs_3_), channel_id=1, source_target_pairs={{0,4},{1,5},{2,6},{3,7},{4,0},{5,1},{6,2},{7,3},{8,12},{9,13},{10,... | collective-permute-start | bytes 1179656 | tf_op jit(solution)/shard_map/ppermute | solution.py:38
  81.5 1.0 copy-start.4
  82.5 1.0 copy-start.6
  83.6 20.8 %collective-permute-start.23 = (bf16[256,768]{1,0:T(8,128)(2,1)S(1)}, bf16[256,768]{1,0:T(8,128)(2,1)S(1)}, u32[]{:S(2)}, u32[]{:S(2)}) collective-permute-start(bf16[256,768]{1,0:T(8,128)(2,1)S(1)} %get-tuple-element.74), channel_id=1, source_target_pairs={{0,8},{8,0},{16,24},{24,16},{1,9},{9,1},{17,25},{25,17},{2,10},{10... | collective-permute-start | bytes 1179656 | tf_op jit(solution)/shard_map/ppermute | solution.py:38
  84.9 22.4 %collective-permute-start.24 = (bf16[256,768]{1,0:T(8,128)(2,1)S(1)}, bf16[256,768]{1,0:T(8,128)(2,1)S(1)}, u32[]{:S(2)}, u32[]{:S(2)}) collective-permute-start(bf16[256,768]{1,0:T(8,128)(2,1)S(1)} %get-tuple-element.75), channel_id=1, source_target_pairs={{0,16},{8,24},{16,0},{24,8},{1,17},{9,25},{17,1},{25,9},{2,18},{10... | collective-permute-start | bytes 1179656 | tf_op jit(solution)/shard_map/ppermute | solution.py:38
  85.7 21.6 %collective-permute-start.25 = (bf16[256,768]{1,0:T(8,128)(2,1)S(1)}, bf16[256,768]{1,0:T(8,128)(2,1)S(1)}, u32[]{:S(2)}, u32[]{:S(2)}) collective-permute-start(bf16[256,768]{1,0:T(8,128)(2,1)S(1)} %get-tuple-element.76), channel_id=1, source_target_pairs={{0,24},{8,16},{16,8},{24,0},{1,25},{9,17},{17,9},{25,1},{2,26},{10... | collective-permute-start | bytes 1179656 | tf_op jit(solution)/shard_map/ppermute | solution.py:38
  88.5 5.9 %collective-permute-start.19 = (bf16[1,24,768]{2,1,0:T(8,128)(2,1)S(1)}, bf16[1,24,768]{2,1,0:T(8,128)(2,1)S(1)}, u32[]{:S(2)}, u32[]{:S(2)}) collective-permute-start(bf16[1,24,768]{2,1,0:T(8,128)(2,1)S(1)} %get-tuple-element.69), channel_id=1, source_target_pairs={{0,2},{1,3},{2,0},{3,1},{4,6},{5,7},{6,4},{7,5},{8,10},{9,11},{10,... | collective-permute-start | bytes 110600 | tf_op jit(solution)/shard_map/ppermute | solution.py:38
  102.3 6.3 %collective-permute-start.20 = (bf16[24,768]{1,0:T(8,128)(2,1)S(1)}, bf16[24,768]{1,0:T(8,128)(2,1)S(1)}, u32[]{:S(2)}, u32[]{:S(2)}) collective-permute-start(bf16[24,768]{1,0:T(8,128)(2,1)S(1)} %bitcast.15), channel_id=1, source_target_pairs={{0,8},{8,0},{16,24},{24,16},{1,9},{9,1},{17,25},{25,17},{2,10},{10... | collective-permute-start | bytes 110600 | tf_op jit(solution)/shard_map/ppermute | solution.py:38
  103.8 4.9 %collective-permute-start.21 = (bf16[24,768]{1,0:T(8,128)(2,1)S(1)}, bf16[24,768]{1,0:T(8,128)(2,1)S(1)}, u32[]{:S(2)}, u32[]{:S(2)}) collective-permute-start(bf16[24,768]{1,0:T(8,128)(2,1)S(1)} %bitcast.16), channel_id=1, source_target_pairs={{0,16},{8,24},{16,0},{24,8},{1,17},{9,25},{17,1},{25,9},{2,18},{10... | collective-permute-start | bytes 110600 | tf_op jit(solution)/shard_map/ppermute | solution.py:38
  104.3 4.9 %collective-permute-start.22 = (bf16[24,768]{1,0:T(8,128)(2,1)S(1)}, bf16[24,768]{1,0:T(8,128)(2,1)S(1)}, u32[]{:S(2)}, u32[]{:S(2)}) collective-permute-start(bf16[24,768]{1,0:T(8,128)(2,1)S(1)} %bitcast.17), channel_id=1, source_target_pairs={{0,24},{8,16},{16,8},{24,0},{1,25},{9,17},{17,9},{25,1},{2,26},{10... | collective-permute-start | bytes 110600 | tf_op jit(solution)/shard_map/ppermute | solution.py:38

commit v6 on v5

--- a/solution.py
+++ b/solution.py
@@ -282,7 +282,7 @@
         in_specs=[resident] * len(given),
         out_specs=[resident] * (1 + size // share),
         out_shape=[pltpu.VMEM((rows, emb_width), f32)]
-        + [jax.ShapeDtypeStruct((share, emb_width), bf16)] * (size // share),
+        + [pltpu.VMEM((share, emb_width), bf16)] * (size // share),
         input_output_aliases={len(given) - 1: 0},
         scratch_shapes=[pltpu.VMEM((size, emb_width), f32), pltpu.VMEM((size, width), bf16)],
         compiler_params=params(4 * size * width + 4 * size * emb_width),
@@ -514,7 +514,7 @@
         targets = [mask ^ 1 << bit for mask in sent]
         if targets:
             parts.update(zip(targets, sums([[parts[mask], block] for mask, block in zip(targets, passed)], [far])))
-    leaving = sums([[text_grads[mask]] for mask in range(1, dp_count)], [parts[pairs // 2]])
+    leaving = sums([[pinned(text_grads[mask]) if mask in middle else text_grads[mask]] for mask in range(1, dp_count)], [parts[pairs // 2]])
     got = {mask: swap(block, "dp", mask) for mask, block in zip(range(1, dp_count), leaving)}
     arrived = [swap(parts[1 << bit], "tensor", 2 << bit) for bit in range(pairs.bit_length() - 1)]
     grad_images, images_mark = image_grads([parts[0]] + arrived, head_full, factor)

time: 111 us -> 111 us (level)
  no operation moved by 1% of the time
where the time goes in v6:
time: 111 us; the launch traced here: 110 us
  Pallas kernels  42.5 us (38%)
  starting transfers between devices  36 us (32%)
  waiting for transfers between devices  26.4 us (24%)
  local copies, waits for them, and re-layouts  4.71 us (4%)
    ppermute x26, starting transfers between devices, swap(): lax.ppermute(value, axis, [(source, source ^ mask) for source in range(co...  36 us
    ppermute x26, waiting for transfers between devices, swap(): lax.ppermute(value, axis, [(source, source ^ mask) for source in range(co...  26.4 us
    pallas_call x1, Pallas kernels, early(): pl.pallas_call(functools.partial(early_kernel, count), in_specs=[resident...  10.6 us
    pallas_call x1, Pallas kernels, teacher_emb(): pl.pallas_call(teacher_kernel, grid=(rows // chunk,), in_specs=[row(width...  7.32 us
    pallas_call x1, Pallas kernels, late(): pl.pallas_call(functools.partial(late_kernel, count, masks, summed), in_s...  7 us
    unnamed x22, local copies, waits for them, and re-layouts  4.54 us
    pallas_call x1, Pallas kernels, projections(): pl.pallas_call(proj_kernel, in_specs=[pl.BlockSpec(memory_space=pltpu.SME...  3.76 us
    pallas_call x1, Pallas kernels, own_texts(): pl.pallas_call(own_kernel, in_specs=[resident] * 5, out_specs=[resident,...  3.27 us
  transfers between devices with their start and end apart: 26, of which 9 were waited for; matrix products, arithmetic and copies ran while one was open for 0% of the time, Pallas kernels for 28%

profile of v6, /device:TPU:0, one launch (start us, length us, event | category | flops | bytes accessed | tf_op | source)
XLA Modules:
  0.0 110.5 jit_solution(9188534220222797310)
XLA Ops:
  0.6 3.1 %collective-permute-start = (bf16[96,768]{1,0:T(8,128)(2,1)}, bf16[96,768]{1,0:T(8,128)(2,1)S(1)}, u32[]{:S(2)}, u32[]{:S(2)}) collective-permute-start(bf16[96,768]{1,0:T(8,128)(2,1)} %bitcast.19), channel_id=1, source_target_pairs={{0,2},{1,3},{2,0},{3,1},{4,6},{5,7},{6,4},{7,5},{8,10},{9,11},{10,... | collective-permute-start | bytes 442376 | tf_op jit(solution)/shard_map/ppermute | solution.py:38
  3.7 2.6 %collective-permute-start.1 = (bf16[96,768]{1,0:T(8,128)(2,1)}, bf16[96,768]{1,0:T(8,128)(2,1)S(1)}, u32[]{:S(2)}, u32[]{:S(2)}) collective-permute-start(bf16[96,768]{1,0:T(8,128)(2,1)} %bitcast.20), channel_id=1, source_target_pairs={{0,4},{1,5},{2,6},{3,7},{4,0},{5,1},{6,2},{7,3},{8,12},{9,13},{10,... | collective-permute-start | bytes 442376 | tf_op jit(solution)/shard_map/ppermute | solution.py:38
  6.3 0.0 collective-permute-start.2
  6.3 1.5 %shard_map.76 = (bf16[128,2304]{1,0:T(8,128)(2,1)S(1)}, bf16[128,2304]{1,0:T(8,128)(2,1)S(1)}) custom-call(bf16[256,1536]{1,0:T(8,128)(2,1)} %tea_ref.2, bf16[256,768]{1,0:T(8,128)(2,1)} %stu_ref.3), custom_call_target="tpu_custom_call" | custom-call | flops 1572864 | bytes 1572864 | tf_op jit(solution)/shard_map/pallas_call | solution.py:131
  7.8 1.8 %collective-permute-start.4 = (bf16[128,2304]{1,0:T(8,128)(2,1)S(1)}, bf16[128,2304]{1,0:T(8,128)(2,1)}, u32[]{:S(2)}, u32[]{:S(2)}) collective-permute-start(bf16[128,2304]{1,0:T(8,128)(2,1)S(1)} %get-tuple-element.40.low_ref), channel_id=1, source_target_pairs={{0,8},{8,0},{16,24},{24,16},{1,9},{9,1},{17,25},{25,17},{2,10},{10... | collective-permute-start | bytes 1769480 | tf_op jit(solution)/shard_map/ppermute | solution.py:38
  9.6 1.5 %collective-permute-start.7 = (bf16[128,2304]{1,0:T(8,128)(2,1)S(1)}, bf16[128,2304]{1,0:T(8,128)(2,1)}, u32[]{:S(2)}, u32[]{:S(2)}) collective-permute-start(bf16[128,2304]{1,0:T(8,128)(2,1)S(1)} %get-tuple-element.41.high_ref), channel_id=1, source_target_pairs={{0,16},{8,24},{16,0},{24,8},{1,17},{9,25},{17,1},{25,9},{2,18},{10... | collective-permute-start | bytes 1769480 | tf_op jit(solution)/shard_map/ppermute | solution.py:38
  11.1 0.0 collective-permute-done.refs_1_
  11.1 6.8 %collective-permute-done.1.refs_2_ = bf16[96,768]{1,0:T(8,128)(2,1)S(1)} collective-permute-done((bf16[96,768]{1,0:T(8,128)(2,1)}, bf16[96,768]{1,0:T(8,128)(2,1)S(1)}, u32[]{:S(2)}, u32[]{:S(2)}) %collective-permute-start.1) | collective-permute-done | bytes 147488 | tf_op jit(solution)/shard_map/ppermute | solution.py:38
  17.9 0.9 copy-done.9
  18.9 0.1 collective-permute-start.3
  19.0 1.6 %collective-permute-start.5 = (bf16[128,2304]{1,0:T(8,128)(2,1)S(1)}, bf16[128,2304]{1,0:T(8,128)(2,1)}, u32[]{:S(2)}, u32[]{:S(2)}) collective-permute-start(bf16[128,2304]{1,0:T(8,128)(2,1)S(1)} %get-tuple-element.41.high_ref), channel_id=1, source_target_pairs={{0,8},{8,0},{16,24},{24,16},{1,9},{9,1},{17,25},{25,17},{2,10},{10... | collective-permute-start | bytes 1769480 | tf_op jit(solution)/shard_map/ppermute | solution.py:38
  20.5 1.5 %collective-permute-start.6 = (bf16[128,2304]{1,0:T(8,128)(2,1)S(1)}, bf16[128,2304]{1,0:T(8,128)(2,1)}, u32[]{:S(2)}, u32[]{:S(2)}) collective-permute-start(bf16[128,2304]{1,0:T(8,128)(2,1)S(1)} %get-tuple-element.40.low_ref), channel_id=1, source_target_pairs={{0,16},{8,24},{16,0},{24,8},{1,17},{9,25},{17,1},{25,9},{2,18},{10... | collective-permute-start | bytes 1769480 | tf_op jit(solution)/shard_map/ppermute | solution.py:38
  22.0 0.1 stack.53.order_ref
  22.1 0.1 stack.54.order_ref
  22.2 7.3 %shard_map.77 = (bf16[2048,1536]{1,0:T(8,128)(2,1)S(1)}, f32[2048,256]{1,0:T(8,128)S(1)}, bf16[2048,768]{1,0:T(8,128)(2,1)S(1)}) custom-call(bf16[2048,1536]{1,0:T(8,128)(2,1)} %tea_ref.3, bf16[2048,768]{1,0:T(8,128)(2,1)} %images_ref.1, bf16[128,2304]{1,0:T(8,128)(2,1)S(1)} %get-tuple-element.40.low_ref, bf16[128,2304]{1,0:T(8,128)(2,1)S(1)} %get-tuple-element.41.high_ref), custom_call_target="tpu_custom_call" | custom-call | flops 1610612736 | bytes 6291456 | tf_op jit(solution)/shard_map/pallas_call | solution.py:161
  29.5 0.0 collective-permute-done.4.refs_2_
  29.5 0.6 collective-permute-start.8
  30.1 0.5 collective-permute-start.9
  30.6 0.0 collective-permute-done.3.far_ref
  30.6 3.8 %shard_map.79 = (bf16[2048,768]{1,0:T(8,128)(2,1)S(1)}, bf16[2048,768]{1,0:T(8,128)(2,1)S(1)}, bf16[768,768]{1,0:T(8,128)(2,1)S(1)}) custom-call(s32[8]{0:T(128)S(1)} %stack.53.order_ref, bf16[2048,768]{1,0:T(8,128)(2,1)S(1)} %get-tuple-element.42.images_ref, bf16[4,96,768]{2,1,0:T(8,128)(2,1)S(1)} %shard_map.78.near_ref, ...), custom_call_target="tpu_custom_call" | custom-call | flops 2415919104 | bytes 3145728 | tf_op jit(solution)/shard_map/pallas_call | solution.py:196
  34.4 3.3 %shard_map.80 = (f32[2048,768]{1,0:T(8,128)S(1)}, f32[256,768]{1,0:T(8,128)S(1)}) custom-call(f32[2048,256]{1,0:T(8,128)S(1)} %get-tuple-element.44._target_ref.target_ref, bf16[2048,768]{1,0:T(8,128)(2,1)S(1)} %get-tuple-element.45.emb_ref.refs_1_, bf16[128,2304]{1,0:T(8,128)(2,1)S(1)} %get-tuple-element.40.low_ref, ...), custom_call_target="tpu_custom_call" | custom-call | flops 2415919104 | bytes 1179648 | tf_op jit(solution)/shard_map/pallas_call | solution.py:238
  37.7 0.0 copy-start.1
  37.7 0.9 copy-done.1
  38.6 0.0 collective-permute-done.5.refs_3_
  38.6 0.0 collective-permute-done.6.refs_4_
  38.6 10.6 %shard_map.81 = (f32[2048,768]{1,0:T(8,128)S(1)}, bf16[256,768]{1,0:T(8,128)(2,1)S(1)}, bf16[256,768]{1,0:T(8,128)(2,1)S(1)}) custom-call(bf16[2048,1536]{1,0:T(8,128)(2,1)S(1)} %get-tuple-element.43._tea_ref.refs_0_, bf16[2048,768]{1,0:T(8,128)(2,1)S(1)} %get-tuple-element.45.emb_ref.refs_1_, ...), custom_call_target="tpu_custom_call", output_to_operand_aliasing={{0}: (6, {})} | custom-call | flops 8053063680 | bytes 3932160 | tf_op jit(solution)/shard_map/pallas_call | solution.py:280
  49.2 0.0 collective-permute-done.9.refs_5_
  49.2 7.0 %shard_map.82 = (bf16[1024,768]{1,0:T(8,128)(2,1)S(1)}, bf16[256,768]{1,0:T(8,128)(2,1)S(1)}, bf16[256,768]{1,0:T(8,128)(2,1)S(1)}, bf16[256,768]{1,0:T(8,128)(2...) custom-call(s32[8]{0:T(128)S(1)} %stack.54.order_ref, ...), custom_call_target="tpu_custom_call" | custom-call | flops 4026531840 | bytes 3145728 | tf_op jit(solution)/shard_map/pallas_call | solution.py:330
  56.2 0.1 collective-permute-start.10
  56.3 3.4 %collective-permute-done.10.take_ref = bf16[1024,768]{1,0:T(8,128)(2,1)S(1)} collective-permute-done((bf16[1024,768]{1,0:T(8,128)(2,1)S(1)}, bf16[1024,768]{1,0:T(8,128)(2,1)S(1)}, u32[]{:S(2)}, u32[]{:S(2)}) %collective-permute-start.10) | collective-permute-done | bytes 1572896 | tf_op jit(solution)/shard_map/ppermute | solution.py:38
  59.7 3.1 %shard_map.83 = (bf16[4,4,24,768]{3,2,1,0:T(8,128)(2,1)S(1)}, bf16[4,4,24,768]{3,2,1,0:T(8,128)(2,1)}, bf16[256,768]{1,0:T(8,128)(2,1)S(1)}, bf16[256,768]{1,0:T...) custom-call(s32[8]{0:T(128)S(1)} %stack.53.order_ref, ...), custom_call_target="tpu_custom_call" | custom-call | flops 1207959552 | bytes 3145728 | tf_op jit(solution)/shard_map/pallas_call | solution.py:372
  62.8 0.7 copy-done.10
  63.5 0.1 collective-permute-start.13
  63.7 2.4 %collective-permute-start.12 = (bf16[256,768]{1,0:T(8,128)(2,1)}, bf16[256,768]{1,0:T(8,128)(2,1)}, u32[]{:S(2)}, u32[]{:S(2)}) collective-permute-start(bf16[256,768]{1,0:T(8,128)(2,1)} %get-tuple-element.57), channel_id=1, source_target_pairs={{0,2},{1,3},{2,0},{3,1},{4,6},{5,7},{6,4},{7,5},{8,10},{9,11},{10,... | collective-permute-start | bytes 1179656 | tf_op jit(solution)/shard_map/ppermute | solution.py:38
  66.0 0.1 pad_add_fusion.order_ref
  66.1 0.6 shard_map.86
  66.7 1.6 %collective-permute-start.15 = (bf16[4,24,768]{2,1,0:T(8,128)(2,1)S(1)}, bf16[4,24,768]{2,1,0:T(8,128)(2,1)S(1)}, u32[]{:S(2)}, u32[]{:S(2)}) collective-permute-start(bf16[4,24,768]{2,1,0:T(8,128)(2,1)S(1)} %get-tuple-element.63), channel_id=1, source_target_pairs={{0,8},{8,0},{16,24},{24,16},{1,9},{9,1},{17,25},{25,17},{2,10},{10... | collective-permute-start | bytes 442376 | tf_op jit(solution)/shard_map/ppermute | solution.py:38
  68.3 1.5 %collective-permute-start.16 = (bf16[4,24,768]{2,1,0:T(8,128)(2,1)S(1)}, bf16[4,24,768]{2,1,0:T(8,128)(2,1)S(1)}, u32[]{:S(2)}, u32[]{:S(2)}) collective-permute-start(bf16[4,24,768]{2,1,0:T(8,128)(2,1)S(1)} %get-tuple-element.64), channel_id=1, source_target_pairs={{0,16},{8,24},{16,0},{24,8},{1,17},{9,25},{17,1},{25,9},{2,18},{10... | collective-permute-start | bytes 442376 | tf_op jit(solution)/shard_map/ppermute | solution.py:38
  69.8 0.5 collective-permute-start.17
  70.3 2.0 %collective-permute-start.11 = (bf16[256,768]{1,0:T(8,128)(2,1)}, bf16[256,768]{1,0:T(8,128)(2,1)S(1)}, u32[]{:S(2)}, u32[]{:S(2)}) collective-permute-start(bf16[256,768]{1,0:T(8,128)(2,1)} %copy-done.10), channel_id=1, source_target_pairs={{0,2},{1,3},{2,0},{3,1},{4,6},{5,7},{6,4},{7,5},{8,10},{9,11},{10,... | collective-permute-start | bytes 1179656 | tf_op jit(solution)/shard_map/ppermute | solution.py:38
  72.3 1.1 collective-permute-done.15.refs_1_
  73.3 3.7 %collective-permute-done.16.refs_2_ = bf16[4,24,768]{2,1,0:T(8,128)(2,1)S(1)} collective-permute-done((bf16[4,24,768]{2,1,0:T(8,128)(2,1)S(1)}, bf16[4,24,768]{2,1,0:T(8,128)(2,1)S(1)}, u32[]{:S(2)}, u32[]{:S(2)}) %collective-permute-start.16) | collective-permute-done | bytes 147488 | tf_op jit(solution)/shard_map/ppermute | solution.py:38
  77.0 0.1 shard_map.87
  77.1 3.1 %collective-permute-start.18 = (bf16[2,24,768]{2,1,0:T(8,128)(2,1)S(1)}, bf16[2,24,768]{2,1,0:T(8,128)(2,1)S(1)}, u32[]{:S(2)}, u32[]{:S(2)}) collective-permute-start(bf16[2,24,768]{2,1,0:T(8,128)(2,1)S(1)} %get-tuple-element.67), channel_id=1, source_target_pairs={{0,4},{1,5},{2,6},{3,7},{4,0},{5,1},{6,2},{7,3},{8,12},{9,13},{10,... | collective-permute-start | bytes 221192 | tf_op jit(solution)/shard_map/ppermute | solution.py:38
  80.2 1.2 %shard_map.84.refs_3_ = bf16[256,768]{1,0:T(8,128)(2,1)S(1)} custom-call(bf16[256,768]{1,0:T(8,128)(2,1)S(1)} %get-tuple-element.56.refs_0_, bf16[256,768]{1,0:T(8,128)(2,1)} %collective-permute-done.12.refs_1_, bf16[4,4,24,768]{3,2,1,0:T(8,128)(2,1)S(1)} %collective-permute-done.13.refs_2_.far_ref), custom_call_target="tpu_custom_call" | custom-call | tf_op jit(solution)/shard_map/pallas_call | solution.py:80
  81.4 0.1 collective-permute-start.14
  81.5 1.0 copy-done.4
  82.5 1.0 copy-done.6
  83.5 0.1 shard_map.91
  83.6 1.3 %collective-permute-start.23 = (bf16[256,768]{1,0:T(8,128)(2,1)S(1)}, bf16[256,768]{1,0:T(8,128)(2,1)S(1)}, u32[]{:S(2)}, u32[]{:S(2)}) collective-permute-start(bf16[256,768]{1,0:T(8,128)(2,1)S(1)} %get-tuple-element.74), channel_id=1, source_target_pairs={{0,8},{8,0},{16,24},{24,16},{1,9},{9,1},{17,25},{25,17},{2,10},{10... | collective-permute-start | bytes 1179656 | tf_op jit(solution)/shard_map/ppermute | solution.py:38
  84.9 0.8 collective-permute-start.24
  85.7 0.1 collective-permute-done.18.refs_1_
  85.7 2.5 %collective-permute-start.25 = (bf16[256,768]{1,0:T(8,128)(2,1)S(1)}, bf16[256,768]{1,0:T(8,128)(2,1)S(1)}, u32[]{:S(2)}, u32[]{:S(2)}) collective-permute-start(bf16[256,768]{1,0:T(8,128)(2,1)S(1)} %get-tuple-element.76), channel_id=1, source_target_pairs={{0,24},{8,16},{16,8},{24,0},{1,25},{9,17},{17,9},{25,1},{2,26},{10... | collective-permute-start | bytes 1179656 | tf_op jit(solution)/shard_map/ppermute | solution.py:38
  88.2 0.3 collective-permute-done.11.refs_1_.refs_2_
  88.5 3.3 %collective-permute-start.19 = (bf16[1,24,768]{2,1,0:T(8,128)(2,1)S(1)}, bf16[1,24,768]{2,1,0:T(8,128)(2,1)S(1)}, u32[]{:S(2)}, u32[]{:S(2)}) collective-permute-start(bf16[1,24,768]{2,1,0:T(8,128)(2,1)S(1)} %get-tuple-element.69), channel_id=1, source_target_pairs={{0,2},{1,3},{2,0},{3,1},{4,6},{5,7},{6,4},{7,5},{8,10},{9,11},{10,... | collective-permute-start | bytes 110600 | tf_op jit(solution)/shard_map/ppermute | solution.py:38
  91.8 2.6 %collective-permute-done.19.refs_1_ = bf16[1,24,768]{2,1,0:T(8,128)(2,1)S(1)} collective-permute-done((bf16[1,24,768]{2,1,0:T(8,128)(2,1)S(1)}, bf16[1,24,768]{2,1,0:T(8,128)(2,1)S(1)}, u32[]{:S(2)}, u32[]{:S(2)}) %collective-permute-start.19) | collective-permute-done | bytes 36896 | tf_op jit(solution)/shard_map/ppermute | solution.py:38
  94.4 7.9 %collective-permute-done.14.refs_2_.refs_3_ = bf16[256,768]{1,0:T(8,128)(2,1)S(1)} collective-permute-done((bf16[256,768]{1,0:T(8,128)(2,1)S(1)}, bf16[256,768]{1,0:T(8,128)(2,1)S(1)}, u32[]{:S(2)}, u32[]{:S(2)}) %collective-permute-start.14) | collective-permute-done | bytes 393248 | tf_op jit(solution)/shard_map/ppermute | solution.py:38
  102.3 1.4 %collective-permute-start.20 = (bf16[24,768]{1,0:T(8,128)(2,1)S(1)}, bf16[24,768]{1,0:T(8,128)(2,1)S(1)}, u32[]{:S(2)}, u32[]{:S(2)}) collective-permute-start(bf16[24,768]{1,0:T(8,128)(2,1)S(1)} %bitcast.15), channel_id=1, source_target_pairs={{0,8},{8,0},{16,24},{24,16},{1,9},{9,1},{17,25},{25,17},{2,10},{10... | collective-permute-start | bytes 110600 | tf_op jit(solution)/shard_map/ppermute | solution.py:38
  103.8 0.6 collective-permute-start.21
  104.3 1.6 %collective-permute-start.22 = (bf16[24,768]{1,0:T(8,128)(2,1)S(1)}, bf16[24,768]{1,0:T(8,128)(2,1)S(1)}, u32[]{:S(2)}, u32[]{:S(2)}) collective-permute-start(bf16[24,768]{1,0:T(8,128)(2,1)S(1)} %bitcast.17), channel_id=1, source_target_pairs={{0,24},{8,16},{16,8},{24,0},{1,25},{9,17},{17,9},{25,1},{2,26},{10... | collective-permute-start | bytes 110600 | tf_op jit(solution)/shard_map/ppermute | solution.py:38
  105.9 1.4 %shard_map.85 = (f32[256,768]{1,0:T(8,128)}, f32[8,128]{1,0:T(8,128)}) custom-call(bf16[256,768]{1,0:T(8,128)(2,1)S(1)} %get-tuple-element.54.refs_0_, bf16[256,768]{1,0:T(8,128)(2,1)S(1)} %collective-permute-done.11.refs_1_.refs_2_, bf16[256,768]{1,0:T(8,128)(2,1)S(1)} %collective-permute-done.14.refs_2_.refs_3_, bf16[768,768]{1,0:T(8,128)(2,1)S(1)} %get-tuple-element.59.refs_3_), custom_call_target="tpu_custom_call" | custom-call | tf_op jit(solution)/shard_map/pallas_call | solution.py:459
  107.3 1.3 %shard_map.92 = f32[256,768]{1,0:T(8,128)} custom-call(bf16[256,768]{1,0:T(8,128)(2,1)S(1)} %copy-done, f32[256,768]{1,0:T(8,128)S(1)} %copy-done.2, bf16[256,768]{1,0:T(8,128)(2,1)S(1)} %collective-permute-done.23.refs_0_, bf16[256,768]{1,0:T(8,128)(2,1)S(1)} %collective-permute-done.24.refs_1_, bf16[256,768]{1,0:T(8,128)(2,1)S(1)} %collective-permute-done.25.refs_2_), custom_call_target="tpu_custom_call" | custom-call | tf_op jit(solution)/shard_map/pallas_call | solution.py:439
  108.6 0.6 collective-permute-done.22.refs_3_
  109.2 1.3 %shard_map.90 = f32[96,768]{1,0:T(8,128)} custom-call(s32[4]{0:T(128)S(1)} %pad_add_fusion.order_ref, bf16[24,768]{1,0:T(8,128)(2,1)S(1)} %bitcast.18, bf16[24,768]{1,0:T(8,128)(2,1)S(1)} %collective-permute-done.20.refs_1_, bf16[24,768]{1,0:T(8,128)(2,1)S(1)} %collective-permute-done.21.refs_2_, bf16[24,768]{1,0:T(8,128)(2,1)S(1)} %collective-permute-done.22.refs_3_), custom_call_target="tpu_custom_call" | custom-call | tf_op jit(solution)/shard_map/pallas_call | solution.py:415
  (30 shorter events, 0.1 us)
Async XLA Ops:
  0.6 10.5 %collective-permute-start = (bf16[96,768]{1,0:T(8,128)(2,1)}, bf16[96,768]{1,0:T(8,128)(2,1)S(1)}, u32[]{:S(2)}, u32[]{:S(2)}) collective-permute-start(bf16[96,768]{1,0:T(8,128)(2,1)} %bitcast.19), channel_id=1, source_target_pairs={{0,2},{1,3},{2,0},{3,1},{4,6},{5,7},{6,4},{7,5},{8,10},{9,11},{10,... | collective-permute-start | bytes 442376 | tf_op jit(solution)/shard_map/ppermute | solution.py:38
  3.7 14.2 %collective-permute-start.1 = (bf16[96,768]{1,0:T(8,128)(2,1)}, bf16[96,768]{1,0:T(8,128)(2,1)S(1)}, u32[]{:S(2)}, u32[]{:S(2)}) collective-permute-start(bf16[96,768]{1,0:T(8,128)(2,1)} %bitcast.20), channel_id=1, source_target_pairs={{0,4},{1,5},{2,6},{3,7},{4,0},{5,1},{6,2},{7,3},{8,12},{9,13},{10,... | collective-permute-start | bytes 442376 | tf_op jit(solution)/shard_map/ppermute | solution.py:38
  6.3 11.6 %collective-permute-start.2 = (bf16[96,768]{1,0:T(8,128)(2,1)}, bf16[96,768]{1,0:T(8,128)(2,1)S(1)}, u32[]{:S(2)}, u32[]{:S(2)}) collective-permute-start(bf16[96,768]{1,0:T(8,128)(2,1)} %bitcast.21), channel_id=1, source_target_pairs={{0,6},{1,7},{2,4},{3,5},{4,2},{5,3},{6,0},{7,1},{8,14},{9,15},{10,... | collective-permute-start | bytes 442376 | tf_op jit(solution)/shard_map/ppermute | solution.py:38
  7.8 21.7 %collective-permute-start.4 = (bf16[128,2304]{1,0:T(8,128)(2,1)S(1)}, bf16[128,2304]{1,0:T(8,128)(2,1)}, u32[]{:S(2)}, u32[]{:S(2)}) collective-permute-start(bf16[128,2304]{1,0:T(8,128)(2,1)S(1)} %get-tuple-element.40.low_ref), channel_id=1, source_target_pairs={{0,8},{8,0},{16,24},{24,16},{1,9},{9,1},{17,25},{25,17},{2,10},{10... | collective-permute-start | bytes 1769480 | tf_op jit(solution)/shard_map/ppermute | solution.py:38
  9.6 20.5 %collective-permute-start.7 = (bf16[128,2304]{1,0:T(8,128)(2,1)S(1)}, bf16[128,2304]{1,0:T(8,128)(2,1)}, u32[]{:S(2)}, u32[]{:S(2)}) collective-permute-start(bf16[128,2304]{1,0:T(8,128)(2,1)S(1)} %get-tuple-element.41.high_ref), channel_id=1, source_target_pairs={{0,16},{8,24},{16,0},{24,8},{1,17},{9,25},{17,1},{25,9},{2,18},{10... | collective-permute-start | bytes 1769480 | tf_op jit(solution)/shard_map/ppermute | solution.py:38
  17.9 0.9 copy-start.9
  18.9 11.8 %collective-permute-start.3 = (bf16[4,96,768]{2,1,0:T(8,128)(2,1)S(1)}, bf16[4,96,768]{2,1,0:T(8,128)(2,1)S(1)}, u32[]{:S(2)}, u32[]{:S(2)}) collective-permute-start(bf16[4,96,768]{2,1,0:T(8,128)(2,1)S(1)} %shard_map.78.near_ref), channel_id=1, source_target_pairs={{0,1},{1,0},{2,3},{3,2},{4,5},{5,4},{6,7},{7,6},{8,9},{9,8},{10,11... | collective-permute-start | bytes 1769480 | tf_op jit(solution)/shard_map/ppermute | solution.py:38
  19.0 19.6 %collective-permute-start.5 = (bf16[128,2304]{1,0:T(8,128)(2,1)S(1)}, bf16[128,2304]{1,0:T(8,128)(2,1)}, u32[]{:S(2)}, u32[]{:S(2)}) collective-permute-start(bf16[128,2304]{1,0:T(8,128)(2,1)S(1)} %get-tuple-element.41.high_ref), channel_id=1, source_target_pairs={{0,8},{8,0},{16,24},{24,16},{1,9},{9,1},{17,25},{25,17},{2,10},{10... | collective-permute-start | bytes 1769480 | tf_op jit(solution)/shard_map/ppermute | solution.py:38
  20.5 18.1 %collective-permute-start.6 = (bf16[128,2304]{1,0:T(8,128)(2,1)S(1)}, bf16[128,2304]{1,0:T(8,128)(2,1)}, u32[]{:S(2)}, u32[]{:S(2)}) collective-permute-start(bf16[128,2304]{1,0:T(8,128)(2,1)S(1)} %get-tuple-element.40.low_ref), channel_id=1, source_target_pairs={{0,16},{8,24},{16,0},{24,8},{1,17},{9,25},{17,1},{25,9},{2,18},{10... | collective-permute-start | bytes 1769480 | tf_op jit(solution)/shard_map/ppermute | solution.py:38
  29.5 19.6 %collective-permute-start.8 = (bf16[128,2304]{1,0:T(8,128)(2,1)}, bf16[128,2304]{1,0:T(8,128)(2,1)S(1)}, u32[]{:S(2)}, u32[]{:S(2)}) collective-permute-start(bf16[128,2304]{1,0:T(8,128)(2,1)} %collective-permute-done.4.refs_2_), channel_id=1, source_target_pairs={{0,16},{8,24},{16,0},{24,8},{1,17},{9,25},{17,1},{25,9},{2,18},{10... | collective-permute-start | bytes 1769480 | tf_op jit(solution)/shard_map/ppermute | solution.py:38
  30.1 19.0 %collective-permute-start.9 = (bf16[128,2304]{1,0:T(8,128)(2,1)}, bf16[128,2304]{1,0:T(8,128)(2,1)S(1)}, u32[]{:S(2)}, u32[]{:S(2)}) collective-permute-start(bf16[128,2304]{1,0:T(8,128)(2,1)} %collective-permute-done.7.refs_5_), channel_id=1, source_target_pairs={{0,8},{8,0},{16,24},{24,16},{1,9},{9,1},{17,25},{25,17},{2,10},{10... | collective-permute-start | bytes 1769480 | tf_op jit(solution)/shard_map/ppermute | solution.py:38
  37.7 0.9 copy-start.1
  49.1 7.0 %copy-start.3 = (bf16[256,768]{1,0:T(8,128)(2,1)}, bf16[256,768]{1,0:T(8,128)(2,1)S(1)}, u32[]{:S(2)}) copy-start(bf16[256,768]{1,0:T(8,128)(2,1)S(1)} %get-tuple-element.71.refs_0_) | copy-start | bytes 1179652
  49.1 7.0 %copy-start.5 = (bf16[256,768]{1,0:T(8,128)(2,1)}, bf16[256,768]{1,0:T(8,128)(2,1)S(1)}, u32[]{:S(2)}) copy-start(bf16[256,768]{1,0:T(8,128)(2,1)S(1)} %get-tuple-element.72.refs_1_) | copy-start | bytes 1179652
  56.2 6.6 %copy-start.7 = (bf16[256,768]{1,0:T(8,128)(2,1)}, bf16[256,768]{1,0:T(8,128)(2,1)S(1)}, u32[]{:S(2)}) copy-start(bf16[256,768]{1,0:T(8,128)(2,1)S(1)} %get-tuple-element.73.refs_2_) | copy-start | bytes 1179652
  56.2 3.5 %collective-permute-start.10 = (bf16[1024,768]{1,0:T(8,128)(2,1)S(1)}, bf16[1024,768]{1,0:T(8,128)(2,1)S(1)}, u32[]{:S(2)}, u32[]{:S(2)}) collective-permute-start(bf16[1024,768]{1,0:T(8,128)(2,1)S(1)} %get-tuple-element.49), channel_id=1, source_target_pairs={{0,1},{1,0},{2,3},{3,2},{4,5},{5,4},{6,7},{7,6},{8,9},{9,8},{10,11... | collective-permute-start | bytes 4718600 | tf_op jit(solution)/shard_map/ppermute | solution.py:38
  62.8 0.7 copy-start.10
  63.5 2.6 %collective-permute-start.13 = (bf16[4,4,24,768]{3,2,1,0:T(8,128)(2,1)}, bf16[4,4,24,768]{3,2,1,0:T(8,128)(2,1)S(1)}, u32[]{:S(2)}, u32[]{:S(2)}) collective-permute-start(bf16[4,4,24,768]{3,2,1,0:T(8,128)(2,1)} %get-tuple-element.58), channel_id=1, source_target_pairs={{0,1},{1,0},{2,3},{3,2},{4,5},{5,4},{6,7},{7,6},{8,9},{9,8},{10,11... | collective-permute-start | bytes 1769480 | tf_op jit(solution)/shard_map/ppermute | solution.py:38
  63.7 16.5 %collective-permute-start.12 = (bf16[256,768]{1,0:T(8,128)(2,1)}, bf16[256,768]{1,0:T(8,128)(2,1)}, u32[]{:S(2)}, u32[]{:S(2)}) collective-permute-start(bf16[256,768]{1,0:T(8,128)(2,1)} %get-tuple-element.57), channel_id=1, source_target_pairs={{0,2},{1,3},{2,0},{3,1},{4,6},{5,7},{6,4},{7,5},{8,10},{9,11},{10,... | collective-permute-start | bytes 1179656 | tf_op jit(solution)/shard_map/ppermute | solution.py:38
  66.0 15.5 %copy-start.8 = (bf16[256,768]{1,0:T(8,128)(2,1)S(1)}, bf16[256,768]{1,0:T(8,128)(2,1)}, u32[]{:S(2)}) copy-start(bf16[256,768]{1,0:T(8,128)(2,1)} %copy-done.7) | copy-start | bytes 1179652
  66.7 6.6 %collective-permute-start.15 = (bf16[4,24,768]{2,1,0:T(8,128)(2,1)S(1)}, bf16[4,24,768]{2,1,0:T(8,128)(2,1)S(1)}, u32[]{:S(2)}, u32[]{:S(2)}) collective-permute-start(bf16[4,24,768]{2,1,0:T(8,128)(2,1)S(1)} %get-tuple-element.63), channel_id=1, source_target_pairs={{0,8},{8,0},{16,24},{24,16},{1,9},{9,1},{17,25},{25,17},{2,10},{10... | collective-permute-start | bytes 442376 | tf_op jit(solution)/shard_map/ppermute | solution.py:38
  68.3 8.7 %collective-permute-start.16 = (bf16[4,24,768]{2,1,0:T(8,128)(2,1)S(1)}, bf16[4,24,768]{2,1,0:T(8,128)(2,1)S(1)}, u32[]{:S(2)}, u32[]{:S(2)}) collective-permute-start(bf16[4,24,768]{2,1,0:T(8,128)(2,1)S(1)} %get-tuple-element.64), channel_id=1, source_target_pairs={{0,16},{8,24},{16,0},{24,8},{1,17},{9,25},{17,1},{25,9},{2,18},{10... | collective-permute-start | bytes 442376 | tf_op jit(solution)/shard_map/ppermute | solution.py:38
  69.8 7.2 %collective-permute-start.17 = (bf16[4,24,768]{2,1,0:T(8,128)(2,1)S(1)}, bf16[4,24,768]{2,1,0:T(8,128)(2,1)S(1)}, u32[]{:S(2)}, u32[]{:S(2)}) collective-permute-start(bf16[4,24,768]{2,1,0:T(8,128)(2,1)S(1)} %get-tuple-element.65), channel_id=1, source_target_pairs={{0,24},{8,16},{16,8},{24,0},{1,25},{9,17},{17,9},{25,1},{2,26},{10... | collective-permute-start | bytes 442376 | tf_op jit(solution)/shard_map/ppermute | solution.py:38
  70.3 18.3 %collective-permute-start.11 = (bf16[256,768]{1,0:T(8,128)(2,1)}, bf16[256,768]{1,0:T(8,128)(2,1)S(1)}, u32[]{:S(2)}, u32[]{:S(2)}) collective-permute-start(bf16[256,768]{1,0:T(8,128)(2,1)} %copy-done.10), channel_id=1, source_target_pairs={{0,2},{1,3},{2,0},{3,1},{4,6},{5,7},{6,4},{7,5},{8,10},{9,11},{10,... | collective-permute-start | bytes 1179656 | tf_op jit(solution)/shard_map/ppermute | solution.py:38
  77.1 8.7 %collective-permute-start.18 = (bf16[2,24,768]{2,1,0:T(8,128)(2,1)S(1)}, bf16[2,24,768]{2,1,0:T(8,128)(2,1)S(1)}, u32[]{:S(2)}, u32[]{:S(2)}) collective-permute-start(bf16[2,24,768]{2,1,0:T(8,128)(2,1)S(1)} %get-tuple-element.67), channel_id=1, source_target_pairs={{0,4},{1,5},{2,6},{3,7},{4,0},{5,1},{6,2},{7,3},{8,12},{9,13},{10,... | collective-permute-start | bytes 221192 | tf_op jit(solution)/shard_map/ppermute | solution.py:38
  80.2 27.1 %copy-start = (bf16[256,768]{1,0:T(8,128)(2,1)S(1)}, bf16[256,768]{1,0:T(8,128)(2,1)}, u32[]{:S(2)}) copy-start(bf16[256,768]{1,0:T(8,128)(2,1)} %stu_ref.3) | copy-start | bytes 1179652
  80.2 27.1 %copy-start.2 = (f32[256,768]{1,0:T(8,128)S(1)}, f32[256,768]{1,0:T(8,128)}, u32[]{:S(2)}) copy-start(f32[256,768]{1,0:T(8,128)} %copy-done.1) | copy-start | bytes 2359300
  81.4 21.0 %collective-permute-start.14 = (bf16[256,768]{1,0:T(8,128)(2,1)S(1)}, bf16[256,768]{1,0:T(8,128)(2,1)S(1)}, u32[]{:S(2)}, u32[]{:S(2)}) collective-permute-start(bf16[256,768]{1,0:T(8,128)(2,1)S(1)} %shard_map.84.refs_3_), channel_id=1, source_target_pairs={{0,4},{1,5},{2,6},{3,7},{4,0},{5,1},{6,2},{7,3},{8,12},{9,13},{10,... | collective-permute-start | bytes 1179656 | tf_op jit(solution)/shard_map/ppermute | solution.py:38
  81.5 1.0 copy-start.4
  82.5 1.0 copy-start.6
  83.6 20.8 %collective-permute-start.23 = (bf16[256,768]{1,0:T(8,128)(2,1)S(1)}, bf16[256,768]{1,0:T(8,128)(2,1)S(1)}, u32[]{:S(2)}, u32[]{:S(2)}) collective-permute-start(bf16[256,768]{1,0:T(8,128)(2,1)S(1)} %get-tuple-element.74), channel_id=1, source_target_pairs={{0,8},{8,0},{16,24},{24,16},{1,9},{9,1},{17,25},{25,17},{2,10},{10... | collective-permute-start | bytes 1179656 | tf_op jit(solution)/shard_map/ppermute | solution.py:38
  84.9 22.4 %collective-permute-start.24 = (bf16[256,768]{1,0:T(8,128)(2,1)S(1)}, bf16[256,768]{1,0:T(8,128)(2,1)S(1)}, u32[]{:S(2)}, u32[]{:S(2)}) collective-permute-start(bf16[256,768]{1,0:T(8,128)(2,1)S(1)} %get-tuple-element.75), channel_id=1, source_target_pairs={{0,16},{8,24},{16,0},{24,8},{1,17},{9,25},{17,1},{25,9},{2,18},{10... | collective-permute-start | bytes 1179656 | tf_op jit(solution)/shard_map/ppermute | solution.py:38
  85.7 21.6 %collective-permute-start.25 = (bf16[256,768]{1,0:T(8,128)(2,1)S(1)}, bf16[256,768]{1,0:T(8,128)(2,1)S(1)}, u32[]{:S(2)}, u32[]{:S(2)}) collective-permute-start(bf16[256,768]{1,0:T(8,128)(2,1)S(1)} %get-tuple-element.76), channel_id=1, source_target_pairs={{0,24},{8,16},{16,8},{24,0},{1,25},{9,17},{17,9},{25,1},{2,26},{10... | collective-permute-start | bytes 1179656 | tf_op jit(solution)/shard_map/ppermute | solution.py:38
  88.5 5.9 %collective-permute-start.19 = (bf16[1,24,768]{2,1,0:T(8,128)(2,1)S(1)}, bf16[1,24,768]{2,1,0:T(8,128)(2,1)S(1)}, u32[]{:S(2)}, u32[]{:S(2)}) collective-permute-start(bf16[1,24,768]{2,1,0:T(8,128)(2,1)S(1)} %get-tuple-element.69), channel_id=1, source_target_pairs={{0,2},{1,3},{2,0},{3,1},{4,6},{5,7},{6,4},{7,5},{8,10},{9,11},{10,... | collective-permute-start | bytes 110600 | tf_op jit(solution)/shard_map/ppermute | solution.py:38
  102.3 6.3 %collective-permute-start.20 = (bf16[24,768]{1,0:T(8,128)(2,1)S(1)}, bf16[24,768]{1,0:T(8,128)(2,1)S(1)}, u32[]{:S(2)}, u32[]{:S(2)}) collective-permute-start(bf16[24,768]{1,0:T(8,128)(2,1)S(1)} %bitcast.15), channel_id=1, source_target_pairs={{0,8},{8,0},{16,24},{24,16},{1,9},{9,1},{17,25},{25,17},{2,10},{10... | collective-permute-start | bytes 110600 | tf_op jit(solution)/shard_map/ppermute | solution.py:38
  103.8 4.9 %collective-permute-start.21 = (bf16[24,768]{1,0:T(8,128)(2,1)S(1)}, bf16[24,768]{1,0:T(8,128)(2,1)S(1)}, u32[]{:S(2)}, u32[]{:S(2)}) collective-permute-start(bf16[24,768]{1,0:T(8,128)(2,1)S(1)} %bitcast.16), channel_id=1, source_target_pairs={{0,16},{8,24},{16,0},{24,8},{1,17},{9,25},{17,1},{25,9},{2,18},{10... | collective-permute-start | bytes 110600 | tf_op jit(solution)/shard_map/ppermute | solution.py:38
  104.3 4.9 %collective-permute-start.22 = (bf16[24,768]{1,0:T(8,128)(2,1)S(1)}, bf16[24,768]{1,0:T(8,128)(2,1)S(1)}, u32[]{:S(2)}, u32[]{:S(2)}) collective-permute-start(bf16[24,768]{1,0:T(8,128)(2,1)S(1)} %bitcast.17), channel_id=1, source_target_pairs={{0,24},{8,16},{16,8},{24,0},{1,25},{9,17},{17,9},{25,1},{2,26},{10... | collective-permute-start | bytes 110600 | tf_op jit(solution)/shard_map/ppermute | solution.py:38
